TPU v7x, 32 devices: a whole 2x2x4 slice. The times are simulated.
32 devices in a mesh: dp: 4 (over y, x), expert: 8 (over z, core).
Axes of the slice: x: 2, y: 2, z: 4, core: 2. Of those that a mesh axis runs over, the one named last changes fastest.
Arguments:
- tokens: bfloat16 [4096, 2048], P(('dp', 'expert')), may hold values from -6 to 6
- cotangent: bfloat16 [4096, 2048], P(('dp', 'expert')), may hold values from -3 to 3
- w_gate: bfloat16 [8, 2048, 768], P('expert'), may hold values from -0.125 to 0.125
- w_up: bfloat16 [8, 2048, 768], P('expert'), may hold values from -0.125 to 0.125
- w_down: bfloat16 [8, 768, 2048], P('expert'), may hold values from -0.21875 to 0.21875
- slot_rows: int32 [32, 8, 24], P(('dp', 'expert')), may hold values from 0 to 127, as said below
- slot_counts: int32 [32, 8], P(('dp', 'expert')), may hold values from 12 to 24, as said below
- slot_gates: float32 [32, 8, 24], P(('dp', 'expert')), may hold values from 0.1 to 1
- seq_lengths: int32 [32, 4], P(('dp', 'expert')), may hold values from 1 to 32, 96 in all within a row
- matching: int32 [8, 4], P('expert'), may hold values from 0 to 3, as said below
Outputs:
- output: bfloat16 [4096, 2048], P(('dp', 'expert'))
- grad_tokens: bfloat16 [4096, 2048], P(('dp', 'expert'))
- grad_w_gate: float32 [8, 2048, 768], P('expert', 'dp')
- grad_w_up: float32 [8, 2048, 768], P('expert', 'dp')
- grad_w_down: float32 [8, 768, 2048], P('expert', None, 'dp')
Inputs may be any that keep to these rules, and one draw needn't show every extreme that they name: `slot_rows`: within one block the slots of one expert hold distinct rows, and no row is held by more than 8 slots of its block. `slot_counts`: in every draw one expert of the window, drawn anew, has 24 live slots in every block; the others have at least 12. matching[b, g] = g XOR k_b, with k_b of 1 to 3 common to all replicas at block position b, so partners are mutual; in every draw k_b = 2 at one or more positions. `seq_lengths`: the 4 lengths of each block sum to 96.
All inputs are finite; a program needn't handle non-finite values.
Results may differ from a plain program's by a relative error of at most 0.018.
Values may be sent and summed in bfloat16 or wider, within the bound.
No kernel may reach another device: no remote copies, remote signals or barrier semaphores. Data moves between devices by JAX's collectives and lax.ppermute only.
A program may use at most 128 MiB of HBM per device.

v0:
```python
import jax
import jax.numpy as jnp
from jax import lax
from jax.sharding import PartitionSpec as P


def partner_picker(partner, pieces):
    piece_len = pieces[0].shape[0]
    chosen = jnp.arange(piece_len, dtype=jnp.int32) == partner
    return tuple(
        (
            jnp.sum(
                jnp.where(
                    chosen.reshape((piece_len,) + (1,) * (member.ndim - 1)),
                    member,
                    jnp.zeros_like(member),
                ),
                axis=0,
                keepdims=True,
            )
            for member in pieces
        )
    )


def forward_pairs(moved_rows, moved_valid, partner):
    found = partner_picker(
        partner,
        (
            lax.all_gather(moved_rows[None], "dp", axis=0, tiled=True),
            lax.all_gather(moved_valid[None], "dp", axis=0, tiled=True),
        ),
    )
    return (found[0][0], found[1][0])


def backward_pairs(moved_grads, partner):
    found = partner_picker(partner, (lax.all_gather(moved_grads[None], "dp", axis=0, tiled=True),))
    return found[0][0]


def per_device(
    tokens,
    cotangent,
    w_gate,
    w_up,
    w_down,
    slot_rows,
    slot_counts,
    slot_gates,
    seq_lengths,
    matching,
):
    tok_dev, model_width = tokens.shape
    half_rows = tok_dev // 2
    expert_count = lax.axis_size("expert")
    local_experts = w_gate.shape[0]
    window = slot_rows.shape[1]
    capacity = slot_rows.shape[2]
    seq_count = seq_lengths.shape[1]
    slot_len = tok_dev // seq_count
    shift_key = matching[0, 0]
    partner = jnp.bitwise_xor(lax.axis_index("dp"), shift_key)
    positions = jnp.arange(tok_dev, dtype=jnp.int32)
    valid_rows = (positions % slot_len < seq_lengths[0][positions // slot_len]).astype(jnp.bfloat16)
    moved_rows, moved_valid = forward_pairs(tokens[half_rows:], valid_rows[half_rows:], partner)
    shuffled = jnp.concatenate([tokens[:half_rows], moved_rows], axis=0)
    valid_swapped = jnp.concatenate([valid_rows[:half_rows], moved_valid], axis=0).astype(
        jnp.float32
    )
    slot_index = slot_rows[0]
    slot_live = (jnp.arange(capacity, dtype=jnp.int32)[None, :] < slot_counts[0][:, None]).astype(
        jnp.float32
    )
    live_gate = slot_gates[0] * slot_live * valid_swapped[slot_index]
    buffer_shape = (expert_count, local_experts, capacity, model_width)
    picked = shuffled[slot_index].reshape(buffer_shape)
    weighted = (live_gate[:, :, None] * cotangent[slot_index].astype(jnp.float32)).astype(
        jnp.bfloat16
    )
    weighted = weighted.reshape(buffer_shape)
    sent_rows = lax.all_to_all(picked, "expert", split_axis=0, concat_axis=0, tiled=True)
    pre_gate = jnp.einsum("sejd,edf->sejf", sent_rows, w_gate, preferred_element_type=jnp.float32)
    pre_up = jnp.einsum("sejd,edf->sejf", sent_rows, w_up, preferred_element_type=jnp.float32)
    sigmoid_gate = jax.nn.sigmoid(pre_gate)
    hidden = (pre_gate * sigmoid_gate * pre_up).astype(jnp.bfloat16)
    expert_out = jnp.einsum(
        "sejf,efd->sejd", hidden, w_down, preferred_element_type=jnp.float32
    ).astype(jnp.bfloat16)
    expert_out, pre_gate, pre_up, hidden = (expert_out, pre_gate, pre_up, hidden)
    expert_out, pre_gate, pre_up, hidden, sent_rows = (
        expert_out,
        pre_gate,
        pre_up,
        hidden,
        sent_rows,
    )
    back_out = lax.all_to_all(expert_out, "expert", split_axis=0, concat_axis=0, tiled=True)
    sent_grads = lax.all_to_all(weighted, "expert", split_axis=0, concat_axis=0, tiled=True)
    grad_hidden = jnp.einsum(
        "sejd,efd->sejf", sent_grads, w_down, preferred_element_type=jnp.float32
    )
    sigmoid_gate = jax.nn.sigmoid(pre_gate)
    silu_gate = pre_gate * sigmoid_gate
    grad_gate = (
        grad_hidden * pre_up * sigmoid_gate * (1.0 + pre_gate * (1.0 - sigmoid_gate))
    ).astype(jnp.bfloat16)
    grad_up = (grad_hidden * silu_gate).astype(jnp.bfloat16)
    token_rows = jnp.einsum(
        "sejf,edf->sejd", grad_gate, w_gate, preferred_element_type=jnp.float32
    ) + jnp.einsum("sejf,edf->sejd", grad_up, w_up, preferred_element_type=jnp.float32)
    token_rows, grad_gate, grad_up = (token_rows.astype(jnp.bfloat16), grad_gate, grad_up)
    back_rows = lax.all_to_all(token_rows, "expert", split_axis=0, concat_axis=0, tiled=True)
    flat_index = slot_index.reshape(window * capacity)
    hit_table = positions[:, None] == flat_index[None, :]
    gated_table = hit_table.astype(jnp.float32) * live_gate.reshape(1, window * capacity)
    output = jnp.dot(
        gated_table,
        back_out.reshape(window * capacity, model_width).astype(jnp.float32),
        precision=lax.Precision.HIGHEST,
    ).astype(jnp.bfloat16)
    grad_shuffled = jnp.dot(
        hit_table.astype(jnp.bfloat16),
        back_rows.reshape(window * capacity, model_width),
        preferred_element_type=jnp.float32,
    ).astype(jnp.bfloat16)
    grad_moved = backward_pairs(grad_shuffled[half_rows:], partner)
    grad_tokens = jnp.concatenate([grad_shuffled[:half_rows], grad_moved], axis=0)
    part_gate = jnp.einsum(
        "sejd,sejf->edf", sent_rows, grad_gate, preferred_element_type=jnp.float32
    )
    part_up = jnp.einsum("sejd,sejf->edf", sent_rows, grad_up, preferred_element_type=jnp.float32)
    part_down = jnp.einsum("sejd,sejf->edf", sent_grads, hidden, preferred_element_type=jnp.float32)
    grad_w_gate, grad_w_up, down_summed = (
        lax.psum_scatter(
            part_gate.astype(jnp.bfloat16), "dp", scatter_dimension=1, tiled=True
        ).astype(jnp.float32),
        lax.psum_scatter(
            part_up.astype(jnp.bfloat16), "dp", scatter_dimension=1, tiled=True
        ).astype(jnp.float32),
        lax.psum_scatter(
            part_down.astype(jnp.bfloat16), "dp", scatter_dimension=1, tiled=True
        ).astype(jnp.float32),
    )
    grad_w_down = jnp.transpose(down_summed, (0, 2, 1))
    return (output, grad_tokens, grad_w_gate, grad_w_up, grad_w_down)


def solution(mesh):
    return jax.shard_map(
        per_device,
        mesh=mesh,
        in_specs=(
            P(("dp", "expert"), None),
            P(("dp", "expert"), None),
            P("expert", None, None),
            P("expert", None, None),
            P("expert", None, None),
            P(("dp", "expert"), None, None),
            P(("dp", "expert"), None),
            P(("dp", "expert"), None, None),
            P(("dp", "expert"), None),
            P("expert", None),
        ),
        out_specs=(
            P(("dp", "expert"), None),
            P(("dp", "expert"), None),
            P("expert", "dp", None),
            P("expert", "dp", None),
            P("expert", None, "dp"),
        ),
        check_vma=False,
    )
```

profile of v0, /device:TPU:0, one launch (start us, length us, event | category | flops | bytes accessed | tf_op | source)
XLA Modules:
  0.0 306.8 jit_solution(7718438165558174862)
XLA Ops:
  12.5 27.3 %all-gather.6.cloned.1.call-done = bf16[256,2048]{1,0:T(8,128)(2,1)} async-done(((bf16[64,2048]{1,0:T(8,128)(2,1)}), bf16[256,2048]{1,0:T(8,128)(2,1)}) %all-gather.6.cloned.1.call-update) | async-done | bytes 1048592 | tf_op jit(solution)/shard_map/all_gather | solution.py:30
  42.1 3.9 %gather_fusion.1 = bf16[192,2048]{1,0:T(8,128)(2,1)} fusion(bf16[128,2048]{1,0:T(8,128)(2,1)} %pad_maximum_fusion, s32[1024]{0:T(1024)S(1)} %pad_clamp_fusion), kind=kCustom, calls=%fused_computation.1 | custom fusion | bytes 1573632 | tf_op jit(solution)/shard_map/gather | solution.py:77
  46.0 4.6 %all-to-all-start = ((bf16[8,1,24,2048]{3,2,1,0:T(8,128)(2,1)}), bf16[8,1,24,2048]{3,2,1,0:T(8,128)(2,1)}, u32[]{:S(2)}, u32[]{:S(2)}) async-start(bf16[8,1,24,2048]{3,2,1,0:T(8,128)(2,1)} %bitcast.155), calls=%async_computation | async-start | bytes 1572864 | tf_op jit(solution)/shard_map/all_to_all | solution.py:82
  51.2 2.6 compare_convert_fusion
  54.1 8.9 %all-reduce = bf16[256]{0:T(256)(128)(2,1)S(1)} all-reduce(bf16[256]{0:T(256)(128)(2,1)S(1)} %dynamic-update-slice), channel_id=2, replica_groups=mesh['dp'=4,'expert'=8] {'dp'}, use_global_device_ids=true, to_apply=%add | all-reduce | flops 256 | bytes 1024
  64.9 3.9 %gather_fusion.2 = bf16[192,2048]{1,0:T(8,128)(2,1)} fusion(bf16[128,2048]{1,0:T(8,128)(2,1)} %param.11, s32[1024]{0:T(1024)S(1)} %pad_clamp_fusion), kind=kCustom, calls=%fused_computation.2 | custom fusion | bytes 1573632 | tf_op jit(solution)/shard_map/gather | solution.py:78
  71.7 4.5 %all-to-all-start.2 = ((bf16[8,1,24,2048]{3,2,1,0:T(8,128)(2,1)}), bf16[8,1,24,2048]{3,2,1,0:T(8,128)(2,1)}, u32[]{:S(2)}, u32[]{:S(2)}) async-start(bf16[8,1,24,2048]{3,2,1,0:T(8,128)(2,1)} %fusion.30), calls=%async_computation.2 | async-start | bytes 1572864 | tf_op jit(solution)/shard_map/all_to_all | solution.py:99
  76.2 3.9 %fusion.34 = f32[8,1,24,768]{3,2,0,1:T(8,128)} fusion(bf16[1,2048,768]{2,1,0:T(8,128)(2,1)} %param.13, bf16[8,1,24,2048]{3,2,1,0:T(8,128)(2,1)} %all-to-all-done), kind=kOutput, calls=%fused_computation.32 | convolution fusion | flops 603979776 | bytes 4521984 | tf_op jit(solution)/shard_map/sejd,edf->sejf/dot_general | solution.py:84
  80.1 2.8 fusion.31
  82.9 14.4 %all-to-all-done.2 = bf16[8,1,24,2048]{3,2,1,0:T(8,128)(2,1)} async-done(((bf16[8,1,24,2048]{3,2,1,0:T(8,128)(2,1)}), bf16[8,1,24,2048]{3,2,1,0:T(8,128)(2,1)}, u32[]{:S(2)}, u32[]{:S(2)}) %all-to-all-start.2) | async-done | bytes 786464 | tf_op jit(solution)/shard_map/all_to_all | solution.py:99
  97.3 3.6 %multiply_convert_fusion.1 = (bf16[8,1,24,768]{3,2,0,1:T(8,128)(2,1)S(1)}, bf16[8,24,768]{2,1,0:T(8,128)(2,1)S(1)}, bf16[8,24,768]{2,1,0:T(8,128)(2,1)}) fusion(f32[8,1,24,768]{3,2,0,1:T(8,128)} %fusion.31, f32[8,1,24,768]{3,2,0,1:T(8,128)} %fusion.34, bf16[1,768,2048]{2,1,0:T(8,128)(2,1)S(1)} %copy-done, bf16[8,1,24,2048]{3,2,1,0:T(8,128)(2,1)} %all-to-all-done.2), kind=kOutput, calls=%fused_computation.43 | convolution fusion | flops 606191616 | bytes 5996544 | tf_op jit(solution)/shard_map/sejd,efd->sejf/dot_general | solution.py:100
  105.1 4.2 %all-to-all-start.3 = ((bf16[8,1,24,2048]{3,2,1,0:T(8,128)(2,1)}), bf16[8,1,24,2048]{3,2,1,0:T(8,128)(2,1)}, u32[]{:S(2)}, u32[]{:S(2)}) async-start(bf16[8,1,24,2048]{3,2,1,0:T(8,128)(2,1)} %fusion.24), calls=%async_computation.3 | async-start | bytes 1572864 | tf_op jit(solution)/shard_map/all_to_all | solution.py:113
  109.5 20.8 %all-to-all-done.3 = bf16[8,1,24,2048]{3,2,1,0:T(8,128)(2,1)} async-done(((bf16[8,1,24,2048]{3,2,1,0:T(8,128)(2,1)}), bf16[8,1,24,2048]{3,2,1,0:T(8,128)(2,1)}, u32[]{:S(2)}, u32[]{:S(2)}) %all-to-all-start.3) | async-done | bytes 786464 | tf_op jit(solution)/shard_map/all_to_all | solution.py:113
  132.6 3.9 %fusion.14 = bf16[1,2048,768]{2,1,0:T(8,128)(2,1)} fusion(bf16[8,24,768]{2,1,0:T(8,128)(2,1)} %get-tuple-element.27, bf16[8,1,24,2048]{3,2,1,0:T(8,128)(2,1)} %all-to-all-done.2), kind=kOutput, calls=%fused_computation.20 | convolution fusion | flops 605552640 | bytes 4227072 | tf_op jit(solution)/shard_map/sejd,sejf->edf/dot_general | solution.py:133
  136.6 4.0 %fusion.12 = bf16[1,2048,768]{2,1,0:T(8,128)(2,1)} fusion(bf16[8,1,24,2048]{3,2,1,0:T(8,128)(2,1)} %all-to-all-done, bf16[8,1,24,768]{3,2,0,1:T(8,128)(2,1)} %copy-done.5), kind=kOutput, calls=%fused_computation.18 | convolution fusion | flops 605552640 | bytes 4227072 | tf_op jit(solution)/shard_map/sejd,sejf->edf/dot_general | solution.py:129
  140.8 3.9 %fusion.13 = bf16[1,2048,768]{2,1,0:T(8,128)(2,1)} fusion(bf16[8,24,768]{2,1,0:T(8,128)(2,1)} %copy-done.4, bf16[8,1,24,2048]{3,2,1,0:T(8,128)(2,1)} %all-to-all-done), kind=kOutput, calls=%fused_computation.19 | convolution fusion | flops 605552640 | bytes 4227072 | tf_op jit(solution)/shard_map/sejd,sejf->edf/dot_general | solution.py:132
  144.8 2.6 fusion.27
  147.4 4.2 %all-to-all-start.1 = ((bf16[8,1,24,2048]{3,2,1,0:T(8,128)(2,1)}), bf16[8,1,24,2048]{3,2,1,0:T(8,128)(2,1)}, u32[]{:S(2)}, u32[]{:S(2)}) async-start(bf16[8,1,24,2048]{3,2,1,0:T(8,128)(2,1)} %fusion.27), calls=%async_computation.1 | async-start | bytes 1572864 | tf_op jit(solution)/shard_map/all_to_all | solution.py:98
  151.9 20.7 %all-to-all-done.1 = bf16[8,1,24,2048]{3,2,1,0:T(8,128)(2,1)} async-done(((bf16[8,1,24,2048]{3,2,1,0:T(8,128)(2,1)}), bf16[8,1,24,2048]{3,2,1,0:T(8,128)(2,1)}, u32[]{:S(2)}, u32[]{:S(2)}) %all-to-all-start.1) | async-done | bytes 786464 | tf_op jit(solution)/shard_map/all_to_all | solution.py:98
  172.6 2.5 convolution_convert_fusion.1
  177.4 26.8 %reduce-scatter.8.cloned.1.call-done = bf16[1,512,768]{2,1,0:T(8,128)(2,1)} async-done(((bf16[1,2048,768]{2,1,0:T(8,128)(2,1)}), bf16[1,512,768]{2,1,0:T(8,128)(2,1)}) %reduce-scatter.8.cloned.1.call-update) | async-done | bytes 786448 | tf_op jit(solution)/shard_map/reduce_scatter | solution.py:141
  206.6 3.0 copy.26
  209.7 41.4 %reduce-scatter.4.cloned.1.call-done = bf16[1,512,768]{2,1,0:T(8,128)(2,1)} async-done(((bf16[1,2048,768]{2,1,0:T(8,128)(2,1)}), bf16[1,512,768]{2,1,0:T(8,128)(2,1)}) %reduce-scatter.4.cloned.1.call-update) | async-done | bytes 786448 | tf_op jit(solution)/shard_map/reduce_scatter | solution.py:135
  253.4 44.4 %reduce-scatter.6.cloned.1.call-done = bf16[1,512,768]{2,1,0:T(8,128)(2,1)} async-done(((bf16[1,2048,768]{2,1,0:T(8,128)(2,1)}), bf16[1,512,768]{2,1,0:T(8,128)(2,1)}) %reduce-scatter.6.cloned.1.call-update) | async-done | bytes 786448 | tf_op jit(solution)/shard_map/reduce_scatter | solution.py:138
  (65 shorter events, 28.5 us)
Async XLA Ops:
  7.2 90.1 %copy-start = (bf16[1,768,2048]{2,1,0:T(8,128)(2,1)S(1)}, bf16[1,768,2048]{2,1,0:T(8,128)(2,1)}, u32[]{:S(2)}) copy-start(bf16[1,768,2048]{2,1,0:T(8,128)(2,1)} %param.14) | copy-start | bytes 9437188
  7.2 32.6 %all-gather.6.cloned.1.call-start = ((), (), s32[]{:S(2)}) async-start(), calls=%async_computation.10 | async-start | bytes 1310720 | tf_op jit(solution)/shard_map/all_gather | solution.py:30
  42.1 8.5 %copy-start.8 = (s32[1,4]{1,0:T(1,128)S(1)}, s32[1,4]{1,0:T(1,128)}, u32[]{:S(2)}) copy-start(s32[1,4]{1,0:T(1,128)} %param.18) | copy-start | bytes 52
  46.0 25.7 %all-to-all-start = ((bf16[8,1,24,2048]{3,2,1,0:T(8,128)(2,1)}), bf16[8,1,24,2048]{3,2,1,0:T(8,128)(2,1)}, u32[]{:S(2)}, u32[]{:S(2)}) async-start(bf16[8,1,24,2048]{3,2,1,0:T(8,128)(2,1)} %bitcast.155), calls=%async_computation | async-start | bytes 1572864 | tf_op jit(solution)/shard_map/all_to_all | solution.py:82
  64.9 3.9 %copy-start.6 = (f32[1,8,24]{2,1,0:T(8,128)S(1)}, f32[1,8,24]{2,1,0:T(8,128)}, u32[]{:S(2)}) copy-start(f32[1,8,24]{2,1,0:T(8,128)} %param.17) | copy-start | bytes 2308
  64.9 3.9 %copy-start.9 = (s32[1,8]{1,0:T(1,128)S(1)}, s32[1,8]{1,0:T(1,128)}, u32[]{:S(2)}) copy-start(s32[1,8]{1,0:T(1,128)} %param.16) | copy-start | bytes 100
  71.7 25.6 %all-to-all-start.2 = ((bf16[8,1,24,2048]{3,2,1,0:T(8,128)(2,1)}), bf16[8,1,24,2048]{3,2,1,0:T(8,128)(2,1)}, u32[]{:S(2)}, u32[]{:S(2)}) async-start(bf16[8,1,24,2048]{3,2,1,0:T(8,128)(2,1)} %fusion.30), calls=%async_computation.2 | async-start | bytes 1572864 | tf_op jit(solution)/shard_map/all_to_all | solution.py:99
  76.2 3.9 %copy-start.2 = (bf16[1,2048,768]{2,1,0:T(8,128)(2,1)S(1)}, bf16[1,2048,768]{2,1,0:T(8,128)(2,1)}, u32[]{:S(2)}) copy-start(bf16[1,2048,768]{2,1,0:T(8,128)(2,1)} %param.12) | copy-start | bytes 9437188
  97.3 3.7 %copy-start.1 = (bf16[1,2048,768]{2,1,0:T(8,128)(2,1)S(1)}, bf16[1,2048,768]{2,1,0:T(8,128)(2,1)}, u32[]{:S(2)}) copy-start(bf16[1,2048,768]{2,1,0:T(8,128)(2,1)} %param.13) | copy-start | bytes 9437188
  101.0 1.2 copy-start.4
  101.0 1.2 copy-start.5
  101.0 2.1 copy-start.3
  103.1 6.4 %copy-start.7 = (s32[1,8,24]{2,1,0:T(8,128)S(1)}, s32[1,8,24]{2,1,0:T(8,128)}, u32[]{:S(2)}) copy-start(s32[1,8,24]{2,1,0:T(8,128)} %param.15) | copy-start | bytes 2308
  105.1 25.2 %all-to-all-start.3 = ((bf16[8,1,24,2048]{3,2,1,0:T(8,128)(2,1)}), bf16[8,1,24,2048]{3,2,1,0:T(8,128)(2,1)}, u32[]{:S(2)}, u32[]{:S(2)}) async-start(bf16[8,1,24,2048]{3,2,1,0:T(8,128)(2,1)} %fusion.24), calls=%async_computation.3 | async-start | bytes 1572864 | tf_op jit(solution)/shard_map/all_to_all | solution.py:113
  109.4 65.7 %all-gather.8.cloned.1.call-start = ((), (), s32[]{:S(2)}) async-start(), calls=%async_computation.11 | async-start | bytes 1310720 | tf_op jit(solution)/shard_map/all_gather | solution.py:38
  132.6 71.7 %reduce-scatter.8.cloned.1.call-start = ((), (), s32[]{:S(2)}) async-start(), calls=%async_computation.9 | async-start | bytes 3932160 | tf_op jit(solution)/shard_map/reduce_scatter | solution.py:141
  136.5 114.5 %reduce-scatter.4.cloned.1.call-start = ((), (), s32[]{:S(2)}) async-start(), calls=%async_computation.7 | async-start | bytes 3932160 | tf_op jit(solution)/shard_map/reduce_scatter | solution.py:135
  140.6 157.3 %reduce-scatter.6.cloned.1.call-start = ((), (), s32[]{:S(2)}) async-start(), calls=%async_computation.8 | async-start | bytes 3932160 | tf_op jit(solution)/shard_map/reduce_scatter | solution.py:138
  147.4 25.2 %all-to-all-start.1 = ((bf16[8,1,24,2048]{3,2,1,0:T(8,128)(2,1)}), bf16[8,1,24,2048]{3,2,1,0:T(8,128)(2,1)}, u32[]{:S(2)}, u32[]{:S(2)}) async-start(bf16[8,1,24,2048]{3,2,1,0:T(8,128)(2,1)} %fusion.27), calls=%async_computation.1 | async-start | bytes 1572864 | tf_op jit(solution)/shard_map/all_to_all | solution.py:98
Sparse Core Ops, SparseCore 0:
  10.4 29.3 all-gather.5
  132.7 24.5 all-gather.7
  160.3 43.9 reduce-scatter.7
  207.1 43.9 reduce-scatter.3
  253.9 43.9 reduce-scatter.5
where the time goes:
time: 308 us; the launch traced here: 307 us
  waiting for transfers between devices  197 us (64%)
  matrix products  31.9 us (10%)
  local copies, waits for them, and re-layouts  18.6 us (6%)
  starting transfers between devices  17.9 us (6%)
  other arithmetic  17.6 us (6%)
  between operations  15.2 us (5%)
  blocking collectives  8.9 us (3%)
    reduce_scatter x1, waiting for transfers between devices, per_device(): lax.psum_scatter(part_up.astype(jnp.bfloat16), 'dp', scatter_dimension=1,...  44.4 us
    reduce_scatter x1, waiting for transfers between devices, per_device(): lax.psum_scatter(part_gate.astype(jnp.bfloat16), 'dp', scatter_dimension=...  41.4 us
    all_gather x1, waiting for transfers between devices, forward_pairs(): lax.all_gather(moved_rows[None], 'dp', axis=0, tiled=True)  27.3 us
    reduce_scatter x1, waiting for transfers between devices, per_device(): lax.psum_scatter(part_down.astype(jnp.bfloat16), 'dp', scatter_dimension=...  26.8 us
    all_to_all x1, waiting for transfers between devices, per_device(): lax.all_to_all(token_rows, 'expert', split_axis=0, concat_axis=0, tiled=T...  20.8 us
    all_to_all x1, waiting for transfers between devices, per_device(): lax.all_to_all(expert_out, 'expert', split_axis=0, concat_axis=0, tiled=T...  20.7 us
    all_to_all x1, waiting for transfers between devices, per_device(): lax.all_to_all(weighted, 'expert', split_axis=0, concat_axis=0, tiled=True)  14.4 us
    unnamed x1, blocking collectives  8.9 us
  transfers between devices with their start and end apart: 9, of which 8 were waited for; matrix products, arithmetic and copies ran while one was open for 16% of the time, Pallas kernels for 0%

commit v1 on v0

v1 whole, which is shorter than its diff:
```python
import functools

import jax
import jax.numpy as jnp
from jax import lax
from jax.experimental import pallas as pl
from jax.experimental.pallas import tpu as pltpu
from jax.sharding import PartitionSpec as P

F32 = jnp.float32
BF16 = jnp.bfloat16
VMEM = pltpu.VMEM
WHOLE = pl.BlockSpec(memory_space=pltpu.VMEM)
SCALARS = pl.BlockSpec(memory_space=pltpu.SMEM)
TILE = 256
LIMIT = 56 * 1024 * 1024


def params():
    return pltpu.CompilerParams(vmem_limit_bytes=LIMIT)


def cost(flops, bytes_accessed):
    return pl.CostEstimate(flops=int(flops), bytes_accessed=int(bytes_accessed), transcendentals=0)


def xor_permute(array, axis, key):
    size = lax.axis_size(axis)
    return lax.ppermute(array, axis, [(i, i ^ key) for i in range(size)])


def column_of(row, length):
    diagonal = lax.broadcasted_iota(jnp.int32, (length, length), 0) == lax.broadcasted_iota(
        jnp.int32, (length, length), 1
    )
    spread = jnp.where(diagonal, jnp.broadcast_to(row.astype(F32), (length, length)), 0.0)
    return jnp.sum(spread, axis=1, keepdims=True)


def relative_columns(table_ref, me, window, capacity):
    return jnp.concatenate(
        [column_of(table_ref[0, pl.ds(me ^ d, 1), :], capacity) for d in range(window)], axis=0
    )


def slot_onehot(rows_ref, me, window, capacity, tok_dev):
    index = relative_columns(rows_ref, me, window, capacity).astype(jnp.int32)
    lanes = lax.broadcasted_iota(jnp.int32, (window * capacity, tok_dev), 1)
    return lanes == index


def counted_gates(gates_ref, counts_ref, me, window, capacity):
    parts = []
    for d in range(window):
        slot = lax.broadcasted_iota(jnp.int32, (1, capacity), 1)
        gate = gates_ref[0, pl.ds(me ^ d, 1), :]
        gate = jnp.where(slot < counts_ref[0, me ^ d], gate, 0.0)
        parts.append(column_of(gate, capacity))
    return jnp.concatenate(parts, axis=0)


def keep_valid(values, lengths_ref, first_slot, slot_len):
    rows = lax.broadcasted_iota(jnp.int32, values.shape, 0)
    limit = jnp.zeros(values.shape, jnp.int32)
    for slot in range(values.shape[0] // slot_len):
        limit = jnp.where(
            rows // slot_len == slot, slot * slot_len + lengths_ref[0, first_slot + slot], limit
        )
    return jnp.where(rows < limit, values.astype(F32), 0.0).astype(values.dtype)


def prepare_kernel(sizes, rows_ref, gates_ref, counts_ref, lengths_ref, cot_ref, tok_ref, *outs):
    window, capacity, tok_dev, slot_len = sizes
    me = lax.axis_index("expert")
    moved_ref, outs = outs[0], outs[1:]
    half = tok_dev // 2
    moved_ref[...] = keep_valid(tok_ref[...], lengths_ref, half // slot_len, slot_len)
    hit = slot_onehot(rows_ref, me, window, capacity, tok_dev).astype(BF16)
    gate = counted_gates(gates_ref, counts_ref, me, window, capacity)
    picked = jnp.dot(hit, cot_ref[...], preferred_element_type=F32)
    weighted = (gate * picked).astype(BF16)
    for z, out in enumerate(outs):
        out[...] = weighted[z * 2 * capacity : (z + 1) * 2 * capacity]


def prepare(slot_rows, slot_gates, slot_counts, seq_lengths, cotangent, tokens):
    tok_dev, width = tokens.shape
    window, capacity = slot_rows.shape[1:]
    half = tok_dev // 2
    slot_len = tok_dev // seq_lengths.shape[1]
    sizes = (window, capacity, tok_dev, slot_len)
    return pl.pallas_call(
        functools.partial(prepare_kernel, sizes),
        grid=(1,),
        out_shape=[jax.ShapeDtypeStruct((half, width), BF16)]
        + [jax.ShapeDtypeStruct((2 * capacity, width), BF16)] * (window // 2),
        in_specs=[
            pl.BlockSpec(slot_rows.shape, lambda i: (0, 0, 0)),
            pl.BlockSpec(slot_gates.shape, lambda i: (0, 0, 0)),
            SCALARS,
            SCALARS,
            pl.BlockSpec(cotangent.shape, lambda i: (0, 0)),
            pl.BlockSpec((half, width), lambda i: (1, 0)),
        ],
        out_specs=[pl.BlockSpec((half, width), lambda i: (0, 0))]
        + [pl.BlockSpec((2 * capacity, width), lambda i: (0, 0))] * (window // 2),
        compiler_params=params(),
        cost_estimate=cost(2 * window * capacity * tok_dev * width, 5 * tok_dev * width),
        name="prepare",
    )(slot_rows, slot_gates, slot_counts, seq_lengths, cotangent, tokens)


def chosen(key, refs):
    value = refs[0][...].astype(F32)
    for i in range(1, len(refs)):
        value = jnp.where(key == i + 1, refs[i][...].astype(F32), value)
    return value.astype(BF16)


def pick_kernel(sizes, rows_ref, lengths_ref, matching_ref, tok_ref, *refs):
    window, capacity, tok_dev, slot_len, partners = sizes
    me = lax.axis_index("expert")
    arrived, outs = refs[:partners], refs[partners:]
    key = matching_ref[0, 0]
    low = keep_valid(tok_ref[...], lengths_ref, 0, slot_len)
    shuffled = jnp.concatenate([low, chosen(key, arrived)], axis=0)
    hit = slot_onehot(rows_ref, me, window, capacity, tok_dev).astype(BF16)
    picked = jnp.dot(hit, shuffled, preferred_element_type=F32).astype(BF16)
    for z, out in enumerate(outs):
        out[...] = picked[z * 2 * capacity : (z + 1) * 2 * capacity]


def pick(slot_rows, seq_lengths, matching, tokens, arrived):
    tok_dev, width = tokens.shape
    window, capacity = slot_rows.shape[1:]
    half = tok_dev // 2
    slot_len = tok_dev // seq_lengths.shape[1]
    sizes = (window, capacity, tok_dev, slot_len, len(arrived))
    return pl.pallas_call(
        functools.partial(pick_kernel, sizes),
        grid=(1,),
        out_shape=[jax.ShapeDtypeStruct((2 * capacity, width), BF16)] * (window // 2),
        in_specs=[
            pl.BlockSpec(slot_rows.shape, lambda i: (0, 0, 0)),
            SCALARS,
            SCALARS,
            pl.BlockSpec((half, width), lambda i: (0, 0)),
        ]
        + [pl.BlockSpec((half, width), lambda i: (0, 0))] * len(arrived),
        out_specs=[pl.BlockSpec((2 * capacity, width), lambda i: (0, 0))] * (window // 2),
        compiler_params=params(),
        cost_estimate=cost(2 * window * capacity * tok_dev * width, 5 * tok_dev * width),
        name="pick",
    )(slot_rows, seq_lengths, matching, tokens, *arrived)


def joined(direct, crossed, capacity):
    rows = lax.broadcasted_iota(jnp.int32, direct.shape, 0)
    return jnp.where(rows < capacity, direct[...].astype(F32), crossed[...].astype(F32)).astype(BF16)


def expert_kernel(sizes, *refs):
    count, capacity, steps, replicas, share = sizes
    x_refs, w_refs = refs[: 2 * count], refs[2 * count : 4 * count]
    gate_ref, up_ref, down_ref = refs[4 * count : 4 * count + 3]
    outs = refs[4 * count + 3 :]
    tok_refs, out_refs = outs[:count], outs[count : 2 * count]
    slice_refs = outs[2 * count : 2 * count + replicas]
    acts_ref, x_all, w_all, tok_sum, out_sum = outs[2 * count + replicas :]
    step = pl.program_id(0)
    pair = 2 * capacity

    @pl.when(step == 0)
    def _():
        for z in range(count):
            rows = slice(z * pair, (z + 1) * pair)
            x_all[rows, :] = joined(x_refs[2 * z], x_refs[2 * z + 1], capacity)
            w_all[rows, :] = joined(w_refs[2 * z], w_refs[2 * z + 1], capacity)
        me = lax.axis_index("dp")
        for j in range(replicas):
            columns = pl.ds(pl.multiple_of((me ^ j) * share, share), share)
            slice_refs[j][:, :share] = x_all[:, columns]
            slice_refs[j][:, share:] = w_all[:, columns]

    x, w = x_all[...], w_all[...]
    w_gate, w_up, w_down = gate_ref[0], up_ref[0], down_ref[0]
    pre_gate = jnp.dot(x, w_gate, preferred_element_type=F32)
    pre_up = jnp.dot(x, w_up, preferred_element_type=F32)
    turned = (((1,), (1,)), ((), ()))
    grad_hidden = lax.dot_general(w, w_down, turned, preferred_element_type=F32)
    sig = jax.nn.sigmoid(pre_gate)
    silu = pre_gate * sig
    hidden = (silu * pre_up).astype(BF16)
    grad_gate = (grad_hidden * pre_up * sig * (1.0 + pre_gate * (1.0 - sig))).astype(BF16)
    grad_up = (grad_hidden * silu).astype(BF16)
    acts_ref[...] = jnp.concatenate([hidden, grad_gate, grad_up], axis=1)
    tok = lax.dot_general(grad_gate, w_gate, turned, preferred_element_type=F32)
    tok += lax.dot_general(grad_up, w_up, turned, preferred_element_type=F32)
    out = jnp.dot(hidden, w_down, preferred_element_type=F32)

    @pl.when(step == 0)
    def _():
        tok_sum[...] = tok
        out_sum[...] = out

    @pl.when(step > 0)
    def _():
        tok_sum[...] += tok
        out_sum[...] += out

    @pl.when(step == steps - 1)
    def _():
        for z in range(count):
            rows = slice(z * pair, (z + 1) * pair)
            tok_refs[z][...] = tok_sum[rows, :].astype(BF16)
            out_refs[z][...] = out_sum[rows, :].astype(BF16)


def expert(x_pairs, w_pairs, w_gate, w_up, w_down, capacity):
    count = len(x_pairs)
    pair, width = x_pairs[0][0].shape
    hidden_units = w_gate.shape[2]
    rows = count * pair
    replicas = lax.axis_size("dp")
    share = width // replicas
    tile = TILE
    steps = hidden_units // tile
    sizes = (count, capacity, steps, replicas, share)
    flat = [a for p in x_pairs for a in p] + [a for p in w_pairs for a in p]
    fixed = lambda f: (0, 0)
    block = jax.ShapeDtypeStruct((pair, width), BF16)
    acts = jax.ShapeDtypeStruct((rows, 3 * hidden_units), BF16)
    results = pl.pallas_call(
        functools.partial(expert_kernel, sizes),
        grid=(steps,),
        out_shape=[block] * (2 * count)
        + [jax.ShapeDtypeStruct((rows, 2 * share), BF16)] * replicas
        + [acts],
        in_specs=[pl.BlockSpec((pair, width), fixed)] * (4 * count)
        + [
            pl.BlockSpec((1, width, tile), lambda f: (0, 0, f)),
            pl.BlockSpec((1, width, tile), lambda f: (0, 0, f)),
            pl.BlockSpec((1, tile, width), lambda f: (0, f, 0)),
        ],
        out_specs=[pl.BlockSpec((pair, width), fixed)] * (2 * count)
        + [pl.BlockSpec((rows, 2 * share), fixed)] * replicas
        + [pl.BlockSpec((rows, 3 * tile), lambda f: (0, f))],
        scratch_shapes=[
            VMEM((rows, width), BF16),
            VMEM((rows, width), BF16),
            VMEM((rows, width), F32),
            VMEM((rows, width), F32),
        ],
        compiler_params=params(),
        cost_estimate=cost(
            12 * rows * width * hidden_units, 6 * width * hidden_units + 10 * rows * width
        ),
        name="expert",
    )(*flat, w_gate, w_up, w_down)
    token_rows, expert_out = results[:count], results[count : 2 * count]
    slices = results[2 * count : 2 * count + replicas]
    return token_rows, expert_out, slices, results[-1]


def weight_kernel(sizes, *refs):
    parts, share, tile = sizes
    slices, acts = refs[:parts], refs[parts : 2 * parts]
    gate_out, up_out, down_out = refs[2 * parts :]
    across = (((0,), (0,)), ((), ()))
    x = jnp.concatenate([s[:, :share] for s in slices], axis=0)
    w = jnp.concatenate([s[:, share:] for s in slices], axis=0)
    hidden = jnp.concatenate([a[:, :tile] for a in acts], axis=0)
    grad_gate = jnp.concatenate([a[:, tile : 2 * tile] for a in acts], axis=0)
    grad_up = jnp.concatenate([a[:, 2 * tile :] for a in acts], axis=0)
    gate_out[0] = lax.dot_general(x, grad_gate, across, preferred_element_type=F32)
    up_out[0] = lax.dot_general(x, grad_up, across, preferred_element_type=F32)
    down_out[0] = lax.dot_general(hidden, w, across, preferred_element_type=F32)


def weight_grads(slices, acts):
    parts = len(slices)
    share = slices[0].shape[1] // 2
    hidden_units = acts[0].shape[1] // 3
    tile = TILE
    rows = sum(s.shape[0] for s in slices)
    return pl.pallas_call(
        functools.partial(weight_kernel, (parts, share, tile)),
        grid=(hidden_units // tile,),
        out_shape=[
            jax.ShapeDtypeStruct((1, share, hidden_units), F32),
            jax.ShapeDtypeStruct((1, share, hidden_units), F32),
            jax.ShapeDtypeStruct((1, hidden_units, share), F32),
        ],
        in_specs=[pl.BlockSpec(s.shape, lambda f: (0, 0)) for s in slices]
        + [pl.BlockSpec((a.shape[0], 3 * tile), lambda f: (0, f)) for a in acts],
        out_specs=[
            pl.BlockSpec((1, share, tile), lambda f: (0, 0, f)),
            pl.BlockSpec((1, share, tile), lambda f: (0, 0, f)),
            pl.BlockSpec((1, tile, share), lambda f: (0, f, 0)),
        ],
        compiler_params=params(),
        cost_estimate=cost(6 * rows * share * hidden_units, 12 * share * hidden_units),
        name="weight_grads",
    )(*slices, *acts)


def assemble(refs, capacity):
    return jnp.concatenate(
        [joined(refs[2 * z], refs[2 * z + 1], capacity) for z in range(len(refs) // 2)], axis=0
    )


def output_kernel(sizes, rows_ref, gates_ref, counts_ref, *refs):
    window, capacity, tok_dev = sizes
    me = lax.axis_index("expert")
    hit = slot_onehot(rows_ref, me, window, capacity, tok_dev)
    gate = counted_gates(gates_ref, counts_ref, me, window, capacity)
    table = jnp.where(hit, jnp.broadcast_to(gate, hit.shape), 0.0)
    high = table.astype(BF16)
    low = (table - high.astype(F32)).astype(BF16)
    rows = assemble(refs[:-1], capacity)
    across = (((0,), (0,)), ((), ()))
    total = lax.dot_general(high, rows, across, preferred_element_type=F32)
    total += lax.dot_general(low, rows, across, preferred_element_type=F32)
    refs[-1][...] = total.astype(BF16)


def combine_output(slot_rows, slot_gates, slot_counts, pairs, tok_dev):
    window, capacity = slot_rows.shape[1:]
    flat = [a for p in pairs for a in p]
    width = flat[0].shape[1]
    return pl.pallas_call(
        functools.partial(output_kernel, (window, capacity, tok_dev)),
        out_shape=jax.ShapeDtypeStruct((tok_dev, width), BF16),
        in_specs=[WHOLE, WHOLE, SCALARS] + [WHOLE] * len(flat),
        out_specs=WHOLE,
        compiler_params=params(),
        cost_estimate=cost(4 * window * capacity * tok_dev * width, 6 * tok_dev * width),
        name="combine_output",
    )(slot_rows, slot_gates, slot_counts, *flat)


def grads_kernel(sizes, rows_ref, *refs):
    window, capacity, tok_dev = sizes
    me = lax.axis_index("expert")
    hit = slot_onehot(rows_ref, me, window, capacity, tok_dev).astype(BF16)
    rows = assemble(refs[:-2], capacity)
    across = (((0,), (0,)), ((), ()))
    total = lax.dot_general(hit, rows, across, preferred_element_type=F32).astype(BF16)
    refs[-2][...] = total[: tok_dev // 2]
    refs[-1][...] = total[tok_dev // 2 :]


def combine_grads(slot_rows, pairs, tok_dev):
    window, capacity = slot_rows.shape[1:]
    flat = [a for p in pairs for a in p]
    width = flat[0].shape[1]
    half = jax.ShapeDtypeStruct((tok_dev // 2, width), BF16)
    return pl.pallas_call(
        functools.partial(grads_kernel, (window, capacity, tok_dev)),
        out_shape=[half, half],
        in_specs=[WHOLE] * (1 + len(flat)),
        out_specs=[WHOLE, WHOLE],
        compiler_params=params(),
        cost_estimate=cost(2 * window * capacity * tok_dev * width, 6 * tok_dev * width),
        name="combine_grads",
    )(slot_rows, *flat)


def finish_kernel(matching_ref, low_ref, *refs):
    out_ref = refs[-1]
    half = low_ref.shape[0]
    out_ref[:half] = low_ref[...]
    out_ref[half:] = chosen(matching_ref[0, 0], refs[:-1])


def finish(matching, low, arrived):
    half, width = low.shape
    return pl.pallas_call(
        finish_kernel,
        out_shape=jax.ShapeDtypeStruct((2 * half, width), BF16),
        in_specs=[SCALARS, WHOLE] + [WHOLE] * len(arrived),
        out_specs=WHOLE,
        compiler_params=params(),
        cost_estimate=cost(0, 10 * half * width),
        name="finish",
    )(matching, low, *arrived)


def exchange(blocks):
    direct = {0: blocks[0]}
    for z in range(len(blocks) - 1, 0, -1):
        direct[z] = xor_permute(blocks[z], "expert", 2 * z)
    return [(direct[z], xor_permute(direct[z], "expert", 1)) for z in range(len(blocks))]


def spread(array):
    return [array] + [xor_permute(array, "dp", j) for j in range(1, lax.axis_size("dp"))]


def per_device(
    tokens,
    cotangent,
    w_gate,
    w_up,
    w_down,
    slot_rows,
    slot_counts,
    slot_gates,
    seq_lengths,
    matching,
):
    tok_dev = tokens.shape[0]
    capacity = slot_rows.shape[2]
    replicas = lax.axis_size("dp")
    moved, *weighted = prepare(slot_rows, slot_gates, slot_counts, seq_lengths, cotangent, tokens)
    w_pairs = exchange(weighted)
    arrived = spread(moved)[1:]
    picked = pick(slot_rows, seq_lengths, matching, tokens, arrived)
    x_pairs = exchange(picked)
    token_rows, expert_out, slices, acts = expert(x_pairs, w_pairs, w_gate, w_up, w_down, capacity)
    tok_pairs = exchange(token_rows)
    out_pairs = exchange(expert_out)
    all_slices = [slices[0]] + [xor_permute(slices[j], "dp", j) for j in range(1, replicas)]
    all_acts = spread(acts)
    low, high = combine_grads(slot_rows, tok_pairs, tok_dev)
    grad_tokens = finish(matching, low, spread(high)[1:])
    grads = weight_grads(all_slices, all_acts)
    output = combine_output(slot_rows, slot_gates, slot_counts, out_pairs, tok_dev)
    return (output, grad_tokens, *grads)


def solution(mesh):
    return jax.shard_map(
        per_device,
        mesh=mesh,
        in_specs=(
            P(("dp", "expert"), None),
            P(("dp", "expert"), None),
            P("expert", None, None),
            P("expert", None, None),
            P("expert", None, None),
            P(("dp", "expert"), None, None),
            P(("dp", "expert"), None),
            P(("dp", "expert"), None, None),
            P(("dp", "expert"), None),
            P("expert", None),
        ),
        out_specs=(
            P(("dp", "expert"), None),
            P(("dp", "expert"), None),
            P("expert", "dp", None),
            P("expert", "dp", None),
            P("expert", None, "dp"),
        ),
        check_vma=False,
    )
```

time: 308 us -> 185 us (0.60)
  the two profiles are of different devices: /device:TPU:0 before, /device:TPU:8 now
where the time goes in v1:
time: 185 us; the launch traced here: 184 us
  waiting for transfers between devices  116 us (63%)
  Pallas kernels  32.5 us (18%)
  starting transfers between devices  31.5 us (17%)
  local copies, waits for them, and re-layouts  3.79 us (2%)
    ppermute x40, waiting for transfers between devices, xor_permute(): return lax.ppermute(array, axis, [(i, i ^ key) for i in range(size)])  116 us
    ppermute x40, starting transfers between devices, xor_permute(): return lax.ppermute(array, axis, [(i, i ^ key) for i in range(size)])  31.5 us
    pallas_call x1, Pallas kernels, expert(): pl.pallas_call(functools.partial(expert_kernel, sizes), grid=(steps,), ou...  13.2 us
    pallas_call x1, Pallas kernels, weight_grads(): pl.pallas_call(functools.partial(weight_kernel, (parts, share, tile)), gr...  6.12 us
    unnamed x80, local copies, waits for them, and re-layouts  3.79 us
  transfers between devices with their start and end apart: 40, of which 20 were waited for; matrix products, arithmetic and copies ran while one was open for 0% of the time, Pallas kernels for 6%

profile of v1, /device:TPU:8, one launch (start us, length us, event | category | flops | bytes accessed | tf_op | source)
XLA Modules:
  0.0 184.4 jit_solution(10921347278569113469)
XLA Ops:
  0.6 2.6 %prepare.1 = (bf16[64,2048]{1,0:T(8,128)(2,1)}, bf16[48,2048]{1,0:T(8,128)(2,1)}, bf16[48,2048]{1,0:T(8,128)(2,1)}, bf16[48,2048]{1,0:T(8,128)(2,1)}, bf16[48,2048]{1,0:T(8,128)(2,1)}) custom-call(s32[1,8,24]{2,1,0:T(8,128)} %rows_ref.7, f32[1,8,24]{2,1,0:T(8,128)} %gates_ref.3, s32[1,8]{1,0:T(1,128)} %counts_ref.3, s32[1,4]{1,0:T(1,128)} %lengths_ref.3, ...), custom_call_target="tpu_custom_call" | custom-call | flops 100663296 | bytes 1310720 | tf_op jit(solution)/shard_map/prepare/pallas_call | solution.py:92
  3.3 3.0 %collective-permute-start.13 = (bf16[48,2048]{1,0:T(8,128)(2,1)}, bf16[48,2048]{1,0:T(8,128)(2,1)S(1)}, u32[]{:S(2)}, u32[]{:S(2)}) collective-permute-start(bf16[48,2048]{1,0:T(8,128)(2,1)} %get-tuple-element.39), channel_id=1, source_target_pairs={{0,4},{1,5},{2,6},{3,7},{4,0},{5,1},{6,2},{7,3},{8,12},{9,13},{10,... | collective-permute-start | bytes 589832 | tf_op jit(solution)/shard_map/ppermute | solution.py:29
  6.3 2.4 %collective-permute-start.2 = (bf16[64,2048]{1,0:T(8,128)(2,1)}, bf16[64,2048]{1,0:T(8,128)(2,1)S(1)}, u32[]{:S(2)}, u32[]{:S(2)}) collective-permute-start(bf16[64,2048]{1,0:T(8,128)(2,1)} %get-tuple-element.32), channel_id=1, source_target_pairs={{0,24},{8,16},{16,8},{24,0},{1,25},{9,17},{17,9},{25,1},{2,26},{10... | collective-permute-start | bytes 786440 | tf_op jit(solution)/shard_map/ppermute | solution.py:29
  9.8 2.3 %collective-permute-done.11.refs_10_ = bf16[48,2048]{1,0:T(8,128)(2,1)S(1)} collective-permute-done((bf16[48,2048]{1,0:T(8,128)(2,1)}, bf16[48,2048]{1,0:T(8,128)(2,1)S(1)}, u32[]{:S(2)}, u32[]{:S(2)}) %collective-permute-start.11) | collective-permute-done | bytes 196640 | tf_op jit(solution)/shard_map/ppermute | solution.py:29
  16.7 3.8 %collective-permute-done.1.refs_1_ = bf16[64,2048]{1,0:T(8,128)(2,1)S(1)} collective-permute-done((bf16[64,2048]{1,0:T(8,128)(2,1)}, bf16[64,2048]{1,0:T(8,128)(2,1)S(1)}, u32[]{:S(2)}, u32[]{:S(2)}) %collective-permute-start.1) | collective-permute-done | bytes 262176 | tf_op jit(solution)/shard_map/ppermute | solution.py:29
  21.9 2.7 %pick.1 = (bf16[48,2048]{1,0:T(8,128)(2,1)}, bf16[48,2048]{1,0:T(8,128)(2,1)}, bf16[48,2048]{1,0:T(8,128)(2,1)}, bf16[48,2048]{1,0:T(8,128)(2,1)}) custom-call(s32[1,8,24]{2,1,0:T(8,128)} %rows_ref.7, s32[1,4]{1,0:T(1,128)} %lengths_ref.3, s32[1,4]{1,0:T(1,128)} %matching_ref.3, bf16[128,2048]{1,0:T(8,128)(2,1)} %tok_ref.3, bf16[64,2048]{1,0:T(8,128)(2,1)} %copy-done.3, ...), custom_call_target="tpu_custom_call" | custom-call | flops 100663296 | bytes 1310720 | tf_op jit(solution)/shard_map/pick/pallas_call | solution.py:139
  28.6 5.2 %collective-permute-done.4.refs_2_ = bf16[48,2048]{1,0:T(8,128)(2,1)S(1)} collective-permute-done((bf16[48,2048]{1,0:T(8,128)(2,1)}, bf16[48,2048]{1,0:T(8,128)(2,1)S(1)}, u32[]{:S(2)}, u32[]{:S(2)}) %collective-permute-start.4) | collective-permute-done | bytes 196640 | tf_op jit(solution)/shard_map/ppermute | solution.py:29
  33.8 6.8 %collective-permute-done.6.refs_4_ = bf16[48,2048]{1,0:T(8,128)(2,1)S(1)} collective-permute-done((bf16[48,2048]{1,0:T(8,128)(2,1)}, bf16[48,2048]{1,0:T(8,128)(2,1)S(1)}, u32[]{:S(2)}, u32[]{:S(2)}) %collective-permute-start.6) | collective-permute-done | bytes 196640 | tf_op jit(solution)/shard_map/ppermute | solution.py:29
  40.6 4.9 %collective-permute-done.8.refs_6_ = bf16[48,2048]{1,0:T(8,128)(2,1)S(1)} collective-permute-done((bf16[48,2048]{1,0:T(8,128)(2,1)}, bf16[48,2048]{1,0:T(8,128)(2,1)S(1)}, u32[]{:S(2)}, u32[]{:S(2)}) %collective-permute-start.8) | collective-permute-done | bytes 196640 | tf_op jit(solution)/shard_map/ppermute | solution.py:29
  47.7 13.2 %expert.1 = (bf16[48,2048]{1,0:T(8,128)(2,1)}, bf16[48,2048]{1,0:T(8,128)(2,1)}, bf16[48,2048]{1,0:T(8,128)(2,1)}, bf16[48,2048]{1,0:T(8,128)(2,1)}, bf16[48,204...) custom-call(bf16[48,2048]{1,0:T(8,128)(2,1)} %get-tuple-element.33.r, ...), custom_call_target="tpu_custom_call" | custom-call | flops 3623878656 | bytes 13369344 | tf_op jit(solution)/shard_map/expert/pallas_call | solution.py:233
  63.1 2.9 %collective-permute-start.27 = (bf16[48,2048]{1,0:T(8,128)(2,1)}, bf16[48,2048]{1,0:T(8,128)(2,1)S(1)}, u32[]{:S(2)}, u32[]{:S(2)}) collective-permute-start(bf16[48,2048]{1,0:T(8,128)(2,1)} %get-tuple-element.47), channel_id=1, source_target_pairs={{0,4},{1,5},{2,6},{3,7},{4,0},{5,1},{6,2},{7,3},{8,12},{9,13},{10,... | collective-permute-start | bytes 589832 | tf_op jit(solution)/shard_map/ppermute | solution.py:29
  66.4 3.1 %collective-permute-done.18.refs_2_ = bf16[48,2048]{1,0:T(8,128)(2,1)S(1)} collective-permute-done((bf16[48,2048]{1,0:T(8,128)(2,1)}, bf16[48,2048]{1,0:T(8,128)(2,1)S(1)}, u32[]{:S(2)}, u32[]{:S(2)}) %collective-permute-start.18) | collective-permute-done | bytes 196640 | tf_op jit(solution)/shard_map/ppermute | solution.py:29
  73.1 4.3 %collective-permute-done.25.refs_2_ = bf16[48,2048]{1,0:T(8,128)(2,1)S(1)} collective-permute-done((bf16[48,2048]{1,0:T(8,128)(2,1)}, bf16[48,2048]{1,0:T(8,128)(2,1)S(1)}, u32[]{:S(2)}, u32[]{:S(2)}) %collective-permute-start.25) | collective-permute-done | bytes 196640 | tf_op jit(solution)/shard_map/ppermute | solution.py:29
  77.5 12.2 %collective-permute-done.27.refs_4_ = bf16[48,2048]{1,0:T(8,128)(2,1)S(1)} collective-permute-done((bf16[48,2048]{1,0:T(8,128)(2,1)}, bf16[48,2048]{1,0:T(8,128)(2,1)S(1)}, u32[]{:S(2)}, u32[]{:S(2)}) %collective-permute-start.27) | collective-permute-done | bytes 196640 | tf_op jit(solution)/shard_map/ppermute | solution.py:29
  89.7 6.1 %collective-permute-done.29.refs_6_ = bf16[48,2048]{1,0:T(8,128)(2,1)S(1)} collective-permute-done((bf16[48,2048]{1,0:T(8,128)(2,1)}, bf16[48,2048]{1,0:T(8,128)(2,1)S(1)}, u32[]{:S(2)}, u32[]{:S(2)}) %collective-permute-start.29) | collective-permute-done | bytes 196640 | tf_op jit(solution)/shard_map/ppermute | solution.py:29
  95.8 3.1 %collective-permute-done.22.refs_6_ = bf16[48,2048]{1,0:T(8,128)(2,1)S(1)} collective-permute-done((bf16[48,2048]{1,0:T(8,128)(2,1)}, bf16[48,2048]{1,0:T(8,128)(2,1)S(1)}, u32[]{:S(2)}, u32[]{:S(2)}) %collective-permute-start.22) | collective-permute-done | bytes 196640 | tf_op jit(solution)/shard_map/ppermute | solution.py:29
  101.5 2.8 %combine_grads.1 = (bf16[64,2048]{1,0:T(8,128)(2,1)}, bf16[64,2048]{1,0:T(8,128)(2,1)}) custom-call(s32[1,8,24]{2,1,0:T(8,128)} %rows_ref.7, bf16[48,2048]{1,0:T(8,128)(2,1)} %get-tuple-element.45.refs_0_, bf16[48,2048]{1,0:T(8,128)(2,1)} %copy-done.16, bf16[48,2048]{1,0:T(8,128)(2,1)} %copy-done.12, bf16[48,2048]{1,0:T(8,128)(2,1)} %copy-done.17, ...), custom_call_target="tpu_custom_call" | custom-call | flops 100663296 | bytes 1572864 | tf_op jit(solution)/shard_map/combine_grads/pallas_call | solution.py:359
  109.4 2.8 %collective-permute-done.34.refs_1_ = bf16[192,1024]{1,0:T(8,128)(2,1)S(1)} collective-permute-done((bf16[192,1024]{1,0:T(8,128)(2,1)}, bf16[192,1024]{1,0:T(8,128)(2,1)S(1)}, u32[]{:S(2)}, u32[]{:S(2)}) %collective-permute-start.34) | collective-permute-done | bytes 393248 | tf_op jit(solution)/shard_map/ppermute | solution.py:29
  113.7 5.2 %collective-permute-done.33.refs_2_ = bf16[64,2048]{1,0:T(8,128)(2,1)S(1)} collective-permute-done((bf16[64,2048]{1,0:T(8,128)(2,1)}, bf16[64,2048]{1,0:T(8,128)(2,1)S(1)}, u32[]{:S(2)}, u32[]{:S(2)}) %collective-permute-start.33) | collective-permute-done | bytes 262176 | tf_op jit(solution)/shard_map/ppermute | solution.py:29
  119.4 39.1 %collective-permute-done.32.refs_1_ = bf16[64,2048]{1,0:T(8,128)(2,1)S(1)} collective-permute-done((bf16[64,2048]{1,0:T(8,128)(2,1)}, bf16[64,2048]{1,0:T(8,128)(2,1)S(1)}, u32[]{:S(2)}, u32[]{:S(2)}) %collective-permute-start.32) | collective-permute-done | bytes 262176 | tf_op jit(solution)/shard_map/ppermute | solution.py:29
  162.1 3.0 %combine_output.1 = bf16[128,2048]{1,0:T(8,128)(2,1)} custom-call(s32[1,8,24]{2,1,0:T(8,128)} %rows_ref.7, f32[1,8,24]{2,1,0:T(8,128)} %gates_ref.3, s32[1,8]{1,0:T(1,128)} %counts_ref.3, bf16[48,2048]{1,0:T(8,128)(2,1)} %get-tuple-element.41.refs_0_, bf16[48,2048]{1,0:T(8,128)(2,1)} %copy-done.9, bf16[48,2048]{1,0:T(8,128)(2,1)} %copy-done.6, ...), custom_call_target="tpu_custom_call" | custom-call | flops 201326592 | bytes 1572864 | tf_op jit(solution)/shard_map/combine_output/pallas_call | solution.py:332
  165.1 2.1 %finish.1 = bf16[128,2048]{1,0:T(8,128)(2,1)} custom-call(s32[1,4]{1,0:T(1,128)} %matching_ref.3, bf16[64,2048]{1,0:T(8,128)(2,1)} %get-tuple-element.49.low_ref, bf16[64,2048]{1,0:T(8,128)(2,1)} %copy-done.5, bf16[64,2048]{1,0:T(8,128)(2,1)} %copy-done.4, bf16[64,2048]{1,0:T(8,128)(2,1)} %copy-done), custom_call_target="tpu_custom_call" | custom-call | bytes 1310720 | tf_op jit(solution)/shard_map/finish/pallas_call | solution.py:379
  167.2 9.3 %collective-permute-done.35.refs_2_ = bf16[192,1024]{1,0:T(8,128)(2,1)S(1)} collective-permute-done((bf16[192,1024]{1,0:T(8,128)(2,1)}, bf16[192,1024]{1,0:T(8,128)(2,1)S(1)}, u32[]{:S(2)}, u32[]{:S(2)}) %collective-permute-start.35) | collective-permute-done | bytes 393248 | tf_op jit(solution)/shard_map/ppermute | solution.py:29
  178.2 6.1 %weight_grads.1 = (f32[1,512,768]{2,1,0:T(8,128)}, f32[1,512,768]{2,1,0:T(8,128)}, f32[1,768,512]{2,1,0:T(8,128)}) custom-call(bf16[192,1024]{1,0:T(8,128)(2,1)} %get-tuple-element.51.refs_0_, bf16[192,1024]{1,0:T(8,128)(2,1)} %copy-done.23, bf16[192,1024]{1,0:T(8,128)(2,1)} %copy-done.24, bf16[192,1024]{1,0:T(8,128)(2,1)} %copy-done.25, ...), custom_call_target="tpu_custom_call" | custom-call | flops 1811939328 | bytes 4718592 | tf_op jit(solution)/shard_map/weight_grads/pallas_call | solution.py:286
  (143 shorter events, 34.3 us)
Async XLA Ops:
  3.3 12.7 %collective-permute-start.13 = (bf16[48,2048]{1,0:T(8,128)(2,1)}, bf16[48,2048]{1,0:T(8,128)(2,1)S(1)}, u32[]{:S(2)}, u32[]{:S(2)}) collective-permute-start(bf16[48,2048]{1,0:T(8,128)(2,1)} %get-tuple-element.39), channel_id=1, source_target_pairs={{0,4},{1,5},{2,6},{3,7},{4,0},{5,1},{6,2},{7,3},{8,12},{9,13},{10,... | collective-permute-start | bytes 589832 | tf_op jit(solution)/shard_map/ppermute | solution.py:29
  8.8 11.8 %collective-permute-start.1 = (bf16[64,2048]{1,0:T(8,128)(2,1)}, bf16[64,2048]{1,0:T(8,128)(2,1)S(1)}, u32[]{:S(2)}, u32[]{:S(2)}) collective-permute-start(bf16[64,2048]{1,0:T(8,128)(2,1)} %get-tuple-element.32), channel_id=1, source_target_pairs={{0,16},{8,24},{16,0},{24,8},{1,17},{9,25},{17,1},{25,9},{2,18},{10... | collective-permute-start | bytes 786440 | tf_op jit(solution)/shard_map/ppermute | solution.py:29
  12.1 14.0 %collective-permute-start.15 = (bf16[48,2048]{1,0:T(8,128)(2,1)}, bf16[48,2048]{1,0:T(8,128)(2,1)S(1)}, u32[]{:S(2)}, u32[]{:S(2)}) collective-permute-start(bf16[48,2048]{1,0:T(8,128)(2,1)} %get-tuple-element.40), channel_id=1, source_target_pairs={{0,6},{1,7},{2,4},{3,5},{4,2},{5,3},{6,0},{7,1},{8,14},{9,15},{10,... | collective-permute-start | bytes 589832 | tf_op jit(solution)/shard_map/ppermute | solution.py:29
  26.2 14.4 %collective-permute-start.6 = (bf16[48,2048]{1,0:T(8,128)(2,1)}, bf16[48,2048]{1,0:T(8,128)(2,1)S(1)}, u32[]{:S(2)}, u32[]{:S(2)}) collective-permute-start(bf16[48,2048]{1,0:T(8,128)(2,1)} %get-tuple-element.35), channel_id=1, source_target_pairs={{0,4},{1,5},{2,6},{3,7},{4,0},{5,1},{6,2},{7,3},{8,12},{9,13},{10,... | collective-permute-start | bytes 589832 | tf_op jit(solution)/shard_map/ppermute | solution.py:29
  26.5 19.0 %collective-permute-start.8 = (bf16[48,2048]{1,0:T(8,128)(2,1)}, bf16[48,2048]{1,0:T(8,128)(2,1)S(1)}, u32[]{:S(2)}, u32[]{:S(2)}) collective-permute-start(bf16[48,2048]{1,0:T(8,128)(2,1)} %get-tuple-element.36), channel_id=1, source_target_pairs={{0,6},{1,7},{2,4},{3,5},{4,2},{5,3},{6,0},{7,1},{8,14},{9,15},{10,... | collective-permute-start | bytes 589832 | tf_op jit(solution)/shard_map/ppermute | solution.py:29
  28.1 17.4 %collective-permute-start.16 = (bf16[48,2048]{1,0:T(8,128)(2,1)S(1)}, bf16[48,2048]{1,0:T(8,128)(2,1)S(1)}, u32[]{:S(2)}, u32[]{:S(2)}) collective-permute-start(bf16[48,2048]{1,0:T(8,128)(2,1)S(1)} %collective-permute-done.15.refs_14_), channel_id=1, source_target_pairs={{0,1},{1,0},{2,3},{3,2},{4,5},{5,4},{6,7},{7,6},{8,9},{9,8},{10,11... | collective-permute-start | bytes 589832 | tf_op jit(solution)/shard_map/ppermute | solution.py:29
  28.1 17.4 %collective-permute-start.3 = (bf16[48,2048]{1,0:T(8,128)(2,1)}, bf16[48,2048]{1,0:T(8,128)(2,1)S(1)}, u32[]{:S(2)}, u32[]{:S(2)}) collective-permute-start(bf16[48,2048]{1,0:T(8,128)(2,1)} %get-tuple-element.33.refs_0_), channel_id=1, source_target_pairs={{0,1},{1,0},{2,3},{3,2},{4,5},{5,4},{6,7},{7,6},{8,9},{9,8},{10,11... | collective-permute-start | bytes 589832 | tf_op jit(solution)/shard_map/ppermute | solution.py:29
  33.8 11.7 %collective-permute-start.5 = (bf16[48,2048]{1,0:T(8,128)(2,1)S(1)}, bf16[48,2048]{1,0:T(8,128)(2,1)S(1)}, u32[]{:S(2)}, u32[]{:S(2)}) collective-permute-start(bf16[48,2048]{1,0:T(8,128)(2,1)S(1)} %collective-permute-done.4.refs_2_), channel_id=1, source_target_pairs={{0,1},{1,0},{2,3},{3,2},{4,5},{5,4},{6,7},{7,6},{8,9},{9,8},{10,11... | collective-permute-start | bytes 589832 | tf_op jit(solution)/shard_map/ppermute | solution.py:29
  61.0 12.1 %collective-permute-start.20 = (bf16[48,2048]{1,0:T(8,128)(2,1)}, bf16[48,2048]{1,0:T(8,128)(2,1)S(1)}, u32[]{:S(2)}, u32[]{:S(2)}) collective-permute-start(bf16[48,2048]{1,0:T(8,128)(2,1)} %get-tuple-element.43), channel_id=1, source_target_pairs={{0,4},{1,5},{2,6},{3,7},{4,0},{5,1},{6,2},{7,3},{8,12},{9,13},{10,... | collective-permute-start | bytes 589832 | tf_op jit(solution)/shard_map/ppermute | solution.py:29
  62.9 14.5 %collective-permute-start.25 = (bf16[48,2048]{1,0:T(8,128)(2,1)}, bf16[48,2048]{1,0:T(8,128)(2,1)S(1)}, u32[]{:S(2)}, u32[]{:S(2)}) collective-permute-start(bf16[48,2048]{1,0:T(8,128)(2,1)} %get-tuple-element.46), channel_id=1, source_target_pairs={{0,2},{1,3},{2,0},{3,1},{4,6},{5,7},{6,4},{7,5},{8,10},{9,11},{10,... | collective-permute-start | bytes 589832 | tf_op jit(solution)/shard_map/ppermute | solution.py:29
  63.1 26.6 %collective-permute-start.27 = (bf16[48,2048]{1,0:T(8,128)(2,1)}, bf16[48,2048]{1,0:T(8,128)(2,1)S(1)}, u32[]{:S(2)}, u32[]{:S(2)}) collective-permute-start(bf16[48,2048]{1,0:T(8,128)(2,1)} %get-tuple-element.47), channel_id=1, source_target_pairs={{0,4},{1,5},{2,6},{3,7},{4,0},{5,1},{6,2},{7,3},{8,12},{9,13},{10,... | collective-permute-start | bytes 589832 | tf_op jit(solution)/shard_map/ppermute | solution.py:29
  66.0 29.8 %collective-permute-start.29 = (bf16[48,2048]{1,0:T(8,128)(2,1)}, bf16[48,2048]{1,0:T(8,128)(2,1)S(1)}, u32[]{:S(2)}, u32[]{:S(2)}) collective-permute-start(bf16[48,2048]{1,0:T(8,128)(2,1)} %get-tuple-element.48), channel_id=1, source_target_pairs={{0,6},{1,7},{2,4},{3,5},{4,2},{5,3},{6,0},{7,1},{8,14},{9,15},{10,... | collective-permute-start | bytes 589832 | tf_op jit(solution)/shard_map/ppermute | solution.py:29
  69.5 29.4 %collective-permute-start.22 = (bf16[48,2048]{1,0:T(8,128)(2,1)}, bf16[48,2048]{1,0:T(8,128)(2,1)S(1)}, u32[]{:S(2)}, u32[]{:S(2)}) collective-permute-start(bf16[48,2048]{1,0:T(8,128)(2,1)} %get-tuple-element.44), channel_id=1, source_target_pairs={{0,6},{1,7},{2,4},{3,5},{4,2},{5,3},{6,0},{7,1},{8,14},{9,15},{10,... | collective-permute-start | bytes 589832 | tf_op jit(solution)/shard_map/ppermute | solution.py:29
  73.1 25.8 %collective-permute-start.24 = (bf16[48,2048]{1,0:T(8,128)(2,1)}, bf16[48,2048]{1,0:T(8,128)(2,1)S(1)}, u32[]{:S(2)}, u32[]{:S(2)}) collective-permute-start(bf16[48,2048]{1,0:T(8,128)(2,1)} %get-tuple-element.45.refs_0_), channel_id=1, source_target_pairs={{0,1},{1,0},{2,3},{3,2},{4,5},{5,4},{6,7},{7,6},{8,9},{9,8},{10,11... | collective-permute-start | bytes 589832 | tf_op jit(solution)/shard_map/ppermute | solution.py:29
  77.5 22.0 %collective-permute-start.26 = (bf16[48,2048]{1,0:T(8,128)(2,1)S(1)}, bf16[48,2048]{1,0:T(8,128)(2,1)S(1)}, u32[]{:S(2)}, u32[]{:S(2)}) collective-permute-start(bf16[48,2048]{1,0:T(8,128)(2,1)S(1)} %collective-permute-done.25.refs_2_), channel_id=1, source_target_pairs={{0,1},{1,0},{2,3},{3,2},{4,5},{5,4},{6,7},{7,6},{8,9},{9,8},{10,11... | collective-permute-start | bytes 589832 | tf_op jit(solution)/shard_map/ppermute | solution.py:29
  100.0 12.2 %collective-permute-start.34 = (bf16[192,1024]{1,0:T(8,128)(2,1)}, bf16[192,1024]{1,0:T(8,128)(2,1)S(1)}, u32[]{:S(2)}, u32[]{:S(2)}) collective-permute-start(bf16[192,1024]{1,0:T(8,128)(2,1)} %get-tuple-element.52), channel_id=1, source_target_pairs={{0,8},{8,0},{16,24},{24,16},{1,9},{9,1},{17,25},{25,17},{2,10},{10... | collective-permute-start | bytes 1179656 | tf_op jit(solution)/shard_map/ppermute | solution.py:29
  104.3 14.6 %collective-permute-start.33 = (bf16[64,2048]{1,0:T(8,128)(2,1)}, bf16[64,2048]{1,0:T(8,128)(2,1)S(1)}, u32[]{:S(2)}, u32[]{:S(2)}) collective-permute-start(bf16[64,2048]{1,0:T(8,128)(2,1)} %get-tuple-element.50), channel_id=1, source_target_pairs={{0,24},{8,16},{16,8},{24,0},{1,25},{9,17},{17,9},{25,1},{2,26},{10... | collective-permute-start | bytes 786440 | tf_op jit(solution)/shard_map/ppermute | solution.py:29
  105.9 70.6 %collective-permute-start.39 = (bf16[192,2304]{1,0:T(8,128)(2,1)}, bf16[192,2304]{1,0:T(8,128)(2,1)S(1)}, u32[]{:S(2)}, u32[]{:S(2)}) collective-permute-start(bf16[192,2304]{1,0:T(8,128)(2,1)} %get-tuple-element.55.refs_4_), channel_id=1, source_target_pairs={{0,24},{8,16},{16,8},{24,0},{1,25},{9,17},{17,9},{25,1},{2,26},{10... | collective-permute-start | bytes 2654216 | tf_op jit(solution)/shard_map/ppermute | solution.py:29
  107.3 69.2 %collective-permute-start.38 = (bf16[192,2304]{1,0:T(8,128)(2,1)}, bf16[192,2304]{1,0:T(8,128)(2,1)S(1)}, u32[]{:S(2)}, u32[]{:S(2)}) collective-permute-start(bf16[192,2304]{1,0:T(8,128)(2,1)} %get-tuple-element.55.refs_4_), channel_id=1, source_target_pairs={{0,16},{8,24},{16,0},{24,8},{1,17},{9,25},{17,1},{25,9},{2,18},{10... | collective-permute-start | bytes 2654216 | tf_op jit(solution)/shard_map/ppermute | solution.py:29
  108.0 68.6 %collective-permute-start.37 = (bf16[192,2304]{1,0:T(8,128)(2,1)}, bf16[192,2304]{1,0:T(8,128)(2,1)S(1)}, u32[]{:S(2)}, u32[]{:S(2)}) collective-permute-start(bf16[192,2304]{1,0:T(8,128)(2,1)} %get-tuple-element.55.refs_4_), channel_id=1, source_target_pairs={{0,8},{8,0},{16,24},{24,16},{1,9},{9,1},{17,25},{25,17},{2,10},{10... | collective-permute-start | bytes 2654216 | tf_op jit(solution)/shard_map/ppermute | solution.py:29
  112.2 46.3 %collective-permute-start.32 = (bf16[64,2048]{1,0:T(8,128)(2,1)}, bf16[64,2048]{1,0:T(8,128)(2,1)S(1)}, u32[]{:S(2)}, u32[]{:S(2)}) collective-permute-start(bf16[64,2048]{1,0:T(8,128)(2,1)} %get-tuple-element.50), channel_id=1, source_target_pairs={{0,16},{8,24},{16,0},{24,8},{1,17},{9,25},{17,1},{25,9},{2,18},{10... | collective-permute-start | bytes 786440 | tf_op jit(solution)/shard_map/ppermute | solution.py:29
  118.9 41.6 %collective-permute-start.31 = (bf16[64,2048]{1,0:T(8,128)(2,1)}, bf16[64,2048]{1,0:T(8,128)(2,1)S(1)}, u32[]{:S(2)}, u32[]{:S(2)}) collective-permute-start(bf16[64,2048]{1,0:T(8,128)(2,1)} %get-tuple-element.50), channel_id=1, source_target_pairs={{0,8},{8,0},{16,24},{24,16},{1,9},{9,1},{17,25},{25,17},{2,10},{10... | collective-permute-start | bytes 786440 | tf_op jit(solution)/shard_map/ppermute | solution.py:29
  158.5 18.0 %collective-permute-start.35 = (bf16[192,1024]{1,0:T(8,128)(2,1)}, bf16[192,1024]{1,0:T(8,128)(2,1)S(1)}, u32[]{:S(2)}, u32[]{:S(2)}) collective-permute-start(bf16[192,1024]{1,0:T(8,128)(2,1)} %get-tuple-element.53), channel_id=1, source_target_pairs={{0,16},{8,24},{16,0},{24,8},{1,17},{9,25},{17,1},{25,9},{2,18},{10... | collective-permute-start | bytes 1179656 | tf_op jit(solution)/shard_map/ppermute | solution.py:29
  160.5 16.0 %collective-permute-start.36 = (bf16[192,1024]{1,0:T(8,128)(2,1)}, bf16[192,1024]{1,0:T(8,128)(2,1)S(1)}, u32[]{:S(2)}, u32[]{:S(2)}) collective-permute-start(bf16[192,1024]{1,0:T(8,128)(2,1)} %get-tuple-element.54), channel_id=1, source_target_pairs={{0,24},{8,16},{16,8},{24,0},{1,25},{9,17},{17,9},{25,1},{2,26},{10... | collective-permute-start | bytes 1179656 | tf_op jit(solution)/shard_map/ppermute | solution.py:29
  (56 other events, 949.7 us)

commit v2 on v0

v2 whole, which is shorter than its diff:
```python
import functools

import jax
import jax.numpy as jnp
from jax import lax
from jax.experimental import pallas as pl
from jax.experimental.pallas import tpu as pltpu
from jax.sharding import PartitionSpec as P

F32 = jnp.float32
BF16 = jnp.bfloat16
VMEM = pltpu.VMEM
WHOLE = pl.BlockSpec(memory_space=pltpu.VMEM)
TILE = 256
MIB = 1024 * 1024


def params(mib):
    return pltpu.CompilerParams(vmem_limit_bytes=mib * MIB)


def in_hbm(*arrays):
    return [pltpu.with_memory_space_constraint(a, pltpu.HBM) for a in arrays]


def cost(flops, bytes_accessed):
    return pl.CostEstimate(flops=int(flops), bytes_accessed=int(bytes_accessed), transcendentals=0)


def xor_permute(array, axis, key):
    size = lax.axis_size(axis)
    return lax.ppermute(array, axis, [(i, i ^ key) for i in range(size)])


def column_of(row, length):
    diagonal = lax.broadcasted_iota(jnp.int32, (length, length), 0) == lax.broadcasted_iota(
        jnp.int32, (length, length), 1
    )
    spread = jnp.where(diagonal, jnp.broadcast_to(row.astype(F32), (length, length)), 0.0)
    return jnp.sum(spread, axis=1, keepdims=True)


def table_columns(table, order):
    return jnp.concatenate([column_of(row, row.shape[1]) for row in (table(e) for e in order)], axis=0)


def keep_valid(values, lengths, first_slot, slot_len):
    rows = lax.broadcasted_iota(jnp.int32, values.shape, 0)
    limit = jnp.zeros(values.shape, jnp.int32)
    for slot in range(values.shape[0] // slot_len):
        used = lengths[:, first_slot + slot : first_slot + slot + 1]
        limit = jnp.where(rows // slot_len == slot, slot * slot_len + used, limit)
    return jnp.where(rows < limit, values.astype(F32), 0.0).astype(values.dtype)


def prepare_kernel(sizes, *refs):
    window, capacity, tok_dev, slot_len = sizes
    sources, outs, held, sems = refs[:7], refs[7:14], refs[14:21], refs[21]
    copies = [
        pltpu.make_async_copy(source, place, sems.at[i])
        for i, (source, place) in enumerate(zip(sources, held))
    ]
    for copy in copies:
        copy.start()
    for copy in copies:
        copy.wait()
    rows_ref, gates_ref, counts_ref, lengths_ref, matching_ref, tok_ref, cot_ref = held
    moved_ref, low_ref, weighted_ref, hit_ref, high_ref, fine_ref, key_ref = outs
    me = lax.axis_index("expert")
    half = tok_dev // 2
    lengths = lengths_ref[...]
    moved_ref[...] = keep_valid(tok_ref[half:, :], lengths, half // slot_len, slot_len)
    low_ref[...] = keep_valid(tok_ref[:half, :], lengths, 0, slot_len)
    key_ref[...] = jnp.broadcast_to(matching_ref[:, :1], key_ref.shape)
    lanes = lax.broadcasted_iota(jnp.int32, (window * capacity, tok_dev), 1)
    row_of = lambda e: rows_ref[0, pl.ds(e, 1), :]
    hit_ref[...] = (
        lanes == table_columns(row_of, [me ^ d for d in range(window)]).astype(jnp.int32)
    ).astype(BF16)

    def gate_of(e):
        slot = lax.broadcasted_iota(jnp.int32, (1, capacity), 1)
        counted = slot < counts_ref[:, e : e + 1]
        return jnp.where(counted, gates_ref[0, e : e + 1, :], 0.0)

    gate = table_columns(gate_of, range(window))
    hit = lanes == table_columns(row_of, range(window)).astype(jnp.int32)
    table = jnp.where(hit, jnp.broadcast_to(gate, hit.shape), 0.0)
    high = table.astype(BF16)
    high_ref[...] = high
    fine_ref[...] = (table - high.astype(F32)).astype(BF16)
    picked = jnp.dot(hit.astype(BF16), cot_ref[...], preferred_element_type=F32)
    weighted = gate * picked
    for e in range(window):
        weighted_ref[e] = weighted[e * capacity : (e + 1) * capacity].astype(BF16)


def prepare(slot_rows, slot_gates, slot_counts, seq_lengths, matching, tokens, cotangent):
    tok_dev, width = tokens.shape
    window, capacity = slot_rows.shape[1:]
    half = tok_dev // 2
    slot_len = tok_dev // seq_lengths.shape[1]
    sources = (slot_rows, slot_gates, slot_counts, seq_lengths, matching, tokens, cotangent)
    table = jax.ShapeDtypeStruct((window * capacity, tok_dev), BF16)
    return pl.pallas_call(
        functools.partial(prepare_kernel, (window, capacity, tok_dev, slot_len)),
        out_shape=[
            jax.ShapeDtypeStruct((half, width), BF16),
            jax.ShapeDtypeStruct((half, width), BF16),
            jax.ShapeDtypeStruct((window, capacity, width), BF16),
            table,
            table,
            table,
            jax.ShapeDtypeStruct((8, 128), jnp.int32),
        ],
        in_specs=[pl.BlockSpec(memory_space=pltpu.HBM)] * len(sources),
        out_specs=[WHOLE] * 7,
        scratch_shapes=[VMEM(a.shape, a.dtype) for a in sources]
        + [pltpu.SemaphoreType.DMA((len(sources),))],
        compiler_params=params(16),
        cost_estimate=cost(2 * window * capacity * tok_dev * width, 5 * tok_dev * width),
        name="prepare",
    )(*in_hbm(*sources))


def chosen(key_ref, refs):
    key = key_ref[:1, :1]
    value = refs[0][...].astype(F32)
    for i in range(1, len(refs)):
        value = jnp.where(key == i + 1, refs[i][...].astype(F32), value)
    return value.astype(BF16)


def pick_kernel(pair, key_ref, hit_ref, low_ref, *refs):
    count = hit_ref.shape[0] // pair
    shuffled = jnp.concatenate([low_ref[...], chosen(key_ref, refs[:-count])], axis=0)
    picked = jnp.dot(hit_ref[...], shuffled, preferred_element_type=F32).astype(BF16)
    for z, out in enumerate(refs[-count:]):
        out[...] = picked[z * pair : (z + 1) * pair]


def pick(key, hit, low, arrived, capacity):
    pair, width = 2 * capacity, low.shape[1]
    slots, tok_dev = hit.shape
    return pl.pallas_call(
        functools.partial(pick_kernel, pair),
        out_shape=[jax.ShapeDtypeStruct((pair, width), BF16)] * (slots // pair),
        in_specs=[WHOLE] * (3 + len(arrived)),
        out_specs=[WHOLE] * (slots // pair),
        compiler_params=params(12),
        cost_estimate=cost(2 * slots * tok_dev * width, 5 * tok_dev * width),
        name="pick",
    )(key, hit, low, *arrived)


def joined(direct, crossed, capacity):
    rows = lax.broadcasted_iota(jnp.int32, direct.shape, 0)
    return jnp.where(rows < capacity, direct[...].astype(F32), crossed[...].astype(F32)).astype(BF16)


def gather_kernel(weighted_ref, rows_ref, shares_ref):
    me = lax.axis_index("expert")
    window, capacity, _ = weighted_ref.shape
    pair = 2 * capacity
    for z in range(window // 2):
        both = [weighted_ref[me ^ (2 * z + core)].astype(F32) for core in range(2)]
        rows_ref[z * pair : (z + 1) * pair, :] = jnp.concatenate(both, axis=0).astype(BF16)
    share = shares_ref.shape[2]
    for g in range(shares_ref.shape[0]):
        shares_ref[g] = rows_ref[:, g * share : (g + 1) * share]


def gather_rows(weighted):
    window, capacity, width = weighted.shape
    rows = window * capacity
    replicas = lax.axis_size("dp")
    return pl.pallas_call(
        gather_kernel,
        out_shape=[
            jax.ShapeDtypeStruct((rows, width), BF16),
            jax.ShapeDtypeStruct((replicas, rows, width // replicas), BF16),
        ],
        in_specs=[WHOLE],
        out_specs=[WHOLE] * 2,
        compiler_params=params(12),
        cost_estimate=cost(0, 8 * rows * width),
        name="gather_rows",
    )(weighted)


def expert_kernel(sizes, *refs):
    count, capacity, tile, replicas = sizes
    x_refs, w_ref, weights = refs[: 2 * count], refs[2 * count], refs[2 * count + 1 : 2 * count + 4]
    tok_refs = refs[2 * count + 4 : 3 * count + 4]
    out_ref, sent_refs = refs[3 * count + 4], refs[3 * count + 5 : 3 * count + 5 + replicas]
    (x_all, hid_all, gg_all, gu_all, gate_ref, up_ref, down_ref, sems) = refs[
        3 * count + 5 + replicas :
    ]
    tiles = hid_all.shape[1] // tile
    copies = []
    for f in range(tiles):
        span = pl.ds(f * tile, tile)
        pieces = [
            (weights[0].at[0, :, span], gate_ref.at[0, :, span]),
            (weights[1].at[0, :, span], up_ref.at[0, :, span]),
            (weights[2].at[0, span, :], down_ref.at[0, span, :]),
        ]
        copies.append(
            [pltpu.make_async_copy(a, b, sems.at[f, i]) for i, (a, b) in enumerate(pieces)]
        )
    for group in copies:
        for copy in group:
            copy.start()
    me = lax.axis_index("expert")
    replica = lax.axis_index("dp")
    pair = 2 * capacity
    width = x_all.shape[1]
    share = width // replicas
    turned = (((1,), (1,)), ((), ()))
    for z in range(count):
        x_all[z * pair : (z + 1) * pair, :] = joined(x_refs[2 * z], x_refs[2 * z + 1], capacity)
    for j, sent in enumerate(sent_refs):
        columns = pl.ds(pl.multiple_of((replica ^ j) * share, share), share)
        sent[:, sent.shape[1] - share :] = x_all[:, columns]
    for f in range(tiles):
        span = slice(f * tile, (f + 1) * tile)
        for copy in copies[f]:
            copy.wait()
        pre_gate = jnp.dot(x_all[...], gate_ref[0, :, span], preferred_element_type=F32)
        pre_up = jnp.dot(x_all[...], up_ref[0, :, span], preferred_element_type=F32)
        grad_hidden = lax.dot_general(
            w_ref[...], down_ref[0, span, :], turned, preferred_element_type=F32
        )
        sig = jax.nn.sigmoid(pre_gate)
        silu = pre_gate * sig
        hid_all[:, span] = (silu * pre_up).astype(BF16)
        gg_all[:, span] = (
            grad_hidden * pre_up * sig * (1.0 + pre_gate * (1.0 - sig))
        ).astype(BF16)
        gu_all[:, span] = (grad_hidden * silu).astype(BF16)
        for sent in sent_refs:
            if sent.shape[1] > share:
                for k, source in enumerate((hid_all, gg_all, gu_all)):
                    sent[:, (3 * f + k) * tile : (3 * f + k + 1) * tile] = source[:, span]
    wide = 2 * tile
    for n in range(width // wide):
        span = slice(n * wide, (n + 1) * wide)
        tok = lax.dot_general(
            gg_all[...], gate_ref[0, span, :], turned, preferred_element_type=F32
        ) + lax.dot_general(gu_all[...], up_ref[0, span, :], turned, preferred_element_type=F32)
        tok = tok.astype(BF16)
        out = jnp.dot(hid_all[...], down_ref[0, :, span], preferred_element_type=F32)
        for z in range(count):
            tok_refs[z][:, span] = tok[z * pair : (z + 1) * pair]
        for d in range(2 * count):
            out_ref[me ^ d, :, span] = out[d * capacity : (d + 1) * capacity].astype(BF16)


def expert(x_pairs, w_rows, w_gate, w_up, w_down, capacity):
    count = len(x_pairs)
    flat = [a for p in x_pairs for a in p]
    pair, width = flat[0].shape
    hidden_units = w_gate.shape[2]
    rows = count * pair
    replicas = lax.axis_size("dp")
    share = width // replicas
    block = jax.ShapeDtypeStruct((pair, width), BF16)
    sent = [jax.ShapeDtypeStruct((rows, 3 * hidden_units + share), BF16)] * replicas
    if replicas == 4:
        sent[3] = jax.ShapeDtypeStruct((rows, share), BF16)
    results = pl.pallas_call(
        functools.partial(expert_kernel, (count, capacity, TILE, replicas)),
        out_shape=[block] * count
        + [jax.ShapeDtypeStruct((2 * count, capacity, width), BF16)]
        + sent,
        in_specs=[WHOLE] * (2 * count + 1) + [pl.BlockSpec(memory_space=pltpu.HBM)] * 3,
        out_specs=[WHOLE] * (count + 1 + replicas),
        scratch_shapes=[VMEM((rows, width), BF16)]
        + [VMEM((rows, hidden_units), BF16)] * 3
        + [VMEM(a.shape, BF16) for a in (w_gate, w_up, w_down)]
        + [pltpu.SemaphoreType.DMA((hidden_units // TILE, 3))],
        compiler_params=params(32 if replicas <= 4 else 56),
        cost_estimate=cost(
            12 * rows * width * hidden_units, 6 * width * hidden_units + 10 * rows * width
        ),
        name="expert",
    )(*flat, w_rows, *in_hbm(w_gate, w_up, w_down))
    return results[:count], results[count], results[count + 1 :]


def weight_kernel(sizes, w_ref, *refs):
    share, tile, parts = sizes
    sources, outs = refs[:-7], refs[-7:-4]
    held, sems = refs[-4:-1], refs[-1]
    me = lax.axis_index("dp")
    acts_width = sources[0].shape[1] - share
    across = (((0,), (0,)), ((), ()))
    x = jnp.concatenate([r[:, r.shape[1] - share :] for r in sources[:parts]], axis=0)
    w = jnp.concatenate([w_ref[me ^ j] for j in range(parts)], axis=0)
    acts = [r for r in sources if r.shape[1] > share]
    copies = []
    for f in range(acts_width // (3 * tile)):
        hidden, grad_gate, grad_up = [
            jnp.concatenate(
                [a[:, (3 * f + k) * tile : (3 * f + k + 1) * tile] for a in acts], axis=0
            )
            for k in range(3)
        ]
        span = pl.ds(f * tile, tile)
        gate_held, up_held, down_held = [h.at[f] for h in held]
        gate_held[...] = lax.dot_general(x, grad_gate, across, preferred_element_type=F32)
        up_held[...] = lax.dot_general(x, grad_up, across, preferred_element_type=F32)
        down_held[...] = lax.dot_general(hidden, w, across, preferred_element_type=F32)
        pieces = [
            (gate_held, outs[0].at[0, :, span]),
            (up_held, outs[1].at[0, :, span]),
            (down_held, outs[2].at[0, span, :]),
        ]
        for i, (a, b) in enumerate(pieces):
            copy = pltpu.make_async_copy(a, b, sems.at[f, i])
            copy.start()
            copies.append(copy)
    for copy in copies:
        copy.wait()


def weight_grads(w_shares, received):
    parts, rows, share = w_shares.shape
    hidden_units = (received[0].shape[1] - share) // 3
    tile = TILE
    tiles = hidden_units // tile
    return pl.pallas_call(
        functools.partial(weight_kernel, (share, tile, parts)),
        out_shape=[
            jax.ShapeDtypeStruct((1, share, hidden_units), F32),
            jax.ShapeDtypeStruct((1, share, hidden_units), F32),
            jax.ShapeDtypeStruct((1, hidden_units, share), F32),
        ],
        in_specs=[WHOLE] * (1 + len(received)),
        out_specs=[pl.BlockSpec(memory_space=pltpu.HBM)] * 3,
        scratch_shapes=[
            VMEM((tiles, share, tile), F32),
            VMEM((tiles, share, tile), F32),
            VMEM((tiles, tile, share), F32),
            pltpu.SemaphoreType.DMA((tiles, 3)),
        ],
        compiler_params=params(24 if parts <= 4 else 56),
        cost_estimate=cost(6 * parts * rows * share * hidden_units, 12 * share * hidden_units),
        name="weight_grads",
    )(w_shares, *received)


def output_kernel(high_ref, fine_ref, back_ref, out_ref):
    window, capacity, width = back_ref.shape
    rows = jnp.concatenate([back_ref[e].astype(F32) for e in range(window)], axis=0).astype(BF16)
    across = (((0,), (0,)), ((), ()))
    total = lax.dot_general(high_ref[...], rows, across, preferred_element_type=F32)
    total += lax.dot_general(fine_ref[...], rows, across, preferred_element_type=F32)
    out_ref[...] = total.astype(BF16)


def combine_output(high, fine, back):
    slots, tok_dev = high.shape
    width = back.shape[2]
    return pl.pallas_call(
        output_kernel,
        out_shape=jax.ShapeDtypeStruct((tok_dev, width), BF16),
        in_specs=[WHOLE] * 3,
        out_specs=WHOLE,
        compiler_params=params(12),
        cost_estimate=cost(4 * slots * tok_dev * width, 6 * tok_dev * width),
        name="combine_output",
    )(high, fine, back)


def grads_kernel(capacity, hit_ref, *refs):
    pairs, (low_ref, high_ref) = refs[:-2], refs[-2:]
    rows = jnp.concatenate(
        [joined(pairs[i], pairs[i + 1], capacity) for i in range(0, len(pairs), 2)], axis=0
    )
    across = (((0,), (0,)), ((), ()))
    total = lax.dot_general(hit_ref[...], rows, across, preferred_element_type=F32).astype(BF16)
    half = low_ref.shape[0]
    low_ref[...] = total[:half]
    high_ref[...] = total[half:]


def combine_grads(hit, pairs, capacity):
    slots, tok_dev = hit.shape
    flat = [a for p in pairs for a in p]
    width = flat[0].shape[1]
    half = jax.ShapeDtypeStruct((tok_dev // 2, width), BF16)
    return pl.pallas_call(
        functools.partial(grads_kernel, capacity),
        out_shape=[half, half],
        in_specs=[WHOLE] * (1 + len(flat)),
        out_specs=[WHOLE, WHOLE],
        compiler_params=params(12),
        cost_estimate=cost(2 * slots * tok_dev * width, 6 * tok_dev * width),
        name="combine_grads",
    )(hit, *flat)


def finish_kernel(key_ref, low_ref, *refs):
    out_ref = refs[-1]
    half = low_ref.shape[0]
    out_ref[:half] = low_ref[...]
    out_ref[half:] = chosen(key_ref, refs[:-1])


def finish(key, low, arrived):
    half, width = low.shape
    return pl.pallas_call(
        finish_kernel,
        out_shape=jax.ShapeDtypeStruct((2 * half, width), BF16),
        in_specs=[WHOLE] * (2 + len(arrived)),
        out_specs=WHOLE,
        compiler_params=params(12),
        cost_estimate=cost(0, 10 * half * width),
        name="finish",
    )(key, low, *arrived)


def exchange(blocks):
    direct = {0: blocks[0]}
    for z in range(len(blocks) - 1, 0, -1):
        direct[z] = xor_permute(blocks[z], "expert", 2 * z)
    return [(direct[z], xor_permute(direct[z], "expert", 1)) for z in range(len(blocks))]


def spread(array):
    return [array] + [xor_permute(array, "dp", j) for j in range(1, lax.axis_size("dp"))]


def spread_acts(sent):
    if lax.axis_size("dp") != 4:
        return [sent[0]] + [xor_permute(sent[j], "dp", j) for j in range(1, len(sent))]
    half = sent[0].shape[0] // 2
    acts = sent[0].shape[1] - sent[3].shape[1]
    near = xor_permute(sent[1], "dp", 1)
    side = xor_permute(sent[2], "dp", 2)
    far = xor_permute(sent[3], "dp", 3)
    halves = [
        xor_permute(side[:half, :acts], "dp", 1),
        xor_permute(near[half:, :acts], "dp", 2),
    ]
    return [sent[0], near, side, far, *halves]


def after(value, *others):
    return lax.optimization_barrier((value, *others))[0]


def all_to_all(array, axis):
    return lax.all_to_all(array, axis, split_axis=0, concat_axis=0, tiled=True)


def per_device(
    tokens,
    cotangent,
    w_gate,
    w_up,
    w_down,
    slot_rows,
    slot_counts,
    slot_gates,
    seq_lengths,
    matching,
):
    capacity = slot_rows.shape[2]
    moved, low, weighted, hit, high, fine, key = prepare(
        slot_rows, slot_gates, slot_counts, seq_lengths, matching, tokens, cotangent
    )
    weighted = all_to_all(weighted, "expert")
    w_rows, w_shares = gather_rows(weighted)
    picked = pick(key, hit, low, spread(moved)[1:], capacity)
    picked = [after(p, w_rows) for p in picked]
    x_pairs = exchange(picked)
    w_shares = all_to_all(w_shares, "dp")
    w_rows = after(w_rows, w_shares)
    token_rows, expert_out, sent = expert(x_pairs, w_rows, w_gate, w_up, w_down, capacity)
    tok_pairs = exchange(token_rows)
    received = spread_acts(sent)
    back = all_to_all(after(expert_out, *[p[0] for p in tok_pairs]), "expert")
    low_grads, high_grads = combine_grads(hit, tok_pairs, capacity)
    grad_tokens = finish(key, low_grads, spread(high_grads)[1:])
    grads = weight_grads(w_shares, received)
    output = combine_output(high, fine, back)
    return (output, grad_tokens, *grads)


def solution(mesh):
    return jax.shard_map(
        per_device,
        mesh=mesh,
        in_specs=(
            P(("dp", "expert"), None),
            P(("dp", "expert"), None),
            P("expert", None, None),
            P("expert", None, None),
            P("expert", None, None),
            P(("dp", "expert"), None, None),
            P(("dp", "expert"), None),
            P(("dp", "expert"), None, None),
            P(("dp", "expert"), None),
            P("expert", None),
        ),
        out_specs=(
            P(("dp", "expert"), None),
            P(("dp", "expert"), None),
            P("expert", "dp", None),
            P("expert", "dp", None),
            P("expert", None, "dp"),
        ),
        check_vma=False,
    )
```

time: 308 us -> 136 us (0.44)
  waiting for transfers between devices: 197 us -> 68.6 us
  matrix products: 31.9 us -> 0 us
  Pallas kernels: 0 us -> 21 us
  starting transfers between devices: 17.9 us -> 37.6 us
  other arithmetic: 17.6 us -> 0 us
  between operations: 15.2 us -> 0.76 us
  local copies, waits for them, and re-layouts: 18.6 us -> 7.16 us
  blocking collectives: 8.9 us -> 0 us
    reduce_scatter x3 -> x0, waiting for transfers between devices: 113 us -> none  [the longest x1 44.4 us: per_device(): lax.psum_scatter(part_up.astype(jnp.bfloat16), 'dp', scatter_dimension=1,...]
    ppermute x0 -> x25, waiting for transfers between devices: none -> 51.1 us  [xor_permute(): return lax.ppermute(array, axis, [(i, i ^ key) for i in range(size)])]
    all_to_all x4 -> x3, waiting for transfers between devices: 56.6 us -> 17.5 us  [all_to_all(): return lax.all_to_all(array, axis, split_axis=0, concat_axis=0, tiled=True)]
    dot_general x11 -> x0, matrix products: 31.9 us -> none  [the longest x1 3.96 us: per_device(): jnp.einsum('sejd,sejf->edf', sent_rows, grad_gate, preferred_element_type...]
    all_gather x2 -> x0, waiting for transfers between devices: 27.3 us -> none  [the longest x1 27.3 us: forward_pairs(): lax.all_gather(moved_rows[None], 'dp', axis=0, tiled=True)]
    ppermute x0 -> x25, starting transfers between devices: none -> 22.9 us  [xor_permute(): return lax.ppermute(array, axis, [(i, i ^ key) for i in range(size)])]
    pallas_call x0 -> x8, Pallas kernels: none -> 21 us  [the longest x1 9.1 us: expert(): pl.pallas_call(functools.partial(expert_kernel, (count, capacity, TILE, r...]
    gather x5 -> x0, local copies, waits for them, and re-layouts: 10.1 us -> none  [the longest x1 3.92 us: per_device(): cotangent[slot_index].astype(jnp.float32)]
  transfers between devices with their start and end apart: 9 -> 28, of which waited for: 8 -> 12; matrix products, arithmetic and copies ran while one was open for 16% -> 2% of each run, Pallas kernels for 0% -> 6%
where the time goes in v2:
time: 136 us; the launch traced here: 135 us
  waiting for transfers between devices  68.6 us (50%)
  starting transfers between devices  37.6 us (28%)
  Pallas kernels  21 us (15%)
  local copies, waits for them, and re-layouts  7.16 us (5%)
    ppermute x25, waiting for transfers between devices, xor_permute(): return lax.ppermute(array, axis, [(i, i ^ key) for i in range(size)])  51.1 us
    ppermute x25, starting transfers between devices, xor_permute(): return lax.ppermute(array, axis, [(i, i ^ key) for i in range(size)])  22.9 us
    all_to_all x3, waiting for transfers between devices, all_to_all(): return lax.all_to_all(array, axis, split_axis=0, concat_axis=0, tiled=True)  17.5 us
    all_to_all x3, starting transfers between devices, all_to_all(): return lax.all_to_all(array, axis, split_axis=0, concat_axis=0, tiled=True)  14.7 us
    pallas_call x1, Pallas kernels, expert(): pl.pallas_call(functools.partial(expert_kernel, (count, capacity, TILE, r...  9.1 us
    unnamed x16, local copies, waits for them, and re-layouts  5.07 us
    pallas_call x1, Pallas kernels, weight_grads(): pl.pallas_call(functools.partial(weight_kernel, (share, tile, parts)), ou...  4.75 us
    pallas_call x1, Pallas kernels, prepare(): pl.pallas_call(functools.partial(prepare_kernel, (window, capacity, tok_d...  3.14 us
  transfers between devices with their start and end apart: 28, of which 12 were waited for; matrix products, arithmetic and copies ran while one was open for 2% of the time, Pallas kernels for 6%

profile of v2, /device:TPU:0, one launch (start us, length us, event | category | flops | bytes accessed | tf_op | source)
XLA Modules:
  0.0 135.0 jit_solution(15624053383856456129)
XLA Ops:
  0.6 3.1 %prepare.1 = (bf16[64,2048]{1,0:T(8,128)(2,1)S(1)}, bf16[64,2048]{1,0:T(8,128)(2,1)S(1)}, bf16[8,24,2048]{2,1,0:T(8,128)(2,1)}, bf16[192,128]{1,0:T(8,128)(2,1)S...) custom-call(s32[1,8,24]{2,1,0:T(8,128)} %refs_0_.1, f32[1,8,24]{2,1,0:T(8,128)} %refs_1_.1, ...), custom_call_target="tpu_custom_call" | custom-call | flops 100663296 | bytes 1310720 | tf_op jit(solution)/shard_map/prepare/pallas_call | solution.py:105
  3.8 6.3 %all-to-all-start = ((bf16[8,24,2048]{2,1,0:T(8,128)(2,1)}), bf16[8,24,2048]{2,1,0:T(8,128)(2,1)S(1)}, u32[]{:S(2)}, u32[]{:S(2)}) async-start(bf16[8,24,2048]{2,1,0:T(8,128)(2,1)} %get-tuple-element.45), calls=%async_computation | async-start | bytes 1572864 | tf_op jit(solution)/shard_map/all_to_all | solution.py:455
  10.1 2.4 %collective-permute-start.2 = (bf16[64,2048]{1,0:T(8,128)(2,1)S(1)}, bf16[64,2048]{1,0:T(8,128)(2,1)S(1)}, u32[]{:S(2)}, u32[]{:S(2)}) collective-permute-start(bf16[64,2048]{1,0:T(8,128)(2,1)S(1)} %get-tuple-element.43), channel_id=1, source_target_pairs={{0,24},{8,16},{16,8},{24,0},{1,25},{9,17},{17,9},{25,1},{2,26},{10... | collective-permute-start | bytes 786440 | tf_op jit(solution)/shard_map/ppermute | solution.py:32
  13.6 17.5 %all-to-all-done.weighted_ref = bf16[8,24,2048]{2,1,0:T(8,128)(2,1)S(1)} async-done(((bf16[8,24,2048]{2,1,0:T(8,128)(2,1)}), bf16[8,24,2048]{2,1,0:T(8,128)(2,1)S(1)}, u32[]{:S(2)}, u32[]{:S(2)}) %all-to-all-start) | async-done | bytes 786464 | tf_op jit(solution)/shard_map/all_to_all | solution.py:455
  33.0 3.8 %all-to-all-start.1 = ((bf16[4,192,512]{2,1,0:T(8,128)(2,1)}), bf16[4,192,512]{2,1,0:T(8,128)(2,1)S(1)}, u32[]{:S(2)}, u32[]{:S(2)}) async-start(bf16[4,192,512]{2,1,0:T(8,128)(2,1)} %get-tuple-element.54), calls=%async_computation.1 | async-start | bytes 1572864 | tf_op jit(solution)/shard_map/all_to_all | solution.py:455
  37.3 1.8 %collective-permute-start.6 = (bf16[48,2048]{1,0:T(8,128)(2,1)S(1)}, bf16[48,2048]{1,0:T(8,128)(2,1)S(1)}, u32[]{:S(2)}, u32[]{:S(2)}) collective-permute-start(bf16[48,2048]{1,0:T(8,128)(2,1)S(1)} %get-tuple-element.51), channel_id=1, source_target_pairs={{0,4},{1,5},{2,6},{3,7},{4,0},{5,1},{6,2},{7,3},{8,12},{9,13},{10,... | collective-permute-start | bytes 589832 | tf_op jit(solution)/shard_map/ppermute | solution.py:32
  39.1 2.6 %collective-permute-start.8 = (bf16[48,2048]{1,0:T(8,128)(2,1)S(1)}, bf16[48,2048]{1,0:T(8,128)(2,1)S(1)}, u32[]{:S(2)}, u32[]{:S(2)}) collective-permute-start(bf16[48,2048]{1,0:T(8,128)(2,1)S(1)} %get-tuple-element.53), channel_id=1, source_target_pairs={{0,6},{1,7},{2,4},{3,5},{4,2},{5,3},{6,0},{7,1},{8,14},{9,15},{10,... | collective-permute-start | bytes 589832 | tf_op jit(solution)/shard_map/ppermute | solution.py:32
  41.7 4.8 %collective-permute-done.4.refs_2_ = bf16[48,2048]{1,0:T(8,128)(2,1)S(1)} collective-permute-done((bf16[48,2048]{1,0:T(8,128)(2,1)S(1)}, bf16[48,2048]{1,0:T(8,128)(2,1)S(1)}, u32[]{:S(2)}, u32[]{:S(2)}) %collective-permute-start.4) | collective-permute-done | bytes 196640 | tf_op jit(solution)/shard_map/ppermute | solution.py:32
  46.5 8.0 %collective-permute-done.6.refs_4_ = bf16[48,2048]{1,0:T(8,128)(2,1)S(1)} collective-permute-done((bf16[48,2048]{1,0:T(8,128)(2,1)S(1)}, bf16[48,2048]{1,0:T(8,128)(2,1)S(1)}, u32[]{:S(2)}, u32[]{:S(2)}) %collective-permute-start.6) | collective-permute-done | bytes 196640 | tf_op jit(solution)/shard_map/ppermute | solution.py:32
  59.2 9.1 %expert.1 = (bf16[48,2048]{1,0:T(8,128)(2,1)S(1)}, bf16[48,2048]{1,0:T(8,128)(2,1)S(1)}, bf16[48,2048]{1,0:T(8,128)(2,1)S(1)}, bf16[48,2048]{1,0:T(8,128)(2,1)S(...) custom-call(bf16[48,2048]{1,0:T(8,128)(2,1)S(1)} %get-tuple-element., ...), custom_call_target="tpu_custom_call" | custom-call | flops 3623878656 | bytes 13369344 | tf_op jit(solution)/shard_map/expert/pallas_call | solution.py:271
  69.3 2.0 %collective-permute-start.20 = (bf16[192,2816]{1,0:T(8,128)(2,1)}, bf16[192,2816]{1,0:T(8,128)(2,1)}, u32[]{:S(2)}, u32[]{:S(2)}) collective-permute-start(bf16[192,2816]{1,0:T(8,128)(2,1)} %get-tuple-element.65), channel_id=1, source_target_pairs={{0,8},{8,0},{16,24},{24,16},{1,9},{9,1},{17,25},{25,17},{2,10},{10... | collective-permute-start | bytes 3244040 | tf_op jit(solution)/shard_map/ppermute | solution.py:32
  71.3 1.5 %collective-permute-start.21 = (bf16[192,2816]{1,0:T(8,128)(2,1)}, bf16[192,2816]{1,0:T(8,128)(2,1)}, u32[]{:S(2)}, u32[]{:S(2)}) collective-permute-start(bf16[192,2816]{1,0:T(8,128)(2,1)} %get-tuple-element.66), channel_id=1, source_target_pairs={{0,16},{8,24},{16,0},{24,8},{1,17},{9,25},{17,1},{25,9},{2,18},{10... | collective-permute-start | bytes 3244040 | tf_op jit(solution)/shard_map/ppermute | solution.py:32
  72.8 2.2 %collective-permute-start.10 = (bf16[48,2048]{1,0:T(8,128)(2,1)S(1)}, bf16[48,2048]{1,0:T(8,128)(2,1)S(1)}, u32[]{:S(2)}, u32[]{:S(2)}) collective-permute-start(bf16[48,2048]{1,0:T(8,128)(2,1)S(1)} %get-tuple-element.58), channel_id=1, source_target_pairs={{0,2},{1,3},{2,0},{3,1},{4,6},{5,7},{6,4},{7,5},{8,10},{9,11},{10,... | collective-permute-start | bytes 589832 | tf_op jit(solution)/shard_map/ppermute | solution.py:32
  75.2 2.2 %collective-permute-start.12 = (bf16[48,2048]{1,0:T(8,128)(2,1)S(1)}, bf16[48,2048]{1,0:T(8,128)(2,1)S(1)}, u32[]{:S(2)}, u32[]{:S(2)}) collective-permute-start(bf16[48,2048]{1,0:T(8,128)(2,1)S(1)} %get-tuple-element.60), channel_id=1, source_target_pairs={{0,6},{1,7},{2,4},{3,5},{4,2},{5,3},{6,0},{7,1},{8,14},{9,15},{10,... | collective-permute-start | bytes 589832 | tf_op jit(solution)/shard_map/ppermute | solution.py:32
  77.4 5.1 %collective-permute-done.10.refs_2_ = bf16[48,2048]{1,0:T(8,128)(2,1)S(1)} collective-permute-done((bf16[48,2048]{1,0:T(8,128)(2,1)S(1)}, bf16[48,2048]{1,0:T(8,128)(2,1)S(1)}, u32[]{:S(2)}, u32[]{:S(2)}) %collective-permute-start.10) | collective-permute-done | bytes 196640 | tf_op jit(solution)/shard_map/ppermute | solution.py:32
  82.5 9.7 %collective-permute-done.11.refs_4_ = bf16[48,2048]{1,0:T(8,128)(2,1)S(1)} collective-permute-done((bf16[48,2048]{1,0:T(8,128)(2,1)S(1)}, bf16[48,2048]{1,0:T(8,128)(2,1)S(1)}, u32[]{:S(2)}, u32[]{:S(2)}) %collective-permute-start.11) | collective-permute-done | bytes 196640 | tf_op jit(solution)/shard_map/ppermute | solution.py:32
  92.2 4.6 %all-to-all-start.2 = ((bf16[8,24,2048]{2,1,0:T(8,128)(2,1)}), bf16[8,24,2048]{2,1,0:T(8,128)(2,1)S(1)}, u32[]{:S(2)}, u32[]{:S(2)}) async-start(bf16[8,24,2048]{2,1,0:T(8,128)(2,1)} %get-tuple-element.61), calls=%async_computation.2 | async-start | bytes 1572864 | tf_op jit(solution)/shard_map/all_to_all | solution.py:455
  101.6 1.8 %collective-permute-start.24 = (bf16[96,2304]{1,0:T(8,128)(2,1)S(1)}, bf16[96,2304]{1,0:T(8,128)(2,1)S(1)}, u32[]{:S(2)}, u32[]{:S(2)}) collective-permute-start(bf16[96,2304]{1,0:T(8,128)(2,1)S(1)} %slice.9), channel_id=1, source_target_pairs={{0,16},{8,24},{16,0},{24,8},{1,17},{9,25},{17,1},{25,9},{2,18},{10... | collective-permute-start | bytes 1327112 | tf_op jit(solution)/shard_map/ppermute | solution.py:32
  104.4 1.5 %collective-permute-start.23 = (bf16[96,2304]{1,0:T(8,128)(2,1)S(1)}, bf16[96,2304]{1,0:T(8,128)(2,1)S(1)}, u32[]{:S(2)}, u32[]{:S(2)}) collective-permute-start(bf16[96,2304]{1,0:T(8,128)(2,1)S(1)} %slice.8), channel_id=1, source_target_pairs={{0,8},{8,0},{16,24},{24,16},{1,9},{9,1},{17,25},{25,17},{2,10},{10... | collective-permute-start | bytes 1327112 | tf_op jit(solution)/shard_map/ppermute | solution.py:32
  106.8 3.4 %collective-permute-done.19.refs_2_ = bf16[64,2048]{1,0:T(8,128)(2,1)S(1)} collective-permute-done((bf16[64,2048]{1,0:T(8,128)(2,1)S(1)}, bf16[64,2048]{1,0:T(8,128)(2,1)S(1)}, u32[]{:S(2)}, u32[]{:S(2)}) %collective-permute-start.19) | collective-permute-done | bytes 262176 | tf_op jit(solution)/shard_map/ppermute | solution.py:32
  110.6 14.7 %collective-permute-done.18.refs_1_ = bf16[64,2048]{1,0:T(8,128)(2,1)S(1)} collective-permute-done((bf16[64,2048]{1,0:T(8,128)(2,1)S(1)}, bf16[64,2048]{1,0:T(8,128)(2,1)S(1)}, u32[]{:S(2)}, u32[]{:S(2)}) %collective-permute-start.18) | collective-permute-done | bytes 262176 | tf_op jit(solution)/shard_map/ppermute | solution.py:32
  126.3 2.8 %collective-permute-done.22.refs_3_ = bf16[192,512]{1,0:T(8,128)(2,1)S(1)} collective-permute-done((bf16[192,512]{1,0:T(8,128)(2,1)S(1)}, bf16[192,512]{1,0:T(8,128)(2,1)S(1)}, u32[]{:S(2)}, u32[]{:S(2)}) %collective-permute-start.22) | collective-permute-done | bytes 196640 | tf_op jit(solution)/shard_map/ppermute | solution.py:32
  129.0 4.8 %weight_grads.1 = (f32[1,512,768]{2,1,0:T(8,128)}, f32[1,512,768]{2,1,0:T(8,128)}, f32[1,768,512]{2,1,0:T(8,128)}) custom-call(bf16[4,192,512]{2,1,0:T(8,128)(2,1)S(1)} %all-to-all-done.1.w_ref, bf16[192,2816]{1,0:T(8,128)(2,1)S(1)} %copy-done.7, bf16[192,2816]{1,0:T(8,128)(2,1)} %collective-permute-done.20.refs_1_, ...), custom_call_target="tpu_custom_call" | custom-call | flops 1811939328 | bytes 4718592 | tf_op jit(solution)/shard_map/weight_grads/pallas_call | solution.py:332
  133.8 1.3 combine_output.1
  (58 shorter events, 17.4 us)
Async XLA Ops:
  3.8 27.3 %all-to-all-start = ((bf16[8,24,2048]{2,1,0:T(8,128)(2,1)}), bf16[8,24,2048]{2,1,0:T(8,128)(2,1)S(1)}, u32[]{:S(2)}, u32[]{:S(2)}) async-start(bf16[8,24,2048]{2,1,0:T(8,128)(2,1)} %get-tuple-element.45), calls=%async_computation | async-start | bytes 1572864 | tf_op jit(solution)/shard_map/all_to_all | solution.py:455
  10.1 26.7 %collective-permute-start.2 = (bf16[64,2048]{1,0:T(8,128)(2,1)S(1)}, bf16[64,2048]{1,0:T(8,128)(2,1)S(1)}, u32[]{:S(2)}, u32[]{:S(2)}) collective-permute-start(bf16[64,2048]{1,0:T(8,128)(2,1)S(1)} %get-tuple-element.43), channel_id=1, source_target_pairs={{0,24},{8,16},{16,8},{24,0},{1,25},{9,17},{17,9},{25,1},{2,26},{10... | collective-permute-start | bytes 786440 | tf_op jit(solution)/shard_map/ppermute | solution.py:32
  12.6 24.2 %collective-permute-start.1 = (bf16[64,2048]{1,0:T(8,128)(2,1)S(1)}, bf16[64,2048]{1,0:T(8,128)(2,1)S(1)}, u32[]{:S(2)}, u32[]{:S(2)}) collective-permute-start(bf16[64,2048]{1,0:T(8,128)(2,1)S(1)} %get-tuple-element.43), channel_id=1, source_target_pairs={{0,16},{8,24},{16,0},{24,8},{1,17},{9,25},{17,1},{25,9},{2,18},{10... | collective-permute-start | bytes 786440 | tf_op jit(solution)/shard_map/ppermute | solution.py:32
  13.1 23.8 %collective-permute-start = (bf16[64,2048]{1,0:T(8,128)(2,1)S(1)}, bf16[64,2048]{1,0:T(8,128)(2,1)S(1)}, u32[]{:S(2)}, u32[]{:S(2)}) collective-permute-start(bf16[64,2048]{1,0:T(8,128)(2,1)S(1)} %get-tuple-element.43), channel_id=1, source_target_pairs={{0,8},{8,0},{16,24},{24,16},{1,9},{9,1},{17,25},{25,17},{2,10},{10... | collective-permute-start | bytes 786440 | tf_op jit(solution)/shard_map/ppermute | solution.py:32
  33.0 22.1 %all-to-all-start.1 = ((bf16[4,192,512]{2,1,0:T(8,128)(2,1)}), bf16[4,192,512]{2,1,0:T(8,128)(2,1)S(1)}, u32[]{:S(2)}, u32[]{:S(2)}) async-start(bf16[4,192,512]{2,1,0:T(8,128)(2,1)} %get-tuple-element.54), calls=%async_computation.1 | async-start | bytes 1572864 | tf_op jit(solution)/shard_map/all_to_all | solution.py:455
  37.2 9.3 %collective-permute-start.4 = (bf16[48,2048]{1,0:T(8,128)(2,1)S(1)}, bf16[48,2048]{1,0:T(8,128)(2,1)S(1)}, u32[]{:S(2)}, u32[]{:S(2)}) collective-permute-start(bf16[48,2048]{1,0:T(8,128)(2,1)S(1)} %get-tuple-element.49), channel_id=1, source_target_pairs={{0,2},{1,3},{2,0},{3,1},{4,6},{5,7},{6,4},{7,5},{8,10},{9,11},{10,... | collective-permute-start | bytes 589832 | tf_op jit(solution)/shard_map/ppermute | solution.py:32
  37.3 17.2 %collective-permute-start.6 = (bf16[48,2048]{1,0:T(8,128)(2,1)S(1)}, bf16[48,2048]{1,0:T(8,128)(2,1)S(1)}, u32[]{:S(2)}, u32[]{:S(2)}) collective-permute-start(bf16[48,2048]{1,0:T(8,128)(2,1)S(1)} %get-tuple-element.51), channel_id=1, source_target_pairs={{0,4},{1,5},{2,6},{3,7},{4,0},{5,1},{6,2},{7,3},{8,12},{9,13},{10,... | collective-permute-start | bytes 589832 | tf_op jit(solution)/shard_map/ppermute | solution.py:32
  39.1 15.4 %collective-permute-start.8 = (bf16[48,2048]{1,0:T(8,128)(2,1)S(1)}, bf16[48,2048]{1,0:T(8,128)(2,1)S(1)}, u32[]{:S(2)}, u32[]{:S(2)}) collective-permute-start(bf16[48,2048]{1,0:T(8,128)(2,1)S(1)} %get-tuple-element.53), channel_id=1, source_target_pairs={{0,6},{1,7},{2,4},{3,5},{4,2},{5,3},{6,0},{7,1},{8,14},{9,15},{10,... | collective-permute-start | bytes 589832 | tf_op jit(solution)/shard_map/ppermute | solution.py:32
  41.7 13.4 %collective-permute-start.3 = (bf16[48,2048]{1,0:T(8,128)(2,1)S(1)}, bf16[48,2048]{1,0:T(8,128)(2,1)S(1)}, u32[]{:S(2)}, u32[]{:S(2)}) collective-permute-start(bf16[48,2048]{1,0:T(8,128)(2,1)S(1)} %get-tuple-element.47.refs_0_), channel_id=1, source_target_pairs={{0,1},{1,0},{2,3},{3,2},{4,5},{5,4},{6,7},{7,6},{8,9},{9,8},{10,11... | collective-permute-start | bytes 589832 | tf_op jit(solution)/shard_map/ppermute | solution.py:32
  46.5 8.6 %collective-permute-start.5 = (bf16[48,2048]{1,0:T(8,128)(2,1)S(1)}, bf16[48,2048]{1,0:T(8,128)(2,1)S(1)}, u32[]{:S(2)}, u32[]{:S(2)}) collective-permute-start(bf16[48,2048]{1,0:T(8,128)(2,1)S(1)} %collective-permute-done.4.refs_2_), channel_id=1, source_target_pairs={{0,1},{1,0},{2,3},{3,2},{4,5},{5,4},{6,7},{7,6},{8,9},{9,8},{10,11... | collective-permute-start | bytes 589832 | tf_op jit(solution)/shard_map/ppermute | solution.py:32
  54.6 2.1 %collective-permute-start.9 = (bf16[48,2048]{1,0:T(8,128)(2,1)S(1)}, bf16[48,2048]{1,0:T(8,128)(2,1)S(1)}, u32[]{:S(2)}, u32[]{:S(2)}) collective-permute-start(bf16[48,2048]{1,0:T(8,128)(2,1)S(1)} %collective-permute-done.8.refs_6_), channel_id=1, source_target_pairs={{0,1},{1,0},{2,3},{3,2},{4,5},{5,4},{6,7},{7,6},{8,9},{9,8},{10,11... | collective-permute-start | bytes 589832 | tf_op jit(solution)/shard_map/ppermute | solution.py:32
  69.3 31.2 %collective-permute-start.20 = (bf16[192,2816]{1,0:T(8,128)(2,1)}, bf16[192,2816]{1,0:T(8,128)(2,1)}, u32[]{:S(2)}, u32[]{:S(2)}) collective-permute-start(bf16[192,2816]{1,0:T(8,128)(2,1)} %get-tuple-element.65), channel_id=1, source_target_pairs={{0,8},{8,0},{16,24},{24,16},{1,9},{9,1},{17,25},{25,17},{2,10},{10... | collective-permute-start | bytes 3244040 | tf_op jit(solution)/shard_map/ppermute | solution.py:32
  71.3 32.0 %collective-permute-start.21 = (bf16[192,2816]{1,0:T(8,128)(2,1)}, bf16[192,2816]{1,0:T(8,128)(2,1)}, u32[]{:S(2)}, u32[]{:S(2)}) collective-permute-start(bf16[192,2816]{1,0:T(8,128)(2,1)} %get-tuple-element.66), channel_id=1, source_target_pairs={{0,16},{8,24},{16,0},{24,8},{1,17},{9,25},{17,1},{25,9},{2,18},{10... | collective-permute-start | bytes 3244040 | tf_op jit(solution)/shard_map/ppermute | solution.py:32
  72.8 9.7 %collective-permute-start.10 = (bf16[48,2048]{1,0:T(8,128)(2,1)S(1)}, bf16[48,2048]{1,0:T(8,128)(2,1)S(1)}, u32[]{:S(2)}, u32[]{:S(2)}) collective-permute-start(bf16[48,2048]{1,0:T(8,128)(2,1)S(1)} %get-tuple-element.58), channel_id=1, source_target_pairs={{0,2},{1,3},{2,0},{3,1},{4,6},{5,7},{6,4},{7,5},{8,10},{9,11},{10,... | collective-permute-start | bytes 589832 | tf_op jit(solution)/shard_map/ppermute | solution.py:32
  75.0 17.2 %collective-permute-start.11 = (bf16[48,2048]{1,0:T(8,128)(2,1)S(1)}, bf16[48,2048]{1,0:T(8,128)(2,1)S(1)}, u32[]{:S(2)}, u32[]{:S(2)}) collective-permute-start(bf16[48,2048]{1,0:T(8,128)(2,1)S(1)} %get-tuple-element.59), channel_id=1, source_target_pairs={{0,4},{1,5},{2,6},{3,7},{4,0},{5,1},{6,2},{7,3},{8,12},{9,13},{10,... | collective-permute-start | bytes 589832 | tf_op jit(solution)/shard_map/ppermute | solution.py:32
  75.2 17.0 %collective-permute-start.12 = (bf16[48,2048]{1,0:T(8,128)(2,1)S(1)}, bf16[48,2048]{1,0:T(8,128)(2,1)S(1)}, u32[]{:S(2)}, u32[]{:S(2)}) collective-permute-start(bf16[48,2048]{1,0:T(8,128)(2,1)S(1)} %get-tuple-element.60), channel_id=1, source_target_pairs={{0,6},{1,7},{2,4},{3,5},{4,2},{5,3},{6,0},{7,1},{8,14},{9,15},{10,... | collective-permute-start | bytes 589832 | tf_op jit(solution)/shard_map/ppermute | solution.py:32
  92.2 41.6 %all-to-all-start.2 = ((bf16[8,24,2048]{2,1,0:T(8,128)(2,1)}), bf16[8,24,2048]{2,1,0:T(8,128)(2,1)S(1)}, u32[]{:S(2)}, u32[]{:S(2)}) async-start(bf16[8,24,2048]{2,1,0:T(8,128)(2,1)} %get-tuple-element.61), calls=%async_computation.2 | async-start | bytes 1572864 | tf_op jit(solution)/shard_map/all_to_all | solution.py:455
  97.3 1.7 %collective-permute-start.15 = (bf16[48,2048]{1,0:T(8,128)(2,1)S(1)}, bf16[48,2048]{1,0:T(8,128)(2,1)S(1)}, u32[]{:S(2)}, u32[]{:S(2)}) collective-permute-start(bf16[48,2048]{1,0:T(8,128)(2,1)S(1)} %collective-permute-done.11.refs_4_), channel_id=1, source_target_pairs={{0,1},{1,0},{2,3},{3,2},{4,5},{5,4},{6,7},{7,6},{8,9},{9,8},{10,11... | collective-permute-start | bytes 589832 | tf_op jit(solution)/shard_map/ppermute | solution.py:32
  100.1 10.1 %collective-permute-start.19 = (bf16[64,2048]{1,0:T(8,128)(2,1)S(1)}, bf16[64,2048]{1,0:T(8,128)(2,1)S(1)}, u32[]{:S(2)}, u32[]{:S(2)}) collective-permute-start(bf16[64,2048]{1,0:T(8,128)(2,1)S(1)} %get-tuple-element.63), channel_id=1, source_target_pairs={{0,24},{8,16},{16,8},{24,0},{1,25},{9,17},{17,9},{25,1},{2,26},{10... | collective-permute-start | bytes 786440 | tf_op jit(solution)/shard_map/ppermute | solution.py:32
  101.6 27.4 %collective-permute-start.24 = (bf16[96,2304]{1,0:T(8,128)(2,1)S(1)}, bf16[96,2304]{1,0:T(8,128)(2,1)S(1)}, u32[]{:S(2)}, u32[]{:S(2)}) collective-permute-start(bf16[96,2304]{1,0:T(8,128)(2,1)S(1)} %slice.9), channel_id=1, source_target_pairs={{0,16},{8,24},{16,0},{24,8},{1,17},{9,25},{17,1},{25,9},{2,18},{10... | collective-permute-start | bytes 1327112 | tf_op jit(solution)/shard_map/ppermute | solution.py:32
  104.4 24.6 %collective-permute-start.23 = (bf16[96,2304]{1,0:T(8,128)(2,1)S(1)}, bf16[96,2304]{1,0:T(8,128)(2,1)S(1)}, u32[]{:S(2)}, u32[]{:S(2)}) collective-permute-start(bf16[96,2304]{1,0:T(8,128)(2,1)S(1)} %slice.8), channel_id=1, source_target_pairs={{0,8},{8,0},{16,24},{24,16},{1,9},{9,1},{17,25},{25,17},{2,10},{10... | collective-permute-start | bytes 1327112 | tf_op jit(solution)/shard_map/ppermute | solution.py:32
  105.9 19.4 %collective-permute-start.18 = (bf16[64,2048]{1,0:T(8,128)(2,1)S(1)}, bf16[64,2048]{1,0:T(8,128)(2,1)S(1)}, u32[]{:S(2)}, u32[]{:S(2)}) collective-permute-start(bf16[64,2048]{1,0:T(8,128)(2,1)S(1)} %get-tuple-element.63), channel_id=1, source_target_pairs={{0,16},{8,24},{16,0},{24,8},{1,17},{9,25},{17,1},{25,9},{2,18},{10... | collective-permute-start | bytes 786440 | tf_op jit(solution)/shard_map/ppermute | solution.py:32
  106.5 18.8 %collective-permute-start.17 = (bf16[64,2048]{1,0:T(8,128)(2,1)S(1)}, bf16[64,2048]{1,0:T(8,128)(2,1)S(1)}, u32[]{:S(2)}, u32[]{:S(2)}) collective-permute-start(bf16[64,2048]{1,0:T(8,128)(2,1)S(1)} %get-tuple-element.63), channel_id=1, source_target_pairs={{0,8},{8,0},{16,24},{24,16},{1,9},{9,1},{17,25},{25,17},{2,10},{10... | collective-permute-start | bytes 786440 | tf_op jit(solution)/shard_map/ppermute | solution.py:32
  110.3 18.8 %collective-permute-start.22 = (bf16[192,512]{1,0:T(8,128)(2,1)S(1)}, bf16[192,512]{1,0:T(8,128)(2,1)S(1)}, u32[]{:S(2)}, u32[]{:S(2)}) collective-permute-start(bf16[192,512]{1,0:T(8,128)(2,1)S(1)} %get-tuple-element.67), channel_id=1, source_target_pairs={{0,24},{8,16},{16,8},{24,0},{1,25},{9,17},{17,9},{25,1},{2,26},{10... | collective-permute-start | bytes 589832 | tf_op jit(solution)/shard_map/ppermute | solution.py:32
  (12 other events, 64.3 us)

commit v3 on v2

v3 whole, which is shorter than its diff:
```python
import functools

import jax
import jax.numpy as jnp
from jax import lax
from jax.experimental import pallas as pl
from jax.experimental.pallas import tpu as pltpu
from jax.sharding import PartitionSpec as P

F32 = jnp.float32
BF16 = jnp.bfloat16
VMEM = pltpu.VMEM
WHOLE = pl.BlockSpec(memory_space=pltpu.VMEM)
TILE = 256
PIECES = 4
MIB = 1024 * 1024


def params(mib):
    return pltpu.CompilerParams(vmem_limit_bytes=mib * MIB)


def in_hbm(*arrays):
    return [pltpu.with_memory_space_constraint(a, pltpu.HBM) for a in arrays]


def cost(flops, bytes_accessed):
    return pl.CostEstimate(flops=int(flops), bytes_accessed=int(bytes_accessed), transcendentals=0)


def xor_permute(array, axis, key):
    size = lax.axis_size(axis)
    return lax.ppermute(array, axis, [(i, i ^ key) for i in range(size)])


def column_of(row, length):
    diagonal = lax.broadcasted_iota(jnp.int32, (length, length), 0) == lax.broadcasted_iota(
        jnp.int32, (length, length), 1
    )
    spread = jnp.where(diagonal, jnp.broadcast_to(row.astype(F32), (length, length)), 0.0)
    return jnp.sum(spread, axis=1, keepdims=True)


def table_columns(table, order):
    return jnp.concatenate([column_of(row, row.shape[1]) for row in (table(e) for e in order)], axis=0)


def keep_valid(values, lengths, first_slot, slot_len):
    rows = lax.broadcasted_iota(jnp.int32, values.shape, 0)
    limit = jnp.zeros(values.shape, jnp.int32)
    for slot in range(values.shape[0] // slot_len):
        used = lengths[:, first_slot + slot : first_slot + slot + 1]
        limit = jnp.where(rows // slot_len == slot, slot * slot_len + used, limit)
    return jnp.where(rows < limit, values.astype(F32), 0.0).astype(values.dtype)


def prepare_kernel(sizes, *refs):
    window, capacity, tok_dev, slot_len = sizes
    sources, outs, held = refs[:6], refs[6:12], refs[12:18]
    high_held, fine_held, sems = refs[18:]
    copies = [
        pltpu.make_async_copy(source, place, sems.at[i])
        for i, (source, place) in enumerate(zip(sources, held))
    ]
    for copy in copies:
        copy.start()
    for copy in copies:
        copy.wait()
    rows_ref, gates_ref, counts_ref, lengths_ref, tok_ref, cot_ref = held
    moved_ref, low_ref, weighted_ref, hit_ref, high_ref, fine_ref = outs
    me = lax.axis_index("expert")
    half = tok_dev // 2
    lengths = lengths_ref[...]
    moved_ref[...] = keep_valid(tok_ref[half:, :], lengths, half // slot_len, slot_len)
    low_ref[...] = keep_valid(tok_ref[:half, :], lengths, 0, slot_len)

    def gate_of(e):
        slot = lax.broadcasted_iota(jnp.int32, (1, capacity), 1)
        owner = lax.broadcasted_iota(jnp.int32, (1, window), 1) == e
        count = jnp.sum(jnp.where(owner, counts_ref[...].astype(F32), 0.0), axis=1, keepdims=True)
        return jnp.where(slot.astype(F32) < count, gates_ref[0, pl.ds(e, 1), :], 0.0)

    order = [me ^ d for d in range(window)]
    gate = table_columns(gate_of, order)
    index = table_columns(lambda e: rows_ref[0, pl.ds(e, 1), :], order).astype(jnp.int32)
    hit = lax.broadcasted_iota(jnp.int32, (window * capacity, tok_dev), 1) == index
    hit_ref[...] = hit.astype(BF16)
    table = jnp.where(hit, jnp.broadcast_to(gate, hit.shape), 0.0)
    high = table.astype(BF16)
    high_held[...] = high
    fine_held[...] = (table - high.astype(F32)).astype(BF16)
    copies = [
        pltpu.make_async_copy(high_held, high_ref, sems.at[0]),
        pltpu.make_async_copy(fine_held, fine_ref, sems.at[1]),
    ]
    for copy in copies:
        copy.start()
    picked = jnp.dot(hit.astype(BF16), cot_ref[...], preferred_element_type=F32)
    weighted = gate * picked
    for d, e in enumerate(order):
        weighted_ref[e] = weighted[d * capacity : (d + 1) * capacity].astype(BF16)
    for copy in copies:
        copy.wait()


def prepare(slot_rows, slot_gates, slot_counts, seq_lengths, tokens, cotangent):
    tok_dev, width = tokens.shape
    window, capacity = slot_rows.shape[1:]
    half = tok_dev // 2
    slot_len = tok_dev // seq_lengths.shape[1]
    sources = (slot_rows, slot_gates, slot_counts, seq_lengths, tokens, cotangent)
    table = jax.ShapeDtypeStruct((window * capacity, tok_dev), BF16)
    return pl.pallas_call(
        functools.partial(prepare_kernel, (window, capacity, tok_dev, slot_len)),
        out_shape=[
            jax.ShapeDtypeStruct((half, width), BF16),
            jax.ShapeDtypeStruct((half, width), BF16),
            jax.ShapeDtypeStruct((window, capacity, width), BF16),
            table,
            pltpu.HBM(table.shape, table.dtype),
            pltpu.HBM(table.shape, table.dtype),
        ],
        in_specs=[pl.BlockSpec(memory_space=pltpu.HBM)] * len(sources),
        out_specs=[WHOLE] * 4 + [pl.BlockSpec(memory_space=pltpu.HBM)] * 2,
        scratch_shapes=[VMEM(a.shape, a.dtype) for a in sources]
        + [VMEM(table.shape, BF16)] * 2
        + [pltpu.SemaphoreType.DMA((len(sources),))],
        compiler_params=params(12),
        cost_estimate=cost(2 * window * capacity * tok_dev * width, 5 * tok_dev * width),
        name="prepare",
    )(*in_hbm(*sources))


def pick_kernel(pair, hit_ref, low_ref, arrived_ref, *outs):
    shuffled = jnp.concatenate([low_ref[...], arrived_ref[...]], axis=0)
    picked = jnp.dot(hit_ref[...], shuffled, preferred_element_type=F32).astype(BF16)
    for z, out in enumerate(outs):
        out[...] = picked[z * pair : (z + 1) * pair]


def pick(hit, low, arrived, capacity):
    pair, width = 2 * capacity, low.shape[1]
    slots, tok_dev = hit.shape
    return pl.pallas_call(
        functools.partial(pick_kernel, pair),
        out_shape=[jax.ShapeDtypeStruct((pair, width), BF16)] * (slots // pair),
        in_specs=[WHOLE] * 3,
        out_specs=[WHOLE] * (slots // pair),
        compiler_params=params(8),
        cost_estimate=cost(2 * slots * tok_dev * width, 5 * tok_dev * width),
        name="pick",
    )(hit, low, arrived)


def joined(direct, crossed, capacity, columns=slice(None)):
    one, other = direct[:, columns].astype(F32), crossed[:, columns].astype(F32)
    rows = lax.broadcasted_iota(jnp.int32, one.shape, 0)
    return jnp.where(rows < capacity, one, other).astype(BF16)


def share_columns(rows, outs):
    me = lax.axis_index("dp")
    share = outs[0].shape[1]
    for j, out in enumerate(outs):
        out[...] = rows[:, pl.ds(pl.multiple_of((me ^ j) * share, share), share)]


def gather_kernel(weighted_ref, rows_ref, shares_ref):
    me = lax.axis_index("expert")
    window, capacity, _ = weighted_ref.shape
    pair = 2 * capacity
    for z in range(window // 2):
        both = [weighted_ref[me ^ (2 * z + core)].astype(F32) for core in range(2)]
        rows_ref[z * pair : (z + 1) * pair, :] = jnp.concatenate(both, axis=0).astype(BF16)
    share = shares_ref.shape[2]
    for g in range(shares_ref.shape[0]):
        shares_ref[g] = rows_ref[:, g * share : (g + 1) * share]


def gather_rows(weighted):
    window, capacity, width = weighted.shape
    rows = window * capacity
    replicas = lax.axis_size("dp")
    return pl.pallas_call(
        gather_kernel,
        out_shape=[
            jax.ShapeDtypeStruct((rows, width), BF16),
            jax.ShapeDtypeStruct((replicas, rows, width // replicas), BF16),
        ],
        in_specs=[WHOLE],
        out_specs=[WHOLE] * 2,
        compiler_params=params(12),
        cost_estimate=cost(0, 8 * rows * width),
        name="gather_rows",
    )(weighted)


def expert_kernel(sizes, *refs):
    count, capacity, tile, replicas = sizes
    x_refs, w_ref, weights = refs[: 2 * count], refs[2 * count], refs[2 * count + 1 : 2 * count + 4]
    tok_refs = refs[2 * count + 4 : 3 * count + 4]
    out_ref, sent_refs = refs[3 * count + 4], refs[3 * count + 5 : 3 * count + 5 + replicas]
    x_all, hid_all, gg_all, gu_all, pre_gate, grad_hidden, own_held, *held, sems = refs[
        3 * count + 5 + replicas :
    ]
    own_copy = pltpu.make_async_copy(own_held, sent_refs[0], sems.at[3, 0])
    sent_refs = [own_held, *sent_refs[1:]]
    gate_ref, up_ref, down_ref = held
    copies = []
    for i, (source, place) in enumerate(zip(weights, held)):
        part = source.shape[1] // PIECES
        pieces = [pl.ds(k * part, part) for k in range(PIECES)]
        copies.append(
            [
                pltpu.make_async_copy(source.at[:, rows, :], place.at[:, rows, :], sems.at[i, k])
                for k, rows in enumerate(pieces)
            ]
        )
    for copy in copies[0] + copies[2]:
        copy.start()
    me = lax.axis_index("expert")
    pair = 2 * capacity
    width = x_all.shape[1]
    share = width // replicas
    turned = (((1,), (1,)), ((), ()))
    for z in range(count):
        x_all[z * pair : (z + 1) * pair, :] = joined(x_refs[2 * z], x_refs[2 * z + 1], capacity)
    share_columns(x_all, [s.at[:, s.shape[1] - share :] for s in sent_refs])
    spans = [slice(f * tile, (f + 1) * tile) for f in range(hid_all.shape[1] // tile)]
    for copy in copies[0]:
        copy.wait()
    for copy in copies[1]:
        copy.start()
    for span in spans:
        pre_gate[:, span] = jnp.dot(x_all[...], gate_ref[0, :, span], preferred_element_type=F32)
    for copy in copies[2]:
        copy.wait()
    for span in spans:
        grad_hidden[:, span] = lax.dot_general(
            w_ref[...], down_ref[0, span, :], turned, preferred_element_type=F32
        )
    for copy in copies[1]:
        copy.wait()
    for f, span in enumerate(spans):
        gate, grad = pre_gate[:, span], grad_hidden[:, span]
        pre_up = jnp.dot(x_all[...], up_ref[0, :, span], preferred_element_type=F32)
        sig = jax.nn.sigmoid(gate)
        silu = gate * sig
        hid_all[:, span] = (silu * pre_up).astype(BF16)
        gg_all[:, span] = (grad * pre_up * sig * (1.0 + gate * (1.0 - sig))).astype(BF16)
        gu_all[:, span] = (grad * silu).astype(BF16)
        for sent in sent_refs:
            if sent.shape[1] > share:
                for k, source in enumerate((hid_all, gg_all, gu_all)):
                    sent[:, (3 * f + k) * tile : (3 * f + k + 1) * tile] = source[:, span]
    own_copy.start()
    wide = 2 * tile
    for n in range(width // wide):
        span = slice(n * wide, (n + 1) * wide)
        tok = lax.dot_general(
            gg_all[...], gate_ref[0, span, :], turned, preferred_element_type=F32
        ) + lax.dot_general(gu_all[...], up_ref[0, span, :], turned, preferred_element_type=F32)
        tok = tok.astype(BF16)
        out = jnp.dot(hid_all[...], down_ref[0, :, span], preferred_element_type=F32)
        for z in range(count):
            tok_refs[z][:, span] = tok[z * pair : (z + 1) * pair]
        for d in range(2 * count):
            out_ref[me ^ d, :, span] = out[d * capacity : (d + 1) * capacity].astype(BF16)
    own_copy.wait()


def expert(x_pairs, w_rows, w_gate, w_up, w_down, capacity):
    count = len(x_pairs)
    flat = [a for p in x_pairs for a in p]
    pair, width = flat[0].shape
    hidden_units = w_gate.shape[2]
    rows = count * pair
    replicas = lax.axis_size("dp")
    share = width // replicas
    block = jax.ShapeDtypeStruct((pair, width), BF16)
    sent = [jax.ShapeDtypeStruct((rows, 3 * hidden_units + share), BF16)] * replicas
    if replicas == 4:
        sent[3] = jax.ShapeDtypeStruct((rows, share), BF16)
    sent[0] = pltpu.HBM(sent[0].shape, sent[0].dtype)
    results = pl.pallas_call(
        functools.partial(expert_kernel, (count, capacity, TILE, replicas)),
        out_shape=[block] * count
        + [jax.ShapeDtypeStruct((2 * count, capacity, width), BF16)]
        + sent,
        in_specs=[WHOLE] * (2 * count + 1) + [pl.BlockSpec(memory_space=pltpu.HBM)] * 3,
        out_specs=[WHOLE] * (count + 1)
        + [pl.BlockSpec(memory_space=pltpu.HBM)]
        + [WHOLE] * (replicas - 1),
        scratch_shapes=[VMEM((rows, width), BF16)]
        + [VMEM((rows, hidden_units), BF16)] * 3
        + [VMEM((rows, hidden_units), F32)] * 2
        + [VMEM(sent[0].shape, BF16)]
        + [VMEM(a.shape, BF16) for a in (w_gate, w_up, w_down)]
        + [pltpu.SemaphoreType.DMA((4, PIECES))],
        compiler_params=params(32 if replicas <= 4 else 56),
        cost_estimate=cost(
            12 * rows * width * hidden_units, 6 * width * hidden_units + 10 * rows * width
        ),
        name="expert",
    )(*flat, w_rows, *in_hbm(w_gate, w_up, w_down))
    return results[:count], results[count], results[count + 1 :]


def final_kernel(sizes, *refs):
    share, tile, parts = sizes
    loads, refs = list(refs[:3]), refs[3:]
    low_ref, arrived_ref, back_ref, w_ref, refs = *refs[:4], refs[4:]
    others, outs, scratch = refs[:-14], refs[-14:-9], refs[-9:]
    own_held, high_ref, fine_ref, out_held, *held, sems, side_sems = scratch
    loads = [
        pltpu.make_async_copy(a, b, side_sems.at[i])
        for i, (a, b) in enumerate(zip(loads, (own_held, high_ref, fine_ref)))
    ]
    half = low_ref.shape[0]
    stores = [
        pltpu.make_async_copy(low_ref, outs[1].at[:half], side_sems.at[3]),
        pltpu.make_async_copy(arrived_ref, outs[1].at[half:], side_sems.at[4]),
    ]
    for copy in loads + stores:
        copy.start()
    for copy in loads:
        copy.wait()
    me = lax.axis_index("dp")
    sources = [own_held, *others]
    acts_width = sources[0].shape[1] - share
    across = (((0,), (0,)), ((), ()))
    x = jnp.concatenate([r[:, r.shape[1] - share :] for r in sources[:parts]], axis=0)
    w = jnp.concatenate([w_ref[me ^ j] for j in range(parts)], axis=0)
    acts = [r for r in sources if r.shape[1] > share]
    for f in range(acts_width // (3 * tile)):
        hidden, grad_gate, grad_up = [
            jnp.concatenate(
                [a[:, (3 * f + k) * tile : (3 * f + k + 1) * tile] for a in acts], axis=0
            )
            for k in range(3)
        ]
        span = pl.ds(f * tile, tile)
        gate_held, up_held, down_held = [h.at[f] for h in held]
        gate_held[...] = lax.dot_general(x, grad_gate, across, preferred_element_type=F32)
        up_held[...] = lax.dot_general(x, grad_up, across, preferred_element_type=F32)
        down_held[...] = lax.dot_general(hidden, w, across, preferred_element_type=F32)
        pieces = [
            (gate_held, outs[2].at[0, :, span]),
            (up_held, outs[3].at[0, :, span]),
            (down_held, outs[4].at[0, span, :]),
        ]
        for i, (a, b) in enumerate(pieces):
            copy = pltpu.make_async_copy(a, b, sems.at[f, i])
            copy.start()
            stores.append(copy)
    expert_id = lax.axis_index("expert")
    rows = jnp.concatenate(
        [back_ref[expert_id ^ d].astype(F32) for d in range(back_ref.shape[0])], axis=0
    ).astype(BF16)
    total = lax.dot_general(high_ref[...], rows, across, preferred_element_type=F32)
    total += lax.dot_general(fine_ref[...], rows, across, preferred_element_type=F32)
    out_held[...] = total.astype(BF16)
    stores.append(pltpu.make_async_copy(out_held, outs[0], side_sems.at[5]))
    stores[-1].start()
    for copy in stores:
        copy.wait()


def final(high, fine, back, low, arrived, w_shares, received):
    parts, rows, share = w_shares.shape
    half, width = low.shape
    hidden_units = (received[0].shape[1] - share) // 3
    tile = TILE
    tiles = hidden_units // tile
    hbm = pl.BlockSpec(memory_space=pltpu.HBM)
    return pl.pallas_call(
        functools.partial(final_kernel, (share, tile, parts)),
        out_shape=[
            jax.ShapeDtypeStruct((2 * half, width), BF16),
            jax.ShapeDtypeStruct((2 * half, width), BF16),
            jax.ShapeDtypeStruct((1, share, hidden_units), F32),
            jax.ShapeDtypeStruct((1, share, hidden_units), F32),
            jax.ShapeDtypeStruct((1, hidden_units, share), F32),
        ],
        in_specs=[hbm] * 3 + [WHOLE] * (3 + len(received)),
        out_specs=[hbm] * 5,
        scratch_shapes=[
            VMEM(received[0].shape, BF16),
            VMEM(high.shape, BF16),
            VMEM(fine.shape, BF16),
            VMEM((2 * half, width), BF16),
            VMEM((tiles, share, tile), F32),
            VMEM((tiles, share, tile), F32),
            VMEM((tiles, tile, share), F32),
            pltpu.SemaphoreType.DMA((tiles, 3)),
            pltpu.SemaphoreType.DMA((6,)),
        ],
        compiler_params=params(24 if parts <= 4 else 60),
        cost_estimate=cost(6 * parts * rows * share * hidden_units, 12 * share * hidden_units),
        name="final",
    )(*in_hbm(received[0], high, fine), low, arrived, back, w_shares, *received[1:])


def grads_kernel(capacity, hit_ref, *refs):
    pairs, (low_ref, high_ref) = refs[:-2], refs[-2:]
    rows = jnp.concatenate(
        [joined(pairs[i], pairs[i + 1], capacity) for i in range(0, len(pairs), 2)], axis=0
    )
    across = (((0,), (0,)), ((), ()))
    total = lax.dot_general(hit_ref[...], rows, across, preferred_element_type=F32).astype(BF16)
    half = low_ref.shape[0]
    low_ref[...] = total[:half]
    high_ref[...] = total[half:]


def combine_grads(hit, pairs, capacity):
    slots, tok_dev = hit.shape
    flat = [a for p in pairs for a in p]
    width = flat[0].shape[1]
    half = jax.ShapeDtypeStruct((tok_dev // 2, width), BF16)
    return pl.pallas_call(
        functools.partial(grads_kernel, capacity),
        out_shape=[half, half],
        in_specs=[WHOLE] * (1 + len(flat)),
        out_specs=[WHOLE, WHOLE],
        compiler_params=params(12),
        cost_estimate=cost(2 * slots * tok_dev * width, 6 * tok_dev * width),
        name="combine_grads",
    )(hit, *flat)


def send_chips(blocks):
    return [xor_permute(b, "expert", 2 * z) if z else b for z, b in enumerate(blocks)]


def cross(direct, waits=()):
    return [
        (block, xor_permute(after(block, *waits) if z else block, "expert", 1))
        for z, block in enumerate(direct)
    ]


def swapped(array, key):
    ways = [
        functools.partial(xor_permute, axis="dp", key=j) for j in range(1, lax.axis_size("dp"))
    ]
    return lax.switch(key - 1, ways, array)


def spread_acts(sent):
    if lax.axis_size("dp") != 4:
        return [sent[0]] + [xor_permute(sent[j], "dp", j) for j in range(1, len(sent))], []
    half = sent[0].shape[0] // 2
    near = xor_permute(sent[1], "dp", 1)
    side = xor_permute(sent[2], "dp", 2)
    far = xor_permute(sent[3], "dp", 3)
    passed = [side[:half], near[half:]]
    halves = [xor_permute(passed[0], "dp", 1), xor_permute(passed[1], "dp", 2)]
    return [sent[0], near, side, far, *halves], passed


def after(value, *others):
    return lax.optimization_barrier((value, *others))[0] if others else value


def all_to_all(array, axis):
    return lax.all_to_all(array, axis, split_axis=0, concat_axis=0, tiled=True)


def per_device(
    tokens,
    cotangent,
    w_gate,
    w_up,
    w_down,
    slot_rows,
    slot_counts,
    slot_gates,
    seq_lengths,
    matching,
):
    capacity = slot_rows.shape[2]
    key = matching[0, 0]
    moved, low, weighted, hit, high, fine = prepare(
        slot_rows, slot_gates, slot_counts, seq_lengths, tokens, cotangent
    )
    weighted = all_to_all(weighted, "expert")
    picked = pick(hit, low, swapped(moved, key), capacity)
    x_direct = send_chips(picked)
    w_rows, w_shares = gather_rows(weighted)
    w_shares = all_to_all(w_shares, "dp")
    x_pairs = cross(x_direct, [w_rows])
    token_rows, expert_out, sent = expert(x_pairs, w_rows, w_gate, w_up, w_down, capacity)
    tok_pairs = cross(send_chips(token_rows))
    received, early = spread_acts(sent)
    back = all_to_all(after(expert_out, w_shares, *[p[0] for p in tok_pairs]), "expert")
    low_grads, high_grads = combine_grads(hit, tok_pairs, capacity)
    return tuple(
        final(high, fine, back, low_grads, swapped(high_grads, key), w_shares, received)
    )


def solution(mesh):
    return jax.shard_map(
        per_device,
        mesh=mesh,
        in_specs=(
            P(("dp", "expert"), None),
            P(("dp", "expert"), None),
            P("expert", None, None),
            P("expert", None, None),
            P("expert", None, None),
            P(("dp", "expert"), None, None),
            P(("dp", "expert"), None),
            P(("dp", "expert"), None, None),
            P(("dp", "expert"), None),
            P("expert", None),
        ),
        out_specs=(
            P(("dp", "expert"), None),
            P(("dp", "expert"), None),
            P("expert", "dp", None),
            P("expert", "dp", None),
            P("expert", None, "dp"),
        ),
        check_vma=False,
    )
```

time: 136 us -> 121 us (0.89)
  waiting for transfers between devices: 68.6 us -> 57.4 us
  starting transfers between devices: 37.6 us -> 34.3 us
  local copies, waits for them, and re-layouts: 7.16 us -> 4.4 us
  Pallas kernels: 21 us -> 22.7 us
    ppermute x25 -> x21, waiting for transfers between devices: 51.1 us -> 42.6 us  [xor_permute(): return lax.ppermute(array, axis, [(i, i ^ key) for i in range(size)])]
    unnamed x16 -> x18, local copies, waits for them, and re-layouts: 5.07 us -> 1.69 us
    ppermute x25 -> x21, starting transfers between devices: 22.9 us -> 19.7 us  [xor_permute(): return lax.ppermute(array, axis, [(i, i ^ key) for i in range(size)])]
    all_to_all x3, waiting for transfers between devices: 17.5 us -> 14.7 us  [all_to_all(): return lax.all_to_all(array, axis, split_axis=0, concat_axis=0, tiled=True)]
    pallas_call x3 -> x1, Pallas kernels: 6.99 us -> 6.35 us  [final(): pl.pallas_call(functools.partial(final_kernel, (share, tile, parts)), out...]
  transfers between devices with their start and end apart: 28 -> 24, of which waited for: 12 -> 11; matrix products, arithmetic and copies ran while one was open for 2% -> 2% of each run, Pallas kernels for 6% -> 11%
where the time goes in v3:
time: 121 us; the launch traced here: 120 us
  waiting for transfers between devices  57.4 us (47%)
  starting transfers between devices  34.3 us (28%)
  Pallas kernels  22.7 us (19%)
  local copies, waits for them, and re-layouts  4.4 us (4%)
    ppermute x21, waiting for transfers between devices, xor_permute(): return lax.ppermute(array, axis, [(i, i ^ key) for i in range(size)])  42.6 us
    ppermute x21, starting transfers between devices, xor_permute(): return lax.ppermute(array, axis, [(i, i ^ key) for i in range(size)])  19.7 us
    all_to_all x3, waiting for transfers between devices, all_to_all(): return lax.all_to_all(array, axis, split_axis=0, concat_axis=0, tiled=True)  14.7 us
    all_to_all x3, starting transfers between devices, all_to_all(): return lax.all_to_all(array, axis, split_axis=0, concat_axis=0, tiled=True)  14.5 us
    pallas_call x1, Pallas kernels, expert(): pl.pallas_call(functools.partial(expert_kernel, (count, capacity, TILE, r...  10.1 us
    pallas_call x1, Pallas kernels, final(): pl.pallas_call(functools.partial(final_kernel, (share, tile, parts)), out...  6.35 us
    pallas_call x1, Pallas kernels, prepare(): pl.pallas_call(functools.partial(prepare_kernel, (window, capacity, tok_d...  3.58 us
    slice x2, local copies, waits for them, and re-layouts, spread_acts(): passed = [side[:half], near[half:]]  2.71 us
  transfers between devices with their start and end apart: 24, of which 11 were waited for; matrix products, arithmetic and copies ran while one was open for 2% of the time, Pallas kernels for 11%

profile of v3, /device:TPU:0, one launch (start us, length us, event | category | flops | bytes accessed | tf_op | source)
XLA Modules:
  0.0 119.6 jit_solution(9858690974811923074)
XLA Ops:
  0.6 3.6 %prepare.1 = (bf16[64,2048]{1,0:T(8,128)(2,1)S(1)}, bf16[64,2048]{1,0:T(8,128)(2,1)S(1)}, bf16[8,24,2048]{2,1,0:T(8,128)(2,1)}, bf16[192,128]{1,0:T(8,128)(2,1)S...) custom-call(s32[1,8,24]{2,1,0:T(8,128)} %refs_0_.1, f32[1,8,24]{2,1,0:T(8,128)} %refs_1_.1, s32[1,8]{1,0:T(1,128)} %refs_2_.1, ...), custom_call_target="tpu_custom_call" | custom-call | flops 100663296 | bytes 1310720 | tf_op jit(solution)/shard_map/prepare/pallas_call | solution.py:113
  4.2 6.3 %all-to-all-start = ((bf16[8,24,2048]{2,1,0:T(8,128)(2,1)}), bf16[8,24,2048]{2,1,0:T(8,128)(2,1)S(1)}, u32[]{:S(2)}, u32[]{:S(2)}) async-start(bf16[8,24,2048]{2,1,0:T(8,128)(2,1)} %get-tuple-element.51), calls=%async_computation | async-start | bytes 1572864 | tf_op jit(solution)/shard_map/all_to_all | solution.py:467
  10.6 9.4 %conditional.2 = (bf16[64,2048]{1,0:T(8,128)(2,1)}) conditional(s32[]{:T(128)} %bitcast, bf16[64,2048]{1,0:T(8,128)(2,1)S(1)} %get-tuple-element.48, bf16[64,2048]{1,0:T(8,128)(2,1)S(1)} %get-tuple-element.48, bf16[64,2048]{1,0:T(8,128)(2,1)S(1)} %get-tuple-element.48), branch_computations={%region_0.0_spmd, %region_1.0_spmd, %region_2.0_spmd} | conditional | bytes 1048624 | solution.py:447
  10.6 1.6 %collective-permute-start.1 = (bf16[64,2048]{1,0:T(8,128)(2,1)S(1)}, bf16[64,2048]{1,0:T(8,128)(2,1)}, u32[]{:S(2)}, u32[]{:S(2)}) collective-permute-start(bf16[64,2048]{1,0:T(8,128)(2,1)S(1)} %param.1), channel_id=1, source_target_pairs={{0,16},{8,24},{16,0},{24,8},{1,17},{9,25},{17,1},{25,9},{2,18},{10... | collective-permute-start | bytes 786440 | tf_op jit(solution)/shard_map/cond/branch_1_fun/ppermute | solution.py:33
  12.2 7.8 %collective-permute-done.1 = bf16[64,2048]{1,0:T(8,128)(2,1)} collective-permute-done((bf16[64,2048]{1,0:T(8,128)(2,1)S(1)}, bf16[64,2048]{1,0:T(8,128)(2,1)}, u32[]{:S(2)}, u32[]{:S(2)}) %collective-permute-start.1) | collective-permute-done | bytes 262176 | tf_op jit(solution)/shard_map/cond/branch_1_fun/ppermute | solution.py:33
  21.3 3.1 %collective-permute-start.11 = (bf16[48,2048]{1,0:T(8,128)(2,1)S(1)}, bf16[48,2048]{1,0:T(8,128)(2,1)S(1)}, u32[]{:S(2)}, u32[]{:S(2)}) collective-permute-start(bf16[48,2048]{1,0:T(8,128)(2,1)S(1)} %get-tuple-element.56), channel_id=1, source_target_pairs={{0,6},{1,7},{2,4},{3,5},{4,2},{5,3},{6,0},{7,1},{8,14},{9,15},{10,... | collective-permute-start | bytes 589832 | tf_op jit(solution)/shard_map/ppermute | solution.py:33
  25.8 14.7 %all-to-all-done.weighted_ref = bf16[8,24,2048]{2,1,0:T(8,128)(2,1)S(1)} async-done(((bf16[8,24,2048]{2,1,0:T(8,128)(2,1)}), bf16[8,24,2048]{2,1,0:T(8,128)(2,1)S(1)}, u32[]{:S(2)}, u32[]{:S(2)}) %all-to-all-start) | async-done | bytes 786464 | tf_op jit(solution)/shard_map/all_to_all | solution.py:467
  41.5 7.0 %collective-permute-done.9.refs_4_ = bf16[48,2048]{1,0:T(8,128)(2,1)S(1)} collective-permute-done((bf16[48,2048]{1,0:T(8,128)(2,1)S(1)}, bf16[48,2048]{1,0:T(8,128)(2,1)S(1)}, u32[]{:S(2)}, u32[]{:S(2)}) %collective-permute-start.9) | collective-permute-done | bytes 196640 | tf_op jit(solution)/shard_map/ppermute | solution.py:33
  49.0 3.7 %all-to-all-start.1 = ((bf16[4,192,512]{2,1,0:T(8,128)(2,1)}), bf16[4,192,512]{2,1,0:T(8,128)(2,1)S(1)}, u32[]{:S(2)}, u32[]{:S(2)}) async-start(bf16[4,192,512]{2,1,0:T(8,128)(2,1)} %get-tuple-element.68), calls=%async_computation.1 | async-start | bytes 1572864 | tf_op jit(solution)/shard_map/all_to_all | solution.py:467
  52.7 10.1 %expert.1 = (bf16[48,2048]{1,0:T(8,128)(2,1)S(1)}, bf16[48,2048]{1,0:T(8,128)(2,1)S(1)}, bf16[48,2048]{1,0:T(8,128)(2,1)S(1)}, bf16[48,2048]{1,0:T(8,128)(2,1)S(...) custom-call(bf16[48,2048]{1,0:T(8,128)(2,1)S(1)} %get-tuple-element., ...), custom_call_target="tpu_custom_call" | custom-call | flops 3623878656 | bytes 13369344 | tf_op jit(solution)/shard_map/expert/pallas_call | solution.py:285
  62.8 2.1 %collective-permute-start.20 = (bf16[192,2816]{1,0:T(8,128)(2,1)}, bf16[192,2816]{1,0:T(8,128)(2,1)S(1)}, u32[]{:S(2)}, u32[]{:S(2)}) collective-permute-start(bf16[192,2816]{1,0:T(8,128)(2,1)} %get-tuple-element.70), channel_id=1, source_target_pairs={{0,8},{8,0},{16,24},{24,16},{1,9},{9,1},{17,25},{25,17},{2,10},{10... | collective-permute-start | bytes 3244040 | tf_op jit(solution)/shard_map/ppermute | solution.py:33
  64.9 1.5 %collective-permute-start.21 = (bf16[192,2816]{1,0:T(8,128)(2,1)}, bf16[192,2816]{1,0:T(8,128)(2,1)}, u32[]{:S(2)}, u32[]{:S(2)}) collective-permute-start(bf16[192,2816]{1,0:T(8,128)(2,1)} %get-tuple-element.71), channel_id=1, source_target_pairs={{0,16},{8,24},{16,0},{24,8},{1,17},{9,25},{17,1},{25,9},{2,18},{10... | collective-permute-start | bytes 3244040 | tf_op jit(solution)/shard_map/ppermute | solution.py:33
  66.4 1.9 %collective-permute-start.16 = (bf16[48,2048]{1,0:T(8,128)(2,1)S(1)}, bf16[48,2048]{1,0:T(8,128)(2,1)S(1)}, u32[]{:S(2)}, u32[]{:S(2)}) collective-permute-start(bf16[48,2048]{1,0:T(8,128)(2,1)S(1)} %get-tuple-element.63), channel_id=1, source_target_pairs={{0,4},{1,5},{2,6},{3,7},{4,0},{5,1},{6,2},{7,3},{8,12},{9,13},{10,... | collective-permute-start | bytes 589832 | tf_op jit(solution)/shard_map/ppermute | solution.py:33
  68.3 2.5 %collective-permute-start.18 = (bf16[48,2048]{1,0:T(8,128)(2,1)S(1)}, bf16[48,2048]{1,0:T(8,128)(2,1)S(1)}, u32[]{:S(2)}, u32[]{:S(2)}) collective-permute-start(bf16[48,2048]{1,0:T(8,128)(2,1)S(1)} %get-tuple-element.64), channel_id=1, source_target_pairs={{0,6},{1,7},{2,4},{3,5},{4,2},{5,3},{6,0},{7,1},{8,14},{9,15},{10,... | collective-permute-start | bytes 589832 | tf_op jit(solution)/shard_map/ppermute | solution.py:33
  70.8 5.0 %collective-permute-done.14.refs_2_ = bf16[48,2048]{1,0:T(8,128)(2,1)S(1)} collective-permute-done((bf16[48,2048]{1,0:T(8,128)(2,1)S(1)}, bf16[48,2048]{1,0:T(8,128)(2,1)S(1)}, u32[]{:S(2)}, u32[]{:S(2)}) %collective-permute-start.14) | collective-permute-done | bytes 196640 | tf_op jit(solution)/shard_map/ppermute | solution.py:33
  75.7 7.8 %collective-permute-done.16.refs_4_ = bf16[48,2048]{1,0:T(8,128)(2,1)S(1)} collective-permute-done((bf16[48,2048]{1,0:T(8,128)(2,1)S(1)}, bf16[48,2048]{1,0:T(8,128)(2,1)S(1)}, u32[]{:S(2)}, u32[]{:S(2)}) %collective-permute-start.16) | collective-permute-done | bytes 196640 | tf_op jit(solution)/shard_map/ppermute | solution.py:33
  84.3 4.5 %all-to-all-start.2 = ((bf16[8,24,2048]{2,1,0:T(8,128)(2,1)}), bf16[8,24,2048]{2,1,0:T(8,128)(2,1)S(1)}, u32[]{:S(2)}, u32[]{:S(2)}) async-start(bf16[8,24,2048]{2,1,0:T(8,128)(2,1)} %get-tuple-element.69), calls=%async_computation.2 | async-start | bytes 1572864 | tf_op jit(solution)/shard_map/all_to_all | solution.py:467
  90.0 1.7 %collective-permute-start.24 = (bf16[96,2816]{1,0:T(8,128)(2,1)}, bf16[96,2816]{1,0:T(8,128)(2,1)S(1)}, u32[]{:S(2)}, u32[]{:S(2)}) collective-permute-start(bf16[96,2816]{1,0:T(8,128)(2,1)} %slice.13), channel_id=1, source_target_pairs={{0,16},{8,24},{16,0},{24,8},{1,17},{9,25},{17,1},{25,9},{2,18},{10... | collective-permute-start | bytes 1622024 | tf_op jit(solution)/shard_map/ppermute | solution.py:33
  91.7 1.9 %slice.12 = bf16[96,2816]{1,0:T(8,128)(2,1)} slice(bf16[192,2816]{1,0:T(8,128)(2,1)} %collective-permute-done.21.refs_8_), slice={[0:96], [0:2816]} | slice | bytes 1081344 | tf_op jit(solution)/shard_map/slice | solution.py:457
  93.6 1.5 %collective-permute-start.23 = (bf16[96,2816]{1,0:T(8,128)(2,1)}, bf16[96,2816]{1,0:T(8,128)(2,1)}, u32[]{:S(2)}, u32[]{:S(2)}) collective-permute-start(bf16[96,2816]{1,0:T(8,128)(2,1)} %slice.12), channel_id=1, source_target_pairs={{0,8},{8,0},{16,24},{24,16},{1,9},{9,1},{17,25},{25,17},{2,10},{10... | collective-permute-start | bytes 1622024 | tf_op jit(solution)/shard_map/ppermute | solution.py:33
  99.2 9.2 %conditional.3 = (bf16[64,2048]{1,0:T(8,128)(2,1)}) conditional(s32[]{:T(128)} %bitcast, bf16[64,2048]{1,0:T(8,128)(2,1)S(1)} %get-tuple-element.66, bf16[64,2048]{1,0:T(8,128)(2,1)S(1)} %get-tuple-element.66, bf16[64,2048]{1,0:T(8,128)(2,1)S(1)} %get-tuple-element.66), branch_computations={%region_3.0_spmd, %region_4.0_spmd, %region_5.0_spmd} | conditional | bytes 1048624 | solution.py:447
  100.2 8.3 %collective-permute-done.4 = bf16[64,2048]{1,0:T(8,128)(2,1)} collective-permute-done((bf16[64,2048]{1,0:T(8,128)(2,1)S(1)}, bf16[64,2048]{1,0:T(8,128)(2,1)}, u32[]{:S(2)}, u32[]{:S(2)}) %collective-permute-start.4) | collective-permute-done | bytes 262176 | tf_op jit(solution)/shard_map/cond/branch_1_fun/ppermute | solution.py:33
  108.5 4.7 %collective-permute-done.22.refs_9_ = bf16[192,512]{1,0:T(8,128)(2,1)} collective-permute-done((bf16[192,512]{1,0:T(8,128)(2,1)}, bf16[192,512]{1,0:T(8,128)(2,1)}, u32[]{:S(2)}, u32[]{:S(2)}) %collective-permute-start.22) | collective-permute-done | bytes 196640 | tf_op jit(solution)/shard_map/ppermute | solution.py:33
  113.2 6.4 %final.1 = (bf16[128,2048]{1,0:T(8,128)(2,1)}, bf16[128,2048]{1,0:T(8,128)(2,1)}, f32[1,512,768]{2,1,0:T(8,128)}, f32[1,512,768]{2,1,0:T(8,128)}, f32[1,768,512]{2,1,0:T(8,128)}) custom-call(bf16[192,2816]{1,0:T(8,128)(2,1)} %get-tuple-element.58.refs_0_, bf16[192,128]{1,0:T(8,128)(2,1)} %get-tuple-element.59.refs_1_, ...), custom_call_target="tpu_custom_call" | custom-call | flops 1811939328 | bytes 4718592 | tf_op jit(solution)/shard_map/final/pallas_call | solution.py:376
  (52 shorter events, 11.3 us)
Async XLA Ops:
  4.2 36.3 %all-to-all-start = ((bf16[8,24,2048]{2,1,0:T(8,128)(2,1)}), bf16[8,24,2048]{2,1,0:T(8,128)(2,1)S(1)}, u32[]{:S(2)}, u32[]{:S(2)}) async-start(bf16[8,24,2048]{2,1,0:T(8,128)(2,1)} %get-tuple-element.51), calls=%async_computation | async-start | bytes 1572864 | tf_op jit(solution)/shard_map/all_to_all | solution.py:467
  10.6 9.4 %collective-permute-start.1 = (bf16[64,2048]{1,0:T(8,128)(2,1)S(1)}, bf16[64,2048]{1,0:T(8,128)(2,1)}, u32[]{:S(2)}, u32[]{:S(2)}) collective-permute-start(bf16[64,2048]{1,0:T(8,128)(2,1)S(1)} %param.1), channel_id=1, source_target_pairs={{0,16},{8,24},{16,0},{24,8},{1,17},{9,25},{17,1},{25,9},{2,18},{10... | collective-permute-start | bytes 786440 | tf_op jit(solution)/shard_map/cond/branch_1_fun/ppermute | solution.py:33
  21.3 20.2 %collective-permute-start.11 = (bf16[48,2048]{1,0:T(8,128)(2,1)S(1)}, bf16[48,2048]{1,0:T(8,128)(2,1)S(1)}, u32[]{:S(2)}, u32[]{:S(2)}) collective-permute-start(bf16[48,2048]{1,0:T(8,128)(2,1)S(1)} %get-tuple-element.56), channel_id=1, source_target_pairs={{0,6},{1,7},{2,4},{3,5},{4,2},{5,3},{6,0},{7,1},{8,14},{9,15},{10,... | collective-permute-start | bytes 589832 | tf_op jit(solution)/shard_map/ppermute | solution.py:33
  24.4 24.1 %collective-permute-start.9 = (bf16[48,2048]{1,0:T(8,128)(2,1)S(1)}, bf16[48,2048]{1,0:T(8,128)(2,1)S(1)}, u32[]{:S(2)}, u32[]{:S(2)}) collective-permute-start(bf16[48,2048]{1,0:T(8,128)(2,1)S(1)} %get-tuple-element.54), channel_id=1, source_target_pairs={{0,4},{1,5},{2,6},{3,7},{4,0},{5,1},{6,2},{7,3},{8,12},{9,13},{10,... | collective-permute-start | bytes 589832 | tf_op jit(solution)/shard_map/ppermute | solution.py:33
  24.4 24.1 %collective-permute-start.7 = (bf16[48,2048]{1,0:T(8,128)(2,1)S(1)}, bf16[48,2048]{1,0:T(8,128)(2,1)S(1)}, u32[]{:S(2)}, u32[]{:S(2)}) collective-permute-start(bf16[48,2048]{1,0:T(8,128)(2,1)S(1)} %get-tuple-element.50), channel_id=1, source_target_pairs={{0,2},{1,3},{2,0},{3,1},{4,6},{5,7},{6,4},{7,5},{8,10},{9,11},{10,... | collective-permute-start | bytes 589832 | tf_op jit(solution)/shard_map/ppermute | solution.py:33
  25.7 26.9 %collective-permute-start.6 = (bf16[48,2048]{1,0:T(8,128)(2,1)S(1)}, bf16[48,2048]{1,0:T(8,128)(2,1)S(1)}, u32[]{:S(2)}, u32[]{:S(2)}) collective-permute-start(bf16[48,2048]{1,0:T(8,128)(2,1)S(1)} %get-tuple-element.49.refs_0_), channel_id=1, source_target_pairs={{0,1},{1,0},{2,3},{3,2},{4,5},{5,4},{6,7},{7,6},{8,9},{9,8},{10,11... | collective-permute-start | bytes 589832 | tf_op jit(solution)/shard_map/ppermute | solution.py:33
  48.4 4.2 %collective-permute-start.8 = (bf16[48,2048]{1,0:T(8,128)(2,1)S(1)}, bf16[48,2048]{1,0:T(8,128)(2,1)S(1)}, u32[]{:S(2)}, u32[]{:S(2)}) collective-permute-start(bf16[48,2048]{1,0:T(8,128)(2,1)S(1)} %collective-permute-done.7.refs_2_), channel_id=1, source_target_pairs={{0,1},{1,0},{2,3},{3,2},{4,5},{5,4},{6,7},{7,6},{8,9},{9,8},{10,11... | collective-permute-start | bytes 589832 | tf_op jit(solution)/shard_map/ppermute | solution.py:33
  48.4 4.2 %collective-permute-start.10 = (bf16[48,2048]{1,0:T(8,128)(2,1)S(1)}, bf16[48,2048]{1,0:T(8,128)(2,1)S(1)}, u32[]{:S(2)}, u32[]{:S(2)}) collective-permute-start(bf16[48,2048]{1,0:T(8,128)(2,1)S(1)} %collective-permute-done.9.refs_4_), channel_id=1, source_target_pairs={{0,1},{1,0},{2,3},{3,2},{4,5},{5,4},{6,7},{7,6},{8,9},{9,8},{10,11... | collective-permute-start | bytes 589832 | tf_op jit(solution)/shard_map/ppermute | solution.py:33
  49.0 3.7 %collective-permute-start.12 = (bf16[48,2048]{1,0:T(8,128)(2,1)S(1)}, bf16[48,2048]{1,0:T(8,128)(2,1)S(1)}, u32[]{:S(2)}, u32[]{:S(2)}) collective-permute-start(bf16[48,2048]{1,0:T(8,128)(2,1)S(1)} %collective-permute-done.11.refs_6_), channel_id=1, source_target_pairs={{0,1},{1,0},{2,3},{3,2},{4,5},{5,4},{6,7},{7,6},{8,9},{9,8},{10,11... | collective-permute-start | bytes 589832 | tf_op jit(solution)/shard_map/ppermute | solution.py:33
  49.0 34.6 %all-to-all-start.1 = ((bf16[4,192,512]{2,1,0:T(8,128)(2,1)}), bf16[4,192,512]{2,1,0:T(8,128)(2,1)S(1)}, u32[]{:S(2)}, u32[]{:S(2)}) async-start(bf16[4,192,512]{2,1,0:T(8,128)(2,1)} %get-tuple-element.68), calls=%async_computation.1 | async-start | bytes 1572864 | tf_op jit(solution)/shard_map/all_to_all | solution.py:467
  62.8 26.3 %collective-permute-start.20 = (bf16[192,2816]{1,0:T(8,128)(2,1)}, bf16[192,2816]{1,0:T(8,128)(2,1)S(1)}, u32[]{:S(2)}, u32[]{:S(2)}) collective-permute-start(bf16[192,2816]{1,0:T(8,128)(2,1)} %get-tuple-element.70), channel_id=1, source_target_pairs={{0,8},{8,0},{16,24},{24,16},{1,9},{9,1},{17,25},{25,17},{2,10},{10... | collective-permute-start | bytes 3244040 | tf_op jit(solution)/shard_map/ppermute | solution.py:33
  64.9 26.8 %collective-permute-start.21 = (bf16[192,2816]{1,0:T(8,128)(2,1)}, bf16[192,2816]{1,0:T(8,128)(2,1)}, u32[]{:S(2)}, u32[]{:S(2)}) collective-permute-start(bf16[192,2816]{1,0:T(8,128)(2,1)} %get-tuple-element.71), channel_id=1, source_target_pairs={{0,16},{8,24},{16,0},{24,8},{1,17},{9,25},{17,1},{25,9},{2,18},{10... | collective-permute-start | bytes 3244040 | tf_op jit(solution)/shard_map/ppermute | solution.py:33
  66.4 9.3 %collective-permute-start.14 = (bf16[48,2048]{1,0:T(8,128)(2,1)S(1)}, bf16[48,2048]{1,0:T(8,128)(2,1)S(1)}, u32[]{:S(2)}, u32[]{:S(2)}) collective-permute-start(bf16[48,2048]{1,0:T(8,128)(2,1)S(1)} %get-tuple-element.62), channel_id=1, source_target_pairs={{0,2},{1,3},{2,0},{3,1},{4,6},{5,7},{6,4},{7,5},{8,10},{9,11},{10,... | collective-permute-start | bytes 589832 | tf_op jit(solution)/shard_map/ppermute | solution.py:33
  66.4 17.1 %collective-permute-start.16 = (bf16[48,2048]{1,0:T(8,128)(2,1)S(1)}, bf16[48,2048]{1,0:T(8,128)(2,1)S(1)}, u32[]{:S(2)}, u32[]{:S(2)}) collective-permute-start(bf16[48,2048]{1,0:T(8,128)(2,1)S(1)} %get-tuple-element.63), channel_id=1, source_target_pairs={{0,4},{1,5},{2,6},{3,7},{4,0},{5,1},{6,2},{7,3},{8,12},{9,13},{10,... | collective-permute-start | bytes 589832 | tf_op jit(solution)/shard_map/ppermute | solution.py:33
  68.3 15.2 %collective-permute-start.18 = (bf16[48,2048]{1,0:T(8,128)(2,1)S(1)}, bf16[48,2048]{1,0:T(8,128)(2,1)S(1)}, u32[]{:S(2)}, u32[]{:S(2)}) collective-permute-start(bf16[48,2048]{1,0:T(8,128)(2,1)S(1)} %get-tuple-element.64), channel_id=1, source_target_pairs={{0,6},{1,7},{2,4},{3,5},{4,2},{5,3},{6,0},{7,1},{8,14},{9,15},{10,... | collective-permute-start | bytes 589832 | tf_op jit(solution)/shard_map/ppermute | solution.py:33
  84.3 28.9 %all-to-all-start.2 = ((bf16[8,24,2048]{2,1,0:T(8,128)(2,1)}), bf16[8,24,2048]{2,1,0:T(8,128)(2,1)S(1)}, u32[]{:S(2)}, u32[]{:S(2)}) async-start(bf16[8,24,2048]{2,1,0:T(8,128)(2,1)} %get-tuple-element.69), calls=%async_computation.2 | async-start | bytes 1572864 | tf_op jit(solution)/shard_map/all_to_all | solution.py:467
  90.0 23.2 %collective-permute-start.24 = (bf16[96,2816]{1,0:T(8,128)(2,1)}, bf16[96,2816]{1,0:T(8,128)(2,1)S(1)}, u32[]{:S(2)}, u32[]{:S(2)}) collective-permute-start(bf16[96,2816]{1,0:T(8,128)(2,1)} %slice.13), channel_id=1, source_target_pairs={{0,16},{8,24},{16,0},{24,8},{1,17},{9,25},{17,1},{25,9},{2,18},{10... | collective-permute-start | bytes 1622024 | tf_op jit(solution)/shard_map/ppermute | solution.py:33
  93.6 19.6 %collective-permute-start.23 = (bf16[96,2816]{1,0:T(8,128)(2,1)}, bf16[96,2816]{1,0:T(8,128)(2,1)}, u32[]{:S(2)}, u32[]{:S(2)}) collective-permute-start(bf16[96,2816]{1,0:T(8,128)(2,1)} %slice.12), channel_id=1, source_target_pairs={{0,8},{8,0},{16,24},{24,16},{1,9},{9,1},{17,25},{25,17},{2,10},{10... | collective-permute-start | bytes 1622024 | tf_op jit(solution)/shard_map/ppermute | solution.py:33
  95.1 1.4 %collective-permute-start.13 = (bf16[48,2048]{1,0:T(8,128)(2,1)S(1)}, bf16[48,2048]{1,0:T(8,128)(2,1)S(1)}, u32[]{:S(2)}, u32[]{:S(2)}) collective-permute-start(bf16[48,2048]{1,0:T(8,128)(2,1)S(1)} %get-tuple-element.61.refs_0_), channel_id=1, source_target_pairs={{0,1},{1,0},{2,3},{3,2},{4,5},{5,4},{6,7},{7,6},{8,9},{9,8},{10,11... | collective-permute-start | bytes 589832 | tf_op jit(solution)/shard_map/ppermute | solution.py:33
  95.1 1.7 %collective-permute-start.15 = (bf16[48,2048]{1,0:T(8,128)(2,1)S(1)}, bf16[48,2048]{1,0:T(8,128)(2,1)S(1)}, u32[]{:S(2)}, u32[]{:S(2)}) collective-permute-start(bf16[48,2048]{1,0:T(8,128)(2,1)S(1)} %copy-done.3), channel_id=1, source_target_pairs={{0,1},{1,0},{2,3},{3,2},{4,5},{5,4},{6,7},{7,6},{8,9},{9,8},{10,11... | collective-permute-start | bytes 589832 | tf_op jit(solution)/shard_map/ppermute | solution.py:33
  95.6 1.7 %collective-permute-start.17 = (bf16[48,2048]{1,0:T(8,128)(2,1)S(1)}, bf16[48,2048]{1,0:T(8,128)(2,1)S(1)}, u32[]{:S(2)}, u32[]{:S(2)}) collective-permute-start(bf16[48,2048]{1,0:T(8,128)(2,1)S(1)} %copy-done.5), channel_id=1, source_target_pairs={{0,1},{1,0},{2,3},{3,2},{4,5},{5,4},{6,7},{7,6},{8,9},{9,8},{10,11... | collective-permute-start | bytes 589832 | tf_op jit(solution)/shard_map/ppermute | solution.py:33
  96.5 1.4 %collective-permute-start.19 = (bf16[48,2048]{1,0:T(8,128)(2,1)S(1)}, bf16[48,2048]{1,0:T(8,128)(2,1)S(1)}, u32[]{:S(2)}, u32[]{:S(2)}) collective-permute-start(bf16[48,2048]{1,0:T(8,128)(2,1)S(1)} %copy-done.7), channel_id=1, source_target_pairs={{0,1},{1,0},{2,3},{3,2},{4,5},{5,4},{6,7},{7,6},{8,9},{9,8},{10,11... | collective-permute-start | bytes 589832 | tf_op jit(solution)/shard_map/ppermute | solution.py:33
  96.8 16.4 %collective-permute-start.22 = (bf16[192,512]{1,0:T(8,128)(2,1)}, bf16[192,512]{1,0:T(8,128)(2,1)}, u32[]{:S(2)}, u32[]{:S(2)}) collective-permute-start(bf16[192,512]{1,0:T(8,128)(2,1)} %get-tuple-element.72), channel_id=1, source_target_pairs={{0,24},{8,16},{16,8},{24,0},{1,25},{9,17},{17,9},{25,1},{2,26},{10... | collective-permute-start | bytes 589832 | tf_op jit(solution)/shard_map/ppermute | solution.py:33
  99.2 9.2 %collective-permute-start.4 = (bf16[64,2048]{1,0:T(8,128)(2,1)S(1)}, bf16[64,2048]{1,0:T(8,128)(2,1)}, u32[]{:S(2)}, u32[]{:S(2)}) collective-permute-start(bf16[64,2048]{1,0:T(8,128)(2,1)S(1)} %param.4), channel_id=1, source_target_pairs={{0,16},{8,24},{16,0},{24,8},{1,17},{9,25},{17,1},{25,9},{2,18},{10... | collective-permute-start | bytes 786440 | tf_op jit(solution)/shard_map/cond/branch_1_fun/ppermute | solution.py:33
  (9 other events, 73.3 us)

commit v4 on v3

--- a/solution.py
+++ b/solution.py
@@ -57,22 +57,20 @@
 def prepare_kernel(sizes, *refs):
     window, capacity, tok_dev, slot_len = sizes
     sources, outs, held = refs[:6], refs[6:12], refs[12:18]
-    high_held, fine_held, sems = refs[18:]
+    high_held, fine_held, weighted_held, sems, out_sems = refs[18:]
     copies = [
         pltpu.make_async_copy(source, place, sems.at[i])
         for i, (source, place) in enumerate(zip(sources, held))
     ]
-    for copy in copies:
-        copy.start()
-    for copy in copies:
-        copy.wait()
+    for i in (0, 1, 2, 5, 3, 4):
+        copies[i].start()
     rows_ref, gates_ref, counts_ref, lengths_ref, tok_ref, cot_ref = held
     moved_ref, low_ref, weighted_ref, hit_ref, high_ref, fine_ref = outs
     me = lax.axis_index("expert")
     half = tok_dev // 2
-    lengths = lengths_ref[...]
-    moved_ref[...] = keep_valid(tok_ref[half:, :], lengths, half // slot_len, slot_len)
-    low_ref[...] = keep_valid(tok_ref[:half, :], lengths, 0, slot_len)
+    pair = 2 * capacity
+    for i in (0, 1, 2, 5):
+        copies[i].wait()
 
     def gate_of(e):
         slot = lax.broadcasted_iota(jnp.int32, (1, capacity), 1)
@@ -84,22 +82,37 @@
     gate = table_columns(gate_of, order)
     index = table_columns(lambda e: rows_ref[0, pl.ds(e, 1), :], order).astype(jnp.int32)
     hit = lax.broadcasted_iota(jnp.int32, (window * capacity, tok_dev), 1) == index
+    picked = jnp.dot(hit.astype(BF16), cot_ref[...], preferred_element_type=F32)
+    weighted = gate * picked
+    swapped_cores = me % 2 == 1
+    for z in range(window // 2):
+        one = weighted[z * pair : z * pair + capacity]
+        other = weighted[z * pair + capacity : (z + 1) * pair]
+        block = jnp.where(
+            swapped_cores,
+            jnp.concatenate([other, one], axis=0),
+            jnp.concatenate([one, other], axis=0),
+        )
+        weighted_held[(me // 2) ^ z] = block.astype(BF16)
     hit_ref[...] = hit.astype(BF16)
     table = jnp.where(hit, jnp.broadcast_to(gate, hit.shape), 0.0)
     high = table.astype(BF16)
     high_held[...] = high
     fine_held[...] = (table - high.astype(F32)).astype(BF16)
-    copies = [
-        pltpu.make_async_copy(high_held, high_ref, sems.at[0]),
-        pltpu.make_async_copy(fine_held, fine_ref, sems.at[1]),
-    ]
-    for copy in copies:
+    stores = [
+        pltpu.make_async_copy(a, b, out_sems.at[i])
+        for i, (a, b) in enumerate(
+            ((weighted_held, weighted_ref), (high_held, high_ref), (fine_held, fine_ref))
+        )
+    ]
+    for copy in stores:
         copy.start()
-    picked = jnp.dot(hit.astype(BF16), cot_ref[...], preferred_element_type=F32)
-    weighted = gate * picked
-    for d, e in enumerate(order):
-        weighted_ref[e] = weighted[d * capacity : (d + 1) * capacity].astype(BF16)
-    for copy in copies:
+    for i in (3, 4):
+        copies[i].wait()
+    lengths = lengths_ref[...]
+    moved_ref[...] = keep_valid(tok_ref[half:, :], lengths, half // slot_len, slot_len)
+    low_ref[...] = keep_valid(tok_ref[:half, :], lengths, 0, slot_len)
+    for copy in stores:
         copy.wait()
 
 
@@ -115,16 +128,19 @@
         out_shape=[
             jax.ShapeDtypeStruct((half, width), BF16),
             jax.ShapeDtypeStruct((half, width), BF16),
-            jax.ShapeDtypeStruct((window, capacity, width), BF16),
+            pltpu.HBM((window // 2, 2 * capacity, width), BF16),
             table,
             pltpu.HBM(table.shape, table.dtype),
             pltpu.HBM(table.shape, table.dtype),
         ],
         in_specs=[pl.BlockSpec(memory_space=pltpu.HBM)] * len(sources),
-        out_specs=[WHOLE] * 4 + [pl.BlockSpec(memory_space=pltpu.HBM)] * 2,
+        out_specs=[WHOLE] * 2
+        + [pl.BlockSpec(memory_space=pltpu.HBM), WHOLE]
+        + [pl.BlockSpec(memory_space=pltpu.HBM)] * 2,
         scratch_shapes=[VMEM(a.shape, a.dtype) for a in sources]
         + [VMEM(table.shape, BF16)] * 2
-        + [pltpu.SemaphoreType.DMA((len(sources),))],
+        + [VMEM((window // 2, 2 * capacity, width), BF16)]
+        + [pltpu.SemaphoreType.DMA((len(sources),)), pltpu.SemaphoreType.DMA((3,))],
         compiler_params=params(12),
         cost_estimate=cost(2 * window * capacity * tok_dev * width, 5 * tok_dev * width),
         name="prepare",
@@ -160,8 +176,10 @@
 
 def share_columns(rows, outs):
     me = lax.axis_index("dp")
-    share = outs[0].shape[1]
+    share = outs[1].shape[1]
     for j, out in enumerate(outs):
+        if out is None:
+            continue
         out[...] = rows[:, pl.ds(pl.multiple_of((me ^ j) * share, share), share)]
 
 
@@ -200,11 +218,16 @@
     x_refs, w_ref, weights = refs[: 2 * count], refs[2 * count], refs[2 * count + 1 : 2 * count + 4]
     tok_refs = refs[2 * count + 4 : 3 * count + 4]
     out_ref, sent_refs = refs[3 * count + 4], refs[3 * count + 5 : 3 * count + 5 + replicas]
-    x_all, hid_all, gg_all, gu_all, pre_gate, grad_hidden, own_held, *held, sems = refs[
+    x_all, hid_all, gg_all, gu_all, pre_gate, grad_hidden, *held, sems = refs[
         3 * count + 5 + replicas :
     ]
-    own_copy = pltpu.make_async_copy(own_held, sent_refs[0], sems.at[3, 0])
-    sent_refs = [own_held, *sent_refs[1:]]
+    wide_count = sum(ref.shape[1] > sent_refs[0].shape[1] for ref in sent_refs)
+    sent_held, held = held[3:], held[:3]
+    sent_copies = [
+        pltpu.make_async_copy(a, b, sems.at[3, 1 + i])
+        for i, (a, b) in enumerate(zip(sent_held, sent_refs[1 : 1 + wide_count]))
+    ]
+    sent_refs = [sent_refs[0], *sent_held, *sent_refs[1 + wide_count :]]
     gate_ref, up_ref, down_ref = held
     copies = []
     for i, (source, place) in enumerate(zip(weights, held)):
@@ -225,7 +248,10 @@
     turned = (((1,), (1,)), ((), ()))
     for z in range(count):
         x_all[z * pair : (z + 1) * pair, :] = joined(x_refs[2 * z], x_refs[2 * z + 1], capacity)
-    share_columns(x_all, [s.at[:, s.shape[1] - share :] for s in sent_refs])
+    own = pl.ds(pl.multiple_of(lax.axis_index("dp") * share, share), share)
+    own_copy = pltpu.make_async_copy(x_all.at[:, own], sent_refs[0], sems.at[3, 0])
+    own_copy.start()
+    share_columns(x_all, [None] + [s.at[:, s.shape[1] - share :] for s in sent_refs[1:]])
     spans = [slice(f * tile, (f + 1) * tile) for f in range(hid_all.shape[1] // tile)]
     for copy in copies[0]:
         copy.wait()
@@ -249,11 +275,12 @@
         hid_all[:, span] = (silu * pre_up).astype(BF16)
         gg_all[:, span] = (grad * pre_up * sig * (1.0 + gate * (1.0 - sig))).astype(BF16)
         gu_all[:, span] = (grad * silu).astype(BF16)
-        for sent in sent_refs:
+        for sent in sent_refs[1:]:
             if sent.shape[1] > share:
                 for k, source in enumerate((hid_all, gg_all, gu_all)):
                     sent[:, (3 * f + k) * tile : (3 * f + k + 1) * tile] = source[:, span]
-    own_copy.start()
+    for copy in sent_copies:
+        copy.start()
     wide = 2 * tile
     for n in range(width // wide):
         span = slice(n * wide, (n + 1) * wide)
@@ -262,11 +289,20 @@
         ) + lax.dot_general(gu_all[...], up_ref[0, span, :], turned, preferred_element_type=F32)
         tok = tok.astype(BF16)
         out = jnp.dot(hid_all[...], down_ref[0, :, span], preferred_element_type=F32)
+        swapped_cores = me % 2 == 1
         for z in range(count):
             tok_refs[z][:, span] = tok[z * pair : (z + 1) * pair]
-        for d in range(2 * count):
-            out_ref[me ^ d, :, span] = out[d * capacity : (d + 1) * capacity].astype(BF16)
-    own_copy.wait()
+        for z in range(count):
+            one = out[z * pair : z * pair + capacity]
+            other = out[z * pair + capacity : (z + 1) * pair]
+            block = jnp.where(
+                swapped_cores,
+                jnp.concatenate([other, one], axis=0),
+                jnp.concatenate([one, other], axis=0),
+            )
+            out_ref[(me // 2) ^ z, :, span] = block.astype(BF16)
+    for copy in [own_copy, *sent_copies]:
+        copy.wait()
 
 
 def expert(x_pairs, w_rows, w_gate, w_up, w_down, capacity):
@@ -281,57 +317,62 @@
     sent = [jax.ShapeDtypeStruct((rows, 3 * hidden_units + share), BF16)] * replicas
     if replicas == 4:
         sent[3] = jax.ShapeDtypeStruct((rows, share), BF16)
-    sent[0] = pltpu.HBM(sent[0].shape, sent[0].dtype)
+    sent[0] = pltpu.HBM((rows, share), BF16)
+    large = [a for a in sent[1:] if a.shape[1] > share]
+    sent[1 : 1 + len(large)] = [pltpu.HBM(a.shape, BF16) for a in large]
     results = pl.pallas_call(
         functools.partial(expert_kernel, (count, capacity, TILE, replicas)),
         out_shape=[block] * count
-        + [jax.ShapeDtypeStruct((2 * count, capacity, width), BF16)]
+        + [jax.ShapeDtypeStruct((count, pair, width), BF16)]
         + sent,
         in_specs=[WHOLE] * (2 * count + 1) + [pl.BlockSpec(memory_space=pltpu.HBM)] * 3,
         out_specs=[WHOLE] * (count + 1)
-        + [pl.BlockSpec(memory_space=pltpu.HBM)]
-        + [WHOLE] * (replicas - 1),
+        + [pl.BlockSpec(memory_space=pltpu.HBM)] * (1 + len(large))
+        + [WHOLE] * (replicas - 1 - len(large)),
         scratch_shapes=[VMEM((rows, width), BF16)]
         + [VMEM((rows, hidden_units), BF16)] * 3
         + [VMEM((rows, hidden_units), F32)] * 2
-        + [VMEM(sent[0].shape, BF16)]
-        + [VMEM(a.shape, BF16) for a in (w_gate, w_up, w_down)]
-        + [pltpu.SemaphoreType.DMA((4, PIECES))],
+        + [VMEM(a.shape, BF16) for a in (w_gate, w_up, w_down, *large)]
+        + [pltpu.SemaphoreType.DMA((4, max(PIECES, 1 + len(large))))],
         compiler_params=params(32 if replicas <= 4 else 56),
         cost_estimate=cost(
             12 * rows * width * hidden_units, 6 * width * hidden_units + 10 * rows * width
         ),
         name="expert",
     )(*flat, w_rows, *in_hbm(w_gate, w_up, w_down))
-    return results[:count], results[count], results[count + 1 :]
+    return (
+        results[:count],
+        results[count].reshape(2 * count, capacity, width),
+        results[count + 1 :],
+    )
 
 
 def final_kernel(sizes, *refs):
     share, tile, parts = sizes
-    loads, refs = list(refs[:3]), refs[3:]
-    low_ref, arrived_ref, back_ref, w_ref, refs = *refs[:4], refs[4:]
-    others, outs, scratch = refs[:-14], refs[-14:-9], refs[-9:]
-    own_held, high_ref, fine_ref, out_held, *held, sems, side_sems = scratch
+    loads, refs = list(refs[:4]), refs[4:]
+    back_ref, low_ref, arrived_ref, w_ref, refs = *refs[:4], refs[4:]
+    sources, outs, scratch = refs[:-15], refs[-15:-10], refs[-10:]
+    own_share, own_acts, high_ref, fine_ref, out_held, *held, sems, side_sems = scratch
     loads = [
         pltpu.make_async_copy(a, b, side_sems.at[i])
-        for i, (a, b) in enumerate(zip(loads, (own_held, high_ref, fine_ref)))
+        for i, (a, b) in enumerate(zip(loads, (own_share, own_acts, high_ref, fine_ref)))
     ]
     half = low_ref.shape[0]
     stores = [
-        pltpu.make_async_copy(low_ref, outs[1].at[:half], side_sems.at[3]),
-        pltpu.make_async_copy(arrived_ref, outs[1].at[half:], side_sems.at[4]),
+        pltpu.make_async_copy(low_ref, outs[1].at[:half], side_sems.at[4]),
+        pltpu.make_async_copy(arrived_ref, outs[1].at[half:], side_sems.at[5]),
     ]
     for copy in loads + stores:
         copy.start()
-    for copy in loads:
-        copy.wait()
+    for copy in loads[:2]:
+        copy.wait()
+    sources = [own_share, *sources]
     me = lax.axis_index("dp")
-    sources = [own_held, *others]
-    acts_width = sources[0].shape[1] - share
+    acts_width = own_acts.shape[1] - share
     across = (((0,), (0,)), ((), ()))
     x = jnp.concatenate([r[:, r.shape[1] - share :] for r in sources[:parts]], axis=0)
     w = jnp.concatenate([w_ref[me ^ j] for j in range(parts)], axis=0)
-    acts = [r for r in sources if r.shape[1] > share]
+    acts = [own_acts] + [r for r in sources if r.shape[1] > share]
     for f in range(acts_width // (3 * tile)):
         hidden, grad_gate, grad_up = [
             jnp.concatenate(
@@ -353,6 +394,8 @@
             copy = pltpu.make_async_copy(a, b, sems.at[f, i])
             copy.start()
             stores.append(copy)
+    for copy in loads[2:]:
+        copy.wait()
     expert_id = lax.axis_index("expert")
     rows = jnp.concatenate(
         [back_ref[expert_id ^ d].astype(F32) for d in range(back_ref.shape[0])], axis=0
@@ -360,16 +403,16 @@
     total = lax.dot_general(high_ref[...], rows, across, preferred_element_type=F32)
     total += lax.dot_general(fine_ref[...], rows, across, preferred_element_type=F32)
     out_held[...] = total.astype(BF16)
-    stores.append(pltpu.make_async_copy(out_held, outs[0], side_sems.at[5]))
+    stores.append(pltpu.make_async_copy(out_held, outs[0], side_sems.at[6]))
     stores[-1].start()
     for copy in stores:
         copy.wait()
 
 
-def final(high, fine, back, low, arrived, w_shares, received):
+def final(high, fine, back, low, arrived, w_shares, own_acts, received):
     parts, rows, share = w_shares.shape
     half, width = low.shape
-    hidden_units = (received[0].shape[1] - share) // 3
+    hidden_units = (own_acts.shape[1] - share) // 3
     tile = TILE
     tiles = hidden_units // tile
     hbm = pl.BlockSpec(memory_space=pltpu.HBM)
@@ -382,10 +425,11 @@
             jax.ShapeDtypeStruct((1, share, hidden_units), F32),
             jax.ShapeDtypeStruct((1, hidden_units, share), F32),
         ],
-        in_specs=[hbm] * 3 + [WHOLE] * (3 + len(received)),
+        in_specs=[hbm] * 4 + [WHOLE] * (3 + len(received)),
         out_specs=[hbm] * 5,
         scratch_shapes=[
             VMEM(received[0].shape, BF16),
+            VMEM(own_acts.shape, BF16),
             VMEM(high.shape, BF16),
             VMEM(fine.shape, BF16),
             VMEM((2 * half, width), BF16),
@@ -393,12 +437,12 @@
             VMEM((tiles, share, tile), F32),
             VMEM((tiles, tile, share), F32),
             pltpu.SemaphoreType.DMA((tiles, 3)),
-            pltpu.SemaphoreType.DMA((6,)),
+            pltpu.SemaphoreType.DMA((7,)),
         ],
         compiler_params=params(24 if parts <= 4 else 60),
         cost_estimate=cost(6 * parts * rows * share * hidden_units, 12 * share * hidden_units),
         name="final",
-    )(*in_hbm(received[0], high, fine), low, arrived, back, w_shares, *received[1:])
+    )(*in_hbm(received[0], own_acts, high, fine), back, low, arrived, w_shares, *received[1:])
 
 
 def grads_kernel(capacity, hit_ref, *refs):
@@ -450,10 +494,11 @@
 def spread_acts(sent):
     if lax.axis_size("dp") != 4:
         return [sent[0]] + [xor_permute(sent[j], "dp", j) for j in range(1, len(sent))], []
-    half = sent[0].shape[0] // 2
+    acts = sent[1].shape[1] - sent[3].shape[1]
     near = xor_permute(sent[1], "dp", 1)
     side = xor_permute(sent[2], "dp", 2)
     far = xor_permute(sent[3], "dp", 3)
+    half = side.shape[0] // 2
     passed = [side[:half], near[half:]]
     halves = [xor_permute(passed[0], "dp", 1), xor_permute(passed[1], "dp", 2)]
     return [sent[0], near, side, far, *halves], passed
@@ -484,6 +529,7 @@
     moved, low, weighted, hit, high, fine = prepare(
         slot_rows, slot_gates, slot_counts, seq_lengths, tokens, cotangent
     )
+    weighted = weighted.reshape(slot_rows.shape[1], capacity, tokens.shape[1])
     weighted = all_to_all(weighted, "expert")
     picked = pick(hit, low, swapped(moved, key), capacity)
     x_direct = send_chips(picked)
@@ -496,7 +542,9 @@
     back = all_to_all(after(expert_out, w_shares, *[p[0] for p in tok_pairs]), "expert")
     low_grads, high_grads = combine_grads(hit, tok_pairs, capacity)
     return tuple(
-        final(high, fine, back, low_grads, swapped(high_grads, key), w_shares, received)
+        final(
+            high, fine, back, low_grads, swapped(high_grads, key), w_shares, sent[1], received
+        )
     )
 
 

time: 121 us -> 122 us (level)
  waiting for transfers between devices: 57.4 us -> 61.1 us
  Pallas kernels: 22.7 us -> 20.6 us
    ppermute x21, waiting for transfers between devices: 42.6 us -> 46.3 us  [xor_permute(): return lax.ppermute(array, axis, [(i, i ^ key) for i in range(size)])]
    pallas_call x1, Pallas kernels: 10.1 us -> 8.84 us  [expert(): pl.pallas_call(functools.partial(expert_kernel, (count, capacity, TILE, r...]
  transfers between devices with their start and end apart: 24 -> 24, of which waited for: 11 -> 10; matrix products, arithmetic and copies ran while one was open for 2% -> 2% of each run, Pallas kernels for 11% -> 9%
where the time goes in v4:
time: 122 us; the launch traced here: 121 us
  waiting for transfers between devices  61.1 us (50%)
  starting transfers between devices  34.3 us (28%)
  Pallas kernels  20.6 us (17%)
  local copies, waits for them, and re-layouts  4.39 us (4%)
    ppermute x21, waiting for transfers between devices, xor_permute(): return lax.ppermute(array, axis, [(i, i ^ key) for i in range(size)])  46.3 us
    ppermute x21, starting transfers between devices, xor_permute(): return lax.ppermute(array, axis, [(i, i ^ key) for i in range(size)])  19.7 us
    all_to_all x3, waiting for transfers between devices, all_to_all(): return lax.all_to_all(array, axis, split_axis=0, concat_axis=0, tiled=True)  14.7 us
    all_to_all x3, starting transfers between devices, all_to_all(): return lax.all_to_all(array, axis, split_axis=0, concat_axis=0, tiled=True)  14.5 us
    pallas_call x1, Pallas kernels, expert(): pl.pallas_call(functools.partial(expert_kernel, (count, capacity, TILE, r...  8.84 us
    pallas_call x1, Pallas kernels, final(): pl.pallas_call(functools.partial(final_kernel, (share, tile, parts)), out...  6.48 us
    slice x2, local copies, waits for them, and re-layouts, spread_acts(): passed = [side[:half], near[half:]]  2.71 us
    pallas_call x1, Pallas kernels, prepare(): pl.pallas_call(functools.partial(prepare_kernel, (window, capacity, tok_d...  2.69 us
  transfers between devices with their start and end apart: 24, of which 10 were waited for; matrix products, arithmetic and copies ran while one was open for 2% of the time, Pallas kernels for 9%

profile of v4, /device:TPU:0, one launch (start us, length us, event | category | flops | bytes accessed | tf_op | source)
XLA Modules:
  0.0 121.2 jit_solution(14687488630840562812)
XLA Ops:
  0.6 2.7 %prepare.1 = (bf16[64,2048]{1,0:T(8,128)(2,1)S(1)}, bf16[64,2048]{1,0:T(8,128)(2,1)S(1)}, bf16[4,48,2048]{2,1,0:T(8,128)(2,1)}, bf16[192,128]{1,0:T(8,128)(2,1)S...) custom-call(s32[1,8,24]{2,1,0:T(8,128)} %refs_0_.1, f32[1,8,24]{2,1,0:T(8,128)} %refs_1_.1, s32[1,8]{1,0:T(1,128)} %refs_2_.1, ...), custom_call_target="tpu_custom_call" | custom-call | flops 100663296 | bytes 1310720 | tf_op jit(solution)/shard_map/prepare/pallas_call | solution.py:126
  3.3 6.3 %all-to-all-start = ((bf16[8,24,2048]{2,1,0:T(8,128)(2,1)}), bf16[8,24,2048]{2,1,0:T(8,128)(2,1)S(1)}, u32[]{:S(2)}, u32[]{:S(2)}) async-start(bf16[8,24,2048]{2,1,0:T(8,128)(2,1)} %bitcast.4), calls=%async_computation | async-start | bytes 1572864 | tf_op jit(solution)/shard_map/all_to_all | solution.py:512
  9.7 9.4 %conditional.2 = (bf16[64,2048]{1,0:T(8,128)(2,1)}) conditional(s32[]{:T(128)} %bitcast, bf16[64,2048]{1,0:T(8,128)(2,1)S(1)} %get-tuple-element.48, bf16[64,2048]{1,0:T(8,128)(2,1)S(1)} %get-tuple-element.48, bf16[64,2048]{1,0:T(8,128)(2,1)S(1)} %get-tuple-element.48), branch_computations={%region_0.0_spmd, %region_1.0_spmd, %region_2.0_spmd} | conditional | bytes 1048624 | solution.py:491
  9.7 1.6 %collective-permute-start.1 = (bf16[64,2048]{1,0:T(8,128)(2,1)S(1)}, bf16[64,2048]{1,0:T(8,128)(2,1)}, u32[]{:S(2)}, u32[]{:S(2)}) collective-permute-start(bf16[64,2048]{1,0:T(8,128)(2,1)S(1)} %param.1), channel_id=1, source_target_pairs={{0,16},{8,24},{16,0},{24,8},{1,17},{9,25},{17,1},{25,9},{2,18},{10... | collective-permute-start | bytes 786440 | tf_op jit(solution)/shard_map/cond/branch_1_fun/ppermute | solution.py:33
  11.3 7.8 %collective-permute-done.1 = bf16[64,2048]{1,0:T(8,128)(2,1)} collective-permute-done((bf16[64,2048]{1,0:T(8,128)(2,1)S(1)}, bf16[64,2048]{1,0:T(8,128)(2,1)}, u32[]{:S(2)}, u32[]{:S(2)}) %collective-permute-start.1) | collective-permute-done | bytes 262176 | tf_op jit(solution)/shard_map/cond/branch_1_fun/ppermute | solution.py:33
  19.1 1.3 %pick.1 = (bf16[48,2048]{1,0:T(8,128)(2,1)S(1)}, bf16[48,2048]{1,0:T(8,128)(2,1)S(1)}, bf16[48,2048]{1,0:T(8,128)(2,1)S(1)}, bf16[48,2048]{1,0:T(8,128)(2,1)S(1)}) custom-call(bf16[192,128]{1,0:T(8,128)(2,1)S(1)} %get-tuple-element.46.hit_ref, bf16[64,2048]{1,0:T(8,128)(2,1)S(1)} %get-tuple-element.47.low_ref, bf16[64,2048]{1,0:T(8,128)(2,1)} %get-tuple-element.73.arrived_ref), custom_call_target="tpu_custom_call" | custom-call | flops 100663296 | bytes 1310720 | tf_op jit(solution)/shard_map/pick/pallas_call | solution.py:160
  21.5 2.1 %collective-permute-start.9 = (bf16[48,2048]{1,0:T(8,128)(2,1)S(1)}, bf16[48,2048]{1,0:T(8,128)(2,1)S(1)}, u32[]{:S(2)}, u32[]{:S(2)}) collective-permute-start(bf16[48,2048]{1,0:T(8,128)(2,1)S(1)} %get-tuple-element.54), channel_id=1, source_target_pairs={{0,4},{1,5},{2,6},{3,7},{4,0},{5,1},{6,2},{7,3},{8,12},{9,13},{10,... | collective-permute-start | bytes 589832 | tf_op jit(solution)/shard_map/ppermute | solution.py:33
  24.9 14.7 %all-to-all-done.weighted_ref = bf16[8,24,2048]{2,1,0:T(8,128)(2,1)S(1)} async-done(((bf16[8,24,2048]{2,1,0:T(8,128)(2,1)}), bf16[8,24,2048]{2,1,0:T(8,128)(2,1)S(1)}, u32[]{:S(2)}, u32[]{:S(2)}) %all-to-all-start) | async-done | bytes 786464 | tf_op jit(solution)/shard_map/all_to_all | solution.py:512
  40.6 7.0 %collective-permute-done.9.refs_4_ = bf16[48,2048]{1,0:T(8,128)(2,1)S(1)} collective-permute-done((bf16[48,2048]{1,0:T(8,128)(2,1)S(1)}, bf16[48,2048]{1,0:T(8,128)(2,1)S(1)}, u32[]{:S(2)}, u32[]{:S(2)}) %collective-permute-start.9) | collective-permute-done | bytes 196640 | tf_op jit(solution)/shard_map/ppermute | solution.py:33
  48.1 3.7 %all-to-all-start.1 = ((bf16[4,192,512]{2,1,0:T(8,128)(2,1)}), bf16[4,192,512]{2,1,0:T(8,128)(2,1)S(1)}, u32[]{:S(2)}, u32[]{:S(2)}) async-start(bf16[4,192,512]{2,1,0:T(8,128)(2,1)} %get-tuple-element.63), calls=%async_computation.1 | async-start | bytes 1572864 | tf_op jit(solution)/shard_map/all_to_all | solution.py:512
  51.8 8.8 %expert.1 = (bf16[48,2048]{1,0:T(8,128)(2,1)S(1)}, bf16[48,2048]{1,0:T(8,128)(2,1)S(1)}, bf16[48,2048]{1,0:T(8,128)(2,1)S(1)}, bf16[48,2048]{1,0:T(8,128)(2,1)S(...) custom-call(bf16[48,2048]{1,0:T(8,128)(2,1)S(1)} %get-tuple-element., ...), custom_call_target="tpu_custom_call" | custom-call | flops 3623878656 | bytes 13369344 | tf_op jit(solution)/shard_map/expert/pallas_call | solution.py:323
  60.7 2.1 %collective-permute-start.21 = (bf16[192,2816]{1,0:T(8,128)(2,1)}, bf16[192,2816]{1,0:T(8,128)(2,1)S(1)}, u32[]{:S(2)}, u32[]{:S(2)}) collective-permute-start(bf16[192,2816]{1,0:T(8,128)(2,1)} %get-tuple-element.71), channel_id=1, source_target_pairs={{0,16},{8,24},{16,0},{24,8},{1,17},{9,25},{17,1},{25,9},{2,18},{10... | collective-permute-start | bytes 3244040 | tf_op jit(solution)/shard_map/ppermute | solution.py:33
  62.8 1.5 %collective-permute-start.20 = (bf16[192,2816]{1,0:T(8,128)(2,1)}, bf16[192,2816]{1,0:T(8,128)(2,1)}, u32[]{:S(2)}, u32[]{:S(2)}) collective-permute-start(bf16[192,2816]{1,0:T(8,128)(2,1)} %get-tuple-element.59.refs_1_), channel_id=1, source_target_pairs={{0,8},{8,0},{16,24},{24,16},{1,9},{9,1},{17,25},{25,17},{2,10},{10... | collective-permute-start | bytes 3244040 | tf_op jit(solution)/shard_map/ppermute | solution.py:33
  64.2 1.9 %collective-permute-start.14 = (bf16[48,2048]{1,0:T(8,128)(2,1)S(1)}, bf16[48,2048]{1,0:T(8,128)(2,1)S(1)}, u32[]{:S(2)}, u32[]{:S(2)}) collective-permute-start(bf16[48,2048]{1,0:T(8,128)(2,1)S(1)} %get-tuple-element.66), channel_id=1, source_target_pairs={{0,4},{1,5},{2,6},{3,7},{4,0},{5,1},{6,2},{7,3},{8,12},{9,13},{10,... | collective-permute-start | bytes 589832 | tf_op jit(solution)/shard_map/ppermute | solution.py:33
  66.1 2.5 %collective-permute-start.15 = (bf16[48,2048]{1,0:T(8,128)(2,1)S(1)}, bf16[48,2048]{1,0:T(8,128)(2,1)S(1)}, u32[]{:S(2)}, u32[]{:S(2)}) collective-permute-start(bf16[48,2048]{1,0:T(8,128)(2,1)S(1)} %get-tuple-element.67), channel_id=1, source_target_pairs={{0,6},{1,7},{2,4},{3,5},{4,2},{5,3},{6,0},{7,1},{8,14},{9,15},{10,... | collective-permute-start | bytes 589832 | tf_op jit(solution)/shard_map/ppermute | solution.py:33
  68.6 4.9 %collective-permute-done.13.refs_2_ = bf16[48,2048]{1,0:T(8,128)(2,1)S(1)} collective-permute-done((bf16[48,2048]{1,0:T(8,128)(2,1)S(1)}, bf16[48,2048]{1,0:T(8,128)(2,1)S(1)}, u32[]{:S(2)}, u32[]{:S(2)}) %collective-permute-start.13) | collective-permute-done | bytes 196640 | tf_op jit(solution)/shard_map/ppermute | solution.py:33
  73.6 7.8 %collective-permute-done.14.refs_4_ = bf16[48,2048]{1,0:T(8,128)(2,1)S(1)} collective-permute-done((bf16[48,2048]{1,0:T(8,128)(2,1)S(1)}, bf16[48,2048]{1,0:T(8,128)(2,1)S(1)}, u32[]{:S(2)}, u32[]{:S(2)}) %collective-permute-start.14) | collective-permute-done | bytes 196640 | tf_op jit(solution)/shard_map/ppermute | solution.py:33
  82.1 4.5 %all-to-all-start.2 = ((bf16[8,24,2048]{2,1,0:T(8,128)(2,1)}), bf16[8,24,2048]{2,1,0:T(8,128)(2,1)S(1)}, u32[]{:S(2)}, u32[]{:S(2)}) async-start(bf16[8,24,2048]{2,1,0:T(8,128)(2,1)} %bitcast.2), calls=%async_computation.2 | async-start | bytes 1572864 | tf_op jit(solution)/shard_map/all_to_all | solution.py:512
  87.9 1.7 %collective-permute-start.23 = (bf16[96,2816]{1,0:T(8,128)(2,1)}, bf16[96,2816]{1,0:T(8,128)(2,1)S(1)}, u32[]{:S(2)}, u32[]{:S(2)}) collective-permute-start(bf16[96,2816]{1,0:T(8,128)(2,1)} %slice.12), channel_id=1, source_target_pairs={{0,8},{8,0},{16,24},{24,16},{1,9},{9,1},{17,25},{25,17},{2,10},{10... | collective-permute-start | bytes 1622024 | tf_op jit(solution)/shard_map/ppermute | solution.py:33
  89.6 1.9 %slice.13 = bf16[96,2816]{1,0:T(8,128)(2,1)} slice(bf16[192,2816]{1,0:T(8,128)(2,1)} %collective-permute-done.20.refs_8_), slice={[96:192], [0:2816]} | slice | bytes 1081344 | tf_op jit(solution)/shard_map/slice | solution.py:502
  91.4 1.5 %collective-permute-start.24 = (bf16[96,2816]{1,0:T(8,128)(2,1)}, bf16[96,2816]{1,0:T(8,128)(2,1)}, u32[]{:S(2)}, u32[]{:S(2)}) collective-permute-start(bf16[96,2816]{1,0:T(8,128)(2,1)} %slice.13), channel_id=1, source_target_pairs={{0,16},{8,24},{16,0},{24,8},{1,17},{9,25},{17,1},{25,9},{2,18},{10... | collective-permute-start | bytes 1622024 | tf_op jit(solution)/shard_map/ppermute | solution.py:33
  97.0 17.7 %conditional.3 = (bf16[64,2048]{1,0:T(8,128)(2,1)}) conditional(s32[]{:T(128)} %bitcast, bf16[64,2048]{1,0:T(8,128)(2,1)S(1)} %get-tuple-element.70, bf16[64,2048]{1,0:T(8,128)(2,1)S(1)} %get-tuple-element.70, bf16[64,2048]{1,0:T(8,128)(2,1)S(1)} %get-tuple-element.70), branch_computations={%region_3.0_spmd, %region_4.0_spmd, %region_5.0_spmd} | conditional | bytes 1048624 | solution.py:491
  98.0 16.7 %collective-permute-done.4 = bf16[64,2048]{1,0:T(8,128)(2,1)} collective-permute-done((bf16[64,2048]{1,0:T(8,128)(2,1)S(1)}, bf16[64,2048]{1,0:T(8,128)(2,1)}, u32[]{:S(2)}, u32[]{:S(2)}) %collective-permute-start.4) | collective-permute-done | bytes 262176 | tf_op jit(solution)/shard_map/cond/branch_1_fun/ppermute | solution.py:33
  114.7 6.5 %final.1 = (bf16[128,2048]{1,0:T(8,128)(2,1)}, bf16[128,2048]{1,0:T(8,128)(2,1)}, f32[1,512,768]{2,1,0:T(8,128)}, f32[1,512,768]{2,1,0:T(8,128)}, f32[1,768,512]{2,1,0:T(8,128)}) custom-call(bf16[192,512]{1,0:T(8,128)(2,1)} %get-tuple-element.58.refs_0_, bf16[192,2816]{1,0:T(8,128)(2,1)} %get-tuple-element.59.refs_1_, ...), custom_call_target="tpu_custom_call" | custom-call | flops 1811939328 | bytes 4718592 | tf_op jit(solution)/shard_map/final/pallas_call | solution.py:419
  (52 shorter events, 10.9 us)
Async XLA Ops:
  3.3 36.3 %all-to-all-start = ((bf16[8,24,2048]{2,1,0:T(8,128)(2,1)}), bf16[8,24,2048]{2,1,0:T(8,128)(2,1)S(1)}, u32[]{:S(2)}, u32[]{:S(2)}) async-start(bf16[8,24,2048]{2,1,0:T(8,128)(2,1)} %bitcast.4), calls=%async_computation | async-start | bytes 1572864 | tf_op jit(solution)/shard_map/all_to_all | solution.py:512
  9.7 9.4 %collective-permute-start.1 = (bf16[64,2048]{1,0:T(8,128)(2,1)S(1)}, bf16[64,2048]{1,0:T(8,128)(2,1)}, u32[]{:S(2)}, u32[]{:S(2)}) collective-permute-start(bf16[64,2048]{1,0:T(8,128)(2,1)S(1)} %param.1), channel_id=1, source_target_pairs={{0,16},{8,24},{16,0},{24,8},{1,17},{9,25},{17,1},{25,9},{2,18},{10... | collective-permute-start | bytes 786440 | tf_op jit(solution)/shard_map/cond/branch_1_fun/ppermute | solution.py:33
  20.4 20.2 %collective-permute-start.11 = (bf16[48,2048]{1,0:T(8,128)(2,1)S(1)}, bf16[48,2048]{1,0:T(8,128)(2,1)S(1)}, u32[]{:S(2)}, u32[]{:S(2)}) collective-permute-start(bf16[48,2048]{1,0:T(8,128)(2,1)S(1)} %get-tuple-element.56), channel_id=1, source_target_pairs={{0,6},{1,7},{2,4},{3,5},{4,2},{5,3},{6,0},{7,1},{8,14},{9,15},{10,... | collective-permute-start | bytes 589832 | tf_op jit(solution)/shard_map/ppermute | solution.py:33
  21.5 26.1 %collective-permute-start.9 = (bf16[48,2048]{1,0:T(8,128)(2,1)S(1)}, bf16[48,2048]{1,0:T(8,128)(2,1)S(1)}, u32[]{:S(2)}, u32[]{:S(2)}) collective-permute-start(bf16[48,2048]{1,0:T(8,128)(2,1)S(1)} %get-tuple-element.54), channel_id=1, source_target_pairs={{0,4},{1,5},{2,6},{3,7},{4,0},{5,1},{6,2},{7,3},{8,12},{9,13},{10,... | collective-permute-start | bytes 589832 | tf_op jit(solution)/shard_map/ppermute | solution.py:33
  23.6 24.0 %collective-permute-start.7 = (bf16[48,2048]{1,0:T(8,128)(2,1)S(1)}, bf16[48,2048]{1,0:T(8,128)(2,1)S(1)}, u32[]{:S(2)}, u32[]{:S(2)}) collective-permute-start(bf16[48,2048]{1,0:T(8,128)(2,1)S(1)} %get-tuple-element.50), channel_id=1, source_target_pairs={{0,2},{1,3},{2,0},{3,1},{4,6},{5,7},{6,4},{7,5},{8,10},{9,11},{10,... | collective-permute-start | bytes 589832 | tf_op jit(solution)/shard_map/ppermute | solution.py:33
  24.9 26.9 %collective-permute-start.6 = (bf16[48,2048]{1,0:T(8,128)(2,1)S(1)}, bf16[48,2048]{1,0:T(8,128)(2,1)S(1)}, u32[]{:S(2)}, u32[]{:S(2)}) collective-permute-start(bf16[48,2048]{1,0:T(8,128)(2,1)S(1)} %get-tuple-element.49.refs_0_), channel_id=1, source_target_pairs={{0,1},{1,0},{2,3},{3,2},{4,5},{5,4},{6,7},{7,6},{8,9},{9,8},{10,11... | collective-permute-start | bytes 589832 | tf_op jit(solution)/shard_map/ppermute | solution.py:33
  47.6 4.2 %collective-permute-start.8 = (bf16[48,2048]{1,0:T(8,128)(2,1)S(1)}, bf16[48,2048]{1,0:T(8,128)(2,1)S(1)}, u32[]{:S(2)}, u32[]{:S(2)}) collective-permute-start(bf16[48,2048]{1,0:T(8,128)(2,1)S(1)} %collective-permute-done.7.refs_2_), channel_id=1, source_target_pairs={{0,1},{1,0},{2,3},{3,2},{4,5},{5,4},{6,7},{7,6},{8,9},{9,8},{10,11... | collective-permute-start | bytes 589832 | tf_op jit(solution)/shard_map/ppermute | solution.py:33
  47.6 4.2 %collective-permute-start.10 = (bf16[48,2048]{1,0:T(8,128)(2,1)S(1)}, bf16[48,2048]{1,0:T(8,128)(2,1)S(1)}, u32[]{:S(2)}, u32[]{:S(2)}) collective-permute-start(bf16[48,2048]{1,0:T(8,128)(2,1)S(1)} %collective-permute-done.9.refs_4_), channel_id=1, source_target_pairs={{0,1},{1,0},{2,3},{3,2},{4,5},{5,4},{6,7},{7,6},{8,9},{9,8},{10,11... | collective-permute-start | bytes 589832 | tf_op jit(solution)/shard_map/ppermute | solution.py:33
  48.1 3.7 %collective-permute-start.12 = (bf16[48,2048]{1,0:T(8,128)(2,1)S(1)}, bf16[48,2048]{1,0:T(8,128)(2,1)S(1)}, u32[]{:S(2)}, u32[]{:S(2)}) collective-permute-start(bf16[48,2048]{1,0:T(8,128)(2,1)S(1)} %collective-permute-done.11.refs_6_), channel_id=1, source_target_pairs={{0,1},{1,0},{2,3},{3,2},{4,5},{5,4},{6,7},{7,6},{8,9},{9,8},{10,11... | collective-permute-start | bytes 589832 | tf_op jit(solution)/shard_map/ppermute | solution.py:33
  48.1 33.3 %all-to-all-start.1 = ((bf16[4,192,512]{2,1,0:T(8,128)(2,1)}), bf16[4,192,512]{2,1,0:T(8,128)(2,1)S(1)}, u32[]{:S(2)}, u32[]{:S(2)}) async-start(bf16[4,192,512]{2,1,0:T(8,128)(2,1)} %get-tuple-element.63), calls=%async_computation.1 | async-start | bytes 1572864 | tf_op jit(solution)/shard_map/all_to_all | solution.py:512
  60.7 26.4 %collective-permute-start.21 = (bf16[192,2816]{1,0:T(8,128)(2,1)}, bf16[192,2816]{1,0:T(8,128)(2,1)S(1)}, u32[]{:S(2)}, u32[]{:S(2)}) collective-permute-start(bf16[192,2816]{1,0:T(8,128)(2,1)} %get-tuple-element.71), channel_id=1, source_target_pairs={{0,16},{8,24},{16,0},{24,8},{1,17},{9,25},{17,1},{25,9},{2,18},{10... | collective-permute-start | bytes 3244040 | tf_op jit(solution)/shard_map/ppermute | solution.py:33
  62.8 26.8 %collective-permute-start.20 = (bf16[192,2816]{1,0:T(8,128)(2,1)}, bf16[192,2816]{1,0:T(8,128)(2,1)}, u32[]{:S(2)}, u32[]{:S(2)}) collective-permute-start(bf16[192,2816]{1,0:T(8,128)(2,1)} %get-tuple-element.59.refs_1_), channel_id=1, source_target_pairs={{0,8},{8,0},{16,24},{24,16},{1,9},{9,1},{17,25},{25,17},{2,10},{10... | collective-permute-start | bytes 3244040 | tf_op jit(solution)/shard_map/ppermute | solution.py:33
  64.2 9.3 %collective-permute-start.13 = (bf16[48,2048]{1,0:T(8,128)(2,1)S(1)}, bf16[48,2048]{1,0:T(8,128)(2,1)S(1)}, u32[]{:S(2)}, u32[]{:S(2)}) collective-permute-start(bf16[48,2048]{1,0:T(8,128)(2,1)S(1)} %get-tuple-element.65), channel_id=1, source_target_pairs={{0,2},{1,3},{2,0},{3,1},{4,6},{5,7},{6,4},{7,5},{8,10},{9,11},{10,... | collective-permute-start | bytes 589832 | tf_op jit(solution)/shard_map/ppermute | solution.py:33
  64.2 17.1 %collective-permute-start.14 = (bf16[48,2048]{1,0:T(8,128)(2,1)S(1)}, bf16[48,2048]{1,0:T(8,128)(2,1)S(1)}, u32[]{:S(2)}, u32[]{:S(2)}) collective-permute-start(bf16[48,2048]{1,0:T(8,128)(2,1)S(1)} %get-tuple-element.66), channel_id=1, source_target_pairs={{0,4},{1,5},{2,6},{3,7},{4,0},{5,1},{6,2},{7,3},{8,12},{9,13},{10,... | collective-permute-start | bytes 589832 | tf_op jit(solution)/shard_map/ppermute | solution.py:33
  66.1 15.2 %collective-permute-start.15 = (bf16[48,2048]{1,0:T(8,128)(2,1)S(1)}, bf16[48,2048]{1,0:T(8,128)(2,1)S(1)}, u32[]{:S(2)}, u32[]{:S(2)}) collective-permute-start(bf16[48,2048]{1,0:T(8,128)(2,1)S(1)} %get-tuple-element.67), channel_id=1, source_target_pairs={{0,6},{1,7},{2,4},{3,5},{4,2},{5,3},{6,0},{7,1},{8,14},{9,15},{10,... | collective-permute-start | bytes 589832 | tf_op jit(solution)/shard_map/ppermute | solution.py:33
  82.1 32.6 %all-to-all-start.2 = ((bf16[8,24,2048]{2,1,0:T(8,128)(2,1)}), bf16[8,24,2048]{2,1,0:T(8,128)(2,1)S(1)}, u32[]{:S(2)}, u32[]{:S(2)}) async-start(bf16[8,24,2048]{2,1,0:T(8,128)(2,1)} %bitcast.2), calls=%async_computation.2 | async-start | bytes 1572864 | tf_op jit(solution)/shard_map/all_to_all | solution.py:512
  87.9 26.8 %collective-permute-start.23 = (bf16[96,2816]{1,0:T(8,128)(2,1)}, bf16[96,2816]{1,0:T(8,128)(2,1)S(1)}, u32[]{:S(2)}, u32[]{:S(2)}) collective-permute-start(bf16[96,2816]{1,0:T(8,128)(2,1)} %slice.12), channel_id=1, source_target_pairs={{0,8},{8,0},{16,24},{24,16},{1,9},{9,1},{17,25},{25,17},{2,10},{10... | collective-permute-start | bytes 1622024 | tf_op jit(solution)/shard_map/ppermute | solution.py:33
  91.4 23.3 %collective-permute-start.24 = (bf16[96,2816]{1,0:T(8,128)(2,1)}, bf16[96,2816]{1,0:T(8,128)(2,1)}, u32[]{:S(2)}, u32[]{:S(2)}) collective-permute-start(bf16[96,2816]{1,0:T(8,128)(2,1)} %slice.13), channel_id=1, source_target_pairs={{0,16},{8,24},{16,0},{24,8},{1,17},{9,25},{17,1},{25,9},{2,18},{10... | collective-permute-start | bytes 1622024 | tf_op jit(solution)/shard_map/ppermute | solution.py:33
  92.9 1.4 %collective-permute-start.16 = (bf16[48,2048]{1,0:T(8,128)(2,1)S(1)}, bf16[48,2048]{1,0:T(8,128)(2,1)S(1)}, u32[]{:S(2)}, u32[]{:S(2)}) collective-permute-start(bf16[48,2048]{1,0:T(8,128)(2,1)S(1)} %get-tuple-element.64.refs_0_), channel_id=1, source_target_pairs={{0,1},{1,0},{2,3},{3,2},{4,5},{5,4},{6,7},{7,6},{8,9},{9,8},{10,11... | collective-permute-start | bytes 589832 | tf_op jit(solution)/shard_map/ppermute | solution.py:33
  92.9 1.7 %collective-permute-start.17 = (bf16[48,2048]{1,0:T(8,128)(2,1)S(1)}, bf16[48,2048]{1,0:T(8,128)(2,1)S(1)}, u32[]{:S(2)}, u32[]{:S(2)}) collective-permute-start(bf16[48,2048]{1,0:T(8,128)(2,1)S(1)} %copy-done.3), channel_id=1, source_target_pairs={{0,1},{1,0},{2,3},{3,2},{4,5},{5,4},{6,7},{7,6},{8,9},{9,8},{10,11... | collective-permute-start | bytes 589832 | tf_op jit(solution)/shard_map/ppermute | solution.py:33
  93.4 1.7 %collective-permute-start.18 = (bf16[48,2048]{1,0:T(8,128)(2,1)S(1)}, bf16[48,2048]{1,0:T(8,128)(2,1)S(1)}, u32[]{:S(2)}, u32[]{:S(2)}) collective-permute-start(bf16[48,2048]{1,0:T(8,128)(2,1)S(1)} %copy-done.5), channel_id=1, source_target_pairs={{0,1},{1,0},{2,3},{3,2},{4,5},{5,4},{6,7},{7,6},{8,9},{9,8},{10,11... | collective-permute-start | bytes 589832 | tf_op jit(solution)/shard_map/ppermute | solution.py:33
  94.3 1.4 %collective-permute-start.19 = (bf16[48,2048]{1,0:T(8,128)(2,1)S(1)}, bf16[48,2048]{1,0:T(8,128)(2,1)S(1)}, u32[]{:S(2)}, u32[]{:S(2)}) collective-permute-start(bf16[48,2048]{1,0:T(8,128)(2,1)S(1)} %copy-done.7), channel_id=1, source_target_pairs={{0,1},{1,0},{2,3},{3,2},{4,5},{5,4},{6,7},{7,6},{8,9},{9,8},{10,11... | collective-permute-start | bytes 589832 | tf_op jit(solution)/shard_map/ppermute | solution.py:33
  94.6 20.1 %collective-permute-start.22 = (bf16[192,512]{1,0:T(8,128)(2,1)}, bf16[192,512]{1,0:T(8,128)(2,1)}, u32[]{:S(2)}, u32[]{:S(2)}) collective-permute-start(bf16[192,512]{1,0:T(8,128)(2,1)} %get-tuple-element.72), channel_id=1, source_target_pairs={{0,24},{8,16},{16,8},{24,0},{1,25},{9,17},{17,9},{25,1},{2,26},{10... | collective-permute-start | bytes 589832 | tf_op jit(solution)/shard_map/ppermute | solution.py:33
  97.1 17.6 %collective-permute-start.4 = (bf16[64,2048]{1,0:T(8,128)(2,1)S(1)}, bf16[64,2048]{1,0:T(8,128)(2,1)}, u32[]{:S(2)}, u32[]{:S(2)}) collective-permute-start(bf16[64,2048]{1,0:T(8,128)(2,1)S(1)} %param.4), channel_id=1, source_target_pairs={{0,16},{8,24},{16,0},{24,8},{1,17},{9,25},{17,1},{25,9},{2,18},{10... | collective-permute-start | bytes 786440 | tf_op jit(solution)/shard_map/cond/branch_1_fun/ppermute | solution.py:33
  (9 other events, 72.5 us)

commit v5 on v4

--- a/solution.py
+++ b/solution.py
@@ -491,6 +491,24 @@
     return lax.switch(key - 1, ways, array)
 
 
+def pass_kernel(part, array_ref, out_ref):
+    half, acts = out_ref.shape
+    out_ref[...] = array_ref[part * half : (part + 1) * half, :acts]
+
+
+def pass_on(array, acts, part):
+    half = jax.ShapeDtypeStruct((array.shape[0] // 2, acts), BF16)
+    return pl.pallas_call(
+        functools.partial(pass_kernel, part),
+        out_shape=half,
+        in_specs=[WHOLE],
+        out_specs=WHOLE,
+        compiler_params=params(8),
+        cost_estimate=cost(0, 4 * half.size),
+        name="pass_on",
+    )(array)
+
+
 def spread_acts(sent):
     if lax.axis_size("dp") != 4:
         return [sent[0]] + [xor_permute(sent[j], "dp", j) for j in range(1, len(sent))], []
@@ -499,7 +517,8 @@
     side = xor_permute(sent[2], "dp", 2)
     far = xor_permute(sent[3], "dp", 3)
     half = side.shape[0] // 2
-    passed = [side[:half], near[half:]]
+    acts = sent[1].shape[1] - sent[3].shape[1]
+    passed = [pass_on(side, acts, 0), pass_on(near, acts, 1)]
     halves = [xor_permute(passed[0], "dp", 1), xor_permute(passed[1], "dp", 2)]
     return [sent[0], near, side, far, *halves], passed
 

time: 122 us -> 122 us (level); the launches traced: 121 us -> 123 us
  Pallas kernels: 20.6 us -> 22.8 us
    slice x2 -> x0, local copies, waits for them, and re-layouts: 2.71 us -> none  [spread_acts(): passed = [side[:half], near[half:]]]
    unnamed x18 -> x20, local copies, waits for them, and re-layouts: 1.68 us -> 3.87 us
    pallas_call x0 -> x2, Pallas kernels: none -> 1.58 us  [pass_on(): pl.pallas_call(functools.partial(pass_kernel, part), out_shape=half, in_s...]
  transfers between devices with their start and end apart: 24 -> 24, of which waited for: 10 -> 10; matrix products, arithmetic and copies ran while one was open for 2% -> 0% of each run, Pallas kernels for 9% -> 11%
where the time goes in v5:
time: 122 us; the launch traced here: 123 us
  waiting for transfers between devices  60.9 us (50%)
  starting transfers between devices  34.3 us (28%)
  Pallas kernels  22.8 us (19%)
  local copies, waits for them, and re-layouts  3.87 us (3%)
    ppermute x21, waiting for transfers between devices, xor_permute(): return lax.ppermute(array, axis, [(i, i ^ key) for i in range(size)])  45.7 us
    ppermute x21, starting transfers between devices, xor_permute(): return lax.ppermute(array, axis, [(i, i ^ key) for i in range(size)])  19.3 us
    all_to_all x3, waiting for transfers between devices, all_to_all(): return lax.all_to_all(array, axis, split_axis=0, concat_axis=0, tiled=True)  15.2 us
    all_to_all x3, starting transfers between devices, all_to_all(): return lax.all_to_all(array, axis, split_axis=0, concat_axis=0, tiled=True)  14.9 us
    pallas_call x1, Pallas kernels, expert(): pl.pallas_call(functools.partial(expert_kernel, (count, capacity, TILE, r...  8.6 us
    pallas_call x1, Pallas kernels, final(): pl.pallas_call(functools.partial(final_kernel, (share, tile, parts)), out...  6.36 us
    unnamed x20, local copies, waits for them, and re-layouts  3.87 us
    pallas_call x1, Pallas kernels, prepare(): pl.pallas_call(functools.partial(prepare_kernel, (window, capacity, tok_d...  2.7 us
  transfers between devices with their start and end apart: 24, of which 10 were waited for; matrix products, arithmetic and copies ran while one was open for 0% of the time, Pallas kernels for 11%

profile of v5, /device:TPU:0, one launch (start us, length us, event | category | flops | bytes accessed | tf_op | source)
XLA Modules:
  0.0 122.7 jit_solution(16268923090506500007)
XLA Ops:
  0.6 2.7 %prepare.1 = (bf16[64,2048]{1,0:T(8,128)(2,1)S(1)}, bf16[64,2048]{1,0:T(8,128)(2,1)S(1)}, bf16[4,48,2048]{2,1,0:T(8,128)(2,1)}, bf16[192,128]{1,0:T(8,128)(2,1)S...) custom-call(s32[1,8,24]{2,1,0:T(8,128)} %refs_0_.1, f32[1,8,24]{2,1,0:T(8,128)} %refs_1_.1, s32[1,8]{1,0:T(1,128)} %refs_2_.1, ...), custom_call_target="tpu_custom_call" | custom-call | flops 100663296 | bytes 1310720 | tf_op jit(solution)/shard_map/prepare/pallas_call | solution.py:126
  3.3 6.3 %all-to-all-start = ((bf16[8,24,2048]{2,1,0:T(8,128)(2,1)}), bf16[8,24,2048]{2,1,0:T(8,128)(2,1)S(1)}, u32[]{:S(2)}, u32[]{:S(2)}) async-start(bf16[8,24,2048]{2,1,0:T(8,128)(2,1)} %bitcast.5), calls=%async_computation | async-start | bytes 1572864 | tf_op jit(solution)/shard_map/all_to_all | solution.py:531
  9.7 8.9 %conditional.2 = (bf16[64,2048]{1,0:T(8,128)(2,1)}) conditional(s32[]{:T(128)} %bitcast, bf16[64,2048]{1,0:T(8,128)(2,1)S(1)} %get-tuple-element.48, bf16[64,2048]{1,0:T(8,128)(2,1)S(1)} %get-tuple-element.48, bf16[64,2048]{1,0:T(8,128)(2,1)S(1)} %get-tuple-element.48), branch_computations={%region_0.0_spmd, %region_1.0_spmd, %region_2.0_spmd} | conditional | bytes 1048624 | solution.py:491
  9.7 1.6 %collective-permute-start.1 = (bf16[64,2048]{1,0:T(8,128)(2,1)S(1)}, bf16[64,2048]{1,0:T(8,128)(2,1)}, u32[]{:S(2)}, u32[]{:S(2)}) collective-permute-start(bf16[64,2048]{1,0:T(8,128)(2,1)S(1)} %param.1), channel_id=1, source_target_pairs={{0,16},{8,24},{16,0},{24,8},{1,17},{9,25},{17,1},{25,9},{2,18},{10... | collective-permute-start | bytes 786440 | tf_op jit(solution)/shard_map/cond/branch_1_fun/ppermute | solution.py:33
  11.3 7.3 %collective-permute-done.1 = bf16[64,2048]{1,0:T(8,128)(2,1)} collective-permute-done((bf16[64,2048]{1,0:T(8,128)(2,1)S(1)}, bf16[64,2048]{1,0:T(8,128)(2,1)}, u32[]{:S(2)}, u32[]{:S(2)}) %collective-permute-start.1) | collective-permute-done | bytes 262176 | tf_op jit(solution)/shard_map/cond/branch_1_fun/ppermute | solution.py:33
  18.6 1.3 %pick.1 = (bf16[48,2048]{1,0:T(8,128)(2,1)S(1)}, bf16[48,2048]{1,0:T(8,128)(2,1)S(1)}, bf16[48,2048]{1,0:T(8,128)(2,1)S(1)}, bf16[48,2048]{1,0:T(8,128)(2,1)S(1)}) custom-call(bf16[192,128]{1,0:T(8,128)(2,1)S(1)} %get-tuple-element.46.hit_ref, bf16[64,2048]{1,0:T(8,128)(2,1)S(1)} %get-tuple-element.47.low_ref, bf16[64,2048]{1,0:T(8,128)(2,1)} %get-tuple-element.73.arrived_ref), custom_call_target="tpu_custom_call" | custom-call | flops 100663296 | bytes 1310720 | tf_op jit(solution)/shard_map/pick/pallas_call | solution.py:160
  19.9 3.5 %collective-permute-start.11 = (bf16[48,2048]{1,0:T(8,128)(2,1)S(1)}, bf16[48,2048]{1,0:T(8,128)(2,1)S(1)}, u32[]{:S(2)}, u32[]{:S(2)}) collective-permute-start(bf16[48,2048]{1,0:T(8,128)(2,1)S(1)} %get-tuple-element.56), channel_id=1, source_target_pairs={{0,6},{1,7},{2,4},{3,5},{4,2},{5,3},{6,0},{7,1},{8,14},{9,15},{10,... | collective-permute-start | bytes 589832 | tf_op jit(solution)/shard_map/ppermute | solution.py:33
  24.4 15.2 %all-to-all-done.weighted_ref = bf16[8,24,2048]{2,1,0:T(8,128)(2,1)S(1)} async-done(((bf16[8,24,2048]{2,1,0:T(8,128)(2,1)}), bf16[8,24,2048]{2,1,0:T(8,128)(2,1)S(1)}, u32[]{:S(2)}, u32[]{:S(2)}) %all-to-all-start) | async-done | bytes 786464 | tf_op jit(solution)/shard_map/all_to_all | solution.py:531
  40.6 7.0 %collective-permute-done.9.refs_4_ = bf16[48,2048]{1,0:T(8,128)(2,1)S(1)} collective-permute-done((bf16[48,2048]{1,0:T(8,128)(2,1)S(1)}, bf16[48,2048]{1,0:T(8,128)(2,1)S(1)}, u32[]{:S(2)}, u32[]{:S(2)}) %collective-permute-start.9) | collective-permute-done | bytes 196640 | tf_op jit(solution)/shard_map/ppermute | solution.py:33
  48.1 3.7 %all-to-all-start.1 = ((bf16[4,192,512]{2,1,0:T(8,128)(2,1)}), bf16[4,192,512]{2,1,0:T(8,128)(2,1)S(1)}, u32[]{:S(2)}, u32[]{:S(2)}) async-start(bf16[4,192,512]{2,1,0:T(8,128)(2,1)} %get-tuple-element.63), calls=%async_computation.1 | async-start | bytes 1572864 | tf_op jit(solution)/shard_map/all_to_all | solution.py:531
  51.8 8.6 %expert.1 = (bf16[48,2048]{1,0:T(8,128)(2,1)S(1)}, bf16[48,2048]{1,0:T(8,128)(2,1)S(1)}, bf16[48,2048]{1,0:T(8,128)(2,1)S(1)}, bf16[48,2048]{1,0:T(8,128)(2,1)S(...) custom-call(bf16[48,2048]{1,0:T(8,128)(2,1)S(1)} %get-tuple-element., ...), custom_call_target="tpu_custom_call" | custom-call | flops 3623878656 | bytes 13369344 | tf_op jit(solution)/shard_map/expert/pallas_call | solution.py:323
  62.0 1.9 %collective-permute-start.14 = (bf16[48,2048]{1,0:T(8,128)(2,1)S(1)}, bf16[48,2048]{1,0:T(8,128)(2,1)S(1)}, u32[]{:S(2)}, u32[]{:S(2)}) collective-permute-start(bf16[48,2048]{1,0:T(8,128)(2,1)S(1)} %get-tuple-element.66), channel_id=1, source_target_pairs={{0,4},{1,5},{2,6},{3,7},{4,0},{5,1},{6,2},{7,3},{8,12},{9,13},{10,... | collective-permute-start | bytes 589832 | tf_op jit(solution)/shard_map/ppermute | solution.py:33
  63.9 2.5 %collective-permute-start.15 = (bf16[48,2048]{1,0:T(8,128)(2,1)S(1)}, bf16[48,2048]{1,0:T(8,128)(2,1)}, u32[]{:S(2)}, u32[]{:S(2)}) collective-permute-start(bf16[48,2048]{1,0:T(8,128)(2,1)S(1)} %get-tuple-element.67), channel_id=1, source_target_pairs={{0,6},{1,7},{2,4},{3,5},{4,2},{5,3},{6,0},{7,1},{8,14},{9,15},{10,... | collective-permute-start | bytes 589832 | tf_op jit(solution)/shard_map/ppermute | solution.py:33
  66.4 2.0 %collective-permute-start.21 = (bf16[192,2816]{1,0:T(8,128)(2,1)}, bf16[192,2816]{1,0:T(8,128)(2,1)S(1)}, u32[]{:S(2)}, u32[]{:S(2)}) collective-permute-start(bf16[192,2816]{1,0:T(8,128)(2,1)} %get-tuple-element.71), channel_id=1, source_target_pairs={{0,16},{8,24},{16,0},{24,8},{1,17},{9,25},{17,1},{25,9},{2,18},{10... | collective-permute-start | bytes 3244040 | tf_op jit(solution)/shard_map/ppermute | solution.py:33
  68.4 1.5 %collective-permute-start.20 = (bf16[192,2816]{1,0:T(8,128)(2,1)}, bf16[192,2816]{1,0:T(8,128)(2,1)S(1)}, u32[]{:S(2)}, u32[]{:S(2)}) collective-permute-start(bf16[192,2816]{1,0:T(8,128)(2,1)} %get-tuple-element.59.refs_1_), channel_id=1, source_target_pairs={{0,8},{8,0},{16,24},{24,16},{1,9},{9,1},{17,25},{25,17},{2,10},{10... | collective-permute-start | bytes 3244040 | tf_op jit(solution)/shard_map/ppermute | solution.py:33
  69.8 2.1 %collective-permute-done.13.refs_2_ = bf16[48,2048]{1,0:T(8,128)(2,1)S(1)} collective-permute-done((bf16[48,2048]{1,0:T(8,128)(2,1)S(1)}, bf16[48,2048]{1,0:T(8,128)(2,1)S(1)}, u32[]{:S(2)}, u32[]{:S(2)}) %collective-permute-start.13) | collective-permute-done | bytes 196640 | tf_op jit(solution)/shard_map/ppermute | solution.py:33
  72.0 7.1 %collective-permute-done.14.refs_4_ = bf16[48,2048]{1,0:T(8,128)(2,1)S(1)} collective-permute-done((bf16[48,2048]{1,0:T(8,128)(2,1)S(1)}, bf16[48,2048]{1,0:T(8,128)(2,1)S(1)}, u32[]{:S(2)}, u32[]{:S(2)}) %collective-permute-start.14) | collective-permute-done | bytes 196640 | tf_op jit(solution)/shard_map/ppermute | solution.py:33
  79.8 4.9 %all-to-all-start.2 = ((bf16[8,24,2048]{2,1,0:T(8,128)(2,1)}), bf16[8,24,2048]{2,1,0:T(8,128)(2,1)}, u32[]{:S(2)}, u32[]{:S(2)}) async-start(bf16[8,24,2048]{2,1,0:T(8,128)(2,1)} %bitcast.4), calls=%async_computation.2 | async-start | bytes 1572864 | tf_op jit(solution)/shard_map/all_to_all | solution.py:531
  84.7 7.2 %collective-permute-done.21.array_ref.refs_9_ = bf16[192,2816]{1,0:T(8,128)(2,1)S(1)} collective-permute-done((bf16[192,2816]{1,0:T(8,128)(2,1)}, bf16[192,2816]{1,0:T(8,128)(2,1)S(1)}, u32[]{:S(2)}, u32[]{:S(2)}) %collective-permute-start.21) | collective-permute-done | bytes 1081376 | tf_op jit(solution)/shard_map/ppermute | solution.py:33
  92.6 1.7 %collective-permute-start.23 = (bf16[96,2304]{1,0:T(8,128)(2,1)}, bf16[96,2304]{1,0:T(8,128)(2,1)S(1)}, u32[]{:S(2)}, u32[]{:S(2)}) collective-permute-start(bf16[96,2304]{1,0:T(8,128)(2,1)} %pass_on.2), channel_id=1, source_target_pairs={{0,8},{8,0},{16,24},{24,16},{1,9},{9,1},{17,25},{25,17},{2,10},{10... | collective-permute-start | bytes 1327112 | tf_op jit(solution)/shard_map/ppermute | solution.py:33
  95.1 1.5 %collective-permute-start.24 = (bf16[96,2304]{1,0:T(8,128)(2,1)}, bf16[96,2304]{1,0:T(8,128)(2,1)}, u32[]{:S(2)}, u32[]{:S(2)}) collective-permute-start(bf16[96,2304]{1,0:T(8,128)(2,1)} %pass_on.3), channel_id=1, source_target_pairs={{0,16},{8,24},{16,0},{24,8},{1,17},{9,25},{17,1},{25,9},{2,18},{10... | collective-permute-start | bytes 1327112 | tf_op jit(solution)/shard_map/ppermute | solution.py:33
  101.6 13.7 %conditional.3 = (bf16[64,2048]{1,0:T(8,128)(2,1)}) conditional(s32[]{:T(128)} %bitcast, bf16[64,2048]{1,0:T(8,128)(2,1)S(1)} %get-tuple-element.70, bf16[64,2048]{1,0:T(8,128)(2,1)S(1)} %get-tuple-element.70, bf16[64,2048]{1,0:T(8,128)(2,1)S(1)} %get-tuple-element.70), branch_computations={%region_3.0_spmd, %region_4.0_spmd, %region_5.0_spmd} | conditional | bytes 1048624 | solution.py:491
  102.3 13.1 %collective-permute-done.4 = bf16[64,2048]{1,0:T(8,128)(2,1)} collective-permute-done((bf16[64,2048]{1,0:T(8,128)(2,1)S(1)}, bf16[64,2048]{1,0:T(8,128)(2,1)}, u32[]{:S(2)}, u32[]{:S(2)}) %collective-permute-start.4) | collective-permute-done | bytes 262176 | tf_op jit(solution)/shard_map/cond/branch_1_fun/ppermute | solution.py:33
  116.3 6.4 %final.1 = (bf16[128,2048]{1,0:T(8,128)(2,1)}, bf16[128,2048]{1,0:T(8,128)(2,1)}, f32[1,512,768]{2,1,0:T(8,128)}, f32[1,512,768]{2,1,0:T(8,128)}, f32[1,768,512]{2,1,0:T(8,128)}) custom-call(bf16[192,512]{1,0:T(8,128)(2,1)} %get-tuple-element.58.refs_0_, bf16[192,2816]{1,0:T(8,128)(2,1)} %get-tuple-element.59.refs_1_, ...), custom_call_target="tpu_custom_call" | custom-call | flops 1811939328 | bytes 4718592 | tf_op jit(solution)/shard_map/final/pallas_call | solution.py:419
  (54 shorter events, 12.9 us)
Async XLA Ops:
  3.3 36.3 %all-to-all-start = ((bf16[8,24,2048]{2,1,0:T(8,128)(2,1)}), bf16[8,24,2048]{2,1,0:T(8,128)(2,1)S(1)}, u32[]{:S(2)}, u32[]{:S(2)}) async-start(bf16[8,24,2048]{2,1,0:T(8,128)(2,1)} %bitcast.5), calls=%async_computation | async-start | bytes 1572864 | tf_op jit(solution)/shard_map/all_to_all | solution.py:531
  9.7 8.9 %collective-permute-start.1 = (bf16[64,2048]{1,0:T(8,128)(2,1)S(1)}, bf16[64,2048]{1,0:T(8,128)(2,1)}, u32[]{:S(2)}, u32[]{:S(2)}) collective-permute-start(bf16[64,2048]{1,0:T(8,128)(2,1)S(1)} %param.1), channel_id=1, source_target_pairs={{0,16},{8,24},{16,0},{24,8},{1,17},{9,25},{17,1},{25,9},{2,18},{10... | collective-permute-start | bytes 786440 | tf_op jit(solution)/shard_map/cond/branch_1_fun/ppermute | solution.py:33
  19.9 20.6 %collective-permute-start.11 = (bf16[48,2048]{1,0:T(8,128)(2,1)S(1)}, bf16[48,2048]{1,0:T(8,128)(2,1)S(1)}, u32[]{:S(2)}, u32[]{:S(2)}) collective-permute-start(bf16[48,2048]{1,0:T(8,128)(2,1)S(1)} %get-tuple-element.56), channel_id=1, source_target_pairs={{0,6},{1,7},{2,4},{3,5},{4,2},{5,3},{6,0},{7,1},{8,14},{9,15},{10,... | collective-permute-start | bytes 589832 | tf_op jit(solution)/shard_map/ppermute | solution.py:33
  23.5 24.1 %collective-permute-start.9 = (bf16[48,2048]{1,0:T(8,128)(2,1)S(1)}, bf16[48,2048]{1,0:T(8,128)(2,1)S(1)}, u32[]{:S(2)}, u32[]{:S(2)}) collective-permute-start(bf16[48,2048]{1,0:T(8,128)(2,1)S(1)} %get-tuple-element.54), channel_id=1, source_target_pairs={{0,4},{1,5},{2,6},{3,7},{4,0},{5,1},{6,2},{7,3},{8,12},{9,13},{10,... | collective-permute-start | bytes 589832 | tf_op jit(solution)/shard_map/ppermute | solution.py:33
  23.5 24.1 %collective-permute-start.7 = (bf16[48,2048]{1,0:T(8,128)(2,1)S(1)}, bf16[48,2048]{1,0:T(8,128)(2,1)S(1)}, u32[]{:S(2)}, u32[]{:S(2)}) collective-permute-start(bf16[48,2048]{1,0:T(8,128)(2,1)S(1)} %get-tuple-element.50), channel_id=1, source_target_pairs={{0,2},{1,3},{2,0},{3,1},{4,6},{5,7},{6,4},{7,5},{8,10},{9,11},{10,... | collective-permute-start | bytes 589832 | tf_op jit(solution)/shard_map/ppermute | solution.py:33
  24.4 27.4 %collective-permute-start.6 = (bf16[48,2048]{1,0:T(8,128)(2,1)S(1)}, bf16[48,2048]{1,0:T(8,128)(2,1)S(1)}, u32[]{:S(2)}, u32[]{:S(2)}) collective-permute-start(bf16[48,2048]{1,0:T(8,128)(2,1)S(1)} %get-tuple-element.49.refs_0_), channel_id=1, source_target_pairs={{0,1},{1,0},{2,3},{3,2},{4,5},{5,4},{6,7},{7,6},{8,9},{9,8},{10,11... | collective-permute-start | bytes 589832 | tf_op jit(solution)/shard_map/ppermute | solution.py:33
  47.6 4.2 %collective-permute-start.8 = (bf16[48,2048]{1,0:T(8,128)(2,1)S(1)}, bf16[48,2048]{1,0:T(8,128)(2,1)S(1)}, u32[]{:S(2)}, u32[]{:S(2)}) collective-permute-start(bf16[48,2048]{1,0:T(8,128)(2,1)S(1)} %collective-permute-done.7.refs_2_), channel_id=1, source_target_pairs={{0,1},{1,0},{2,3},{3,2},{4,5},{5,4},{6,7},{7,6},{8,9},{9,8},{10,11... | collective-permute-start | bytes 589832 | tf_op jit(solution)/shard_map/ppermute | solution.py:33
  47.6 4.2 %collective-permute-start.10 = (bf16[48,2048]{1,0:T(8,128)(2,1)S(1)}, bf16[48,2048]{1,0:T(8,128)(2,1)S(1)}, u32[]{:S(2)}, u32[]{:S(2)}) collective-permute-start(bf16[48,2048]{1,0:T(8,128)(2,1)S(1)} %collective-permute-done.9.refs_4_), channel_id=1, source_target_pairs={{0,1},{1,0},{2,3},{3,2},{4,5},{5,4},{6,7},{7,6},{8,9},{9,8},{10,11... | collective-permute-start | bytes 589832 | tf_op jit(solution)/shard_map/ppermute | solution.py:33
  48.1 3.7 %collective-permute-start.12 = (bf16[48,2048]{1,0:T(8,128)(2,1)S(1)}, bf16[48,2048]{1,0:T(8,128)(2,1)S(1)}, u32[]{:S(2)}, u32[]{:S(2)}) collective-permute-start(bf16[48,2048]{1,0:T(8,128)(2,1)S(1)} %collective-permute-done.11.refs_6_), channel_id=1, source_target_pairs={{0,1},{1,0},{2,3},{3,2},{4,5},{5,4},{6,7},{7,6},{8,9},{9,8},{10,11... | collective-permute-start | bytes 589832 | tf_op jit(solution)/shard_map/ppermute | solution.py:33
  48.1 31.7 %all-to-all-start.1 = ((bf16[4,192,512]{2,1,0:T(8,128)(2,1)}), bf16[4,192,512]{2,1,0:T(8,128)(2,1)S(1)}, u32[]{:S(2)}, u32[]{:S(2)}) async-start(bf16[4,192,512]{2,1,0:T(8,128)(2,1)} %get-tuple-element.63), calls=%async_computation.1 | async-start | bytes 1572864 | tf_op jit(solution)/shard_map/all_to_all | solution.py:531
  62.0 10.0 %collective-permute-start.13 = (bf16[48,2048]{1,0:T(8,128)(2,1)S(1)}, bf16[48,2048]{1,0:T(8,128)(2,1)S(1)}, u32[]{:S(2)}, u32[]{:S(2)}) collective-permute-start(bf16[48,2048]{1,0:T(8,128)(2,1)S(1)} %get-tuple-element.65), channel_id=1, source_target_pairs={{0,2},{1,3},{2,0},{3,1},{4,6},{5,7},{6,4},{7,5},{8,10},{9,11},{10,... | collective-permute-start | bytes 589832 | tf_op jit(solution)/shard_map/ppermute | solution.py:33
  62.0 17.1 %collective-permute-start.14 = (bf16[48,2048]{1,0:T(8,128)(2,1)S(1)}, bf16[48,2048]{1,0:T(8,128)(2,1)S(1)}, u32[]{:S(2)}, u32[]{:S(2)}) collective-permute-start(bf16[48,2048]{1,0:T(8,128)(2,1)S(1)} %get-tuple-element.66), channel_id=1, source_target_pairs={{0,4},{1,5},{2,6},{3,7},{4,0},{5,1},{6,2},{7,3},{8,12},{9,13},{10,... | collective-permute-start | bytes 589832 | tf_op jit(solution)/shard_map/ppermute | solution.py:33
  63.9 15.9 %collective-permute-start.15 = (bf16[48,2048]{1,0:T(8,128)(2,1)S(1)}, bf16[48,2048]{1,0:T(8,128)(2,1)}, u32[]{:S(2)}, u32[]{:S(2)}) collective-permute-start(bf16[48,2048]{1,0:T(8,128)(2,1)S(1)} %get-tuple-element.67), channel_id=1, source_target_pairs={{0,6},{1,7},{2,4},{3,5},{4,2},{5,3},{6,0},{7,1},{8,14},{9,15},{10,... | collective-permute-start | bytes 589832 | tf_op jit(solution)/shard_map/ppermute | solution.py:33
  66.4 25.4 %collective-permute-start.21 = (bf16[192,2816]{1,0:T(8,128)(2,1)}, bf16[192,2816]{1,0:T(8,128)(2,1)S(1)}, u32[]{:S(2)}, u32[]{:S(2)}) collective-permute-start(bf16[192,2816]{1,0:T(8,128)(2,1)} %get-tuple-element.71), channel_id=1, source_target_pairs={{0,16},{8,24},{16,0},{24,8},{1,17},{9,25},{17,1},{25,9},{2,18},{10... | collective-permute-start | bytes 3244040 | tf_op jit(solution)/shard_map/ppermute | solution.py:33
  68.4 25.9 %collective-permute-start.20 = (bf16[192,2816]{1,0:T(8,128)(2,1)}, bf16[192,2816]{1,0:T(8,128)(2,1)S(1)}, u32[]{:S(2)}, u32[]{:S(2)}) collective-permute-start(bf16[192,2816]{1,0:T(8,128)(2,1)} %get-tuple-element.59.refs_1_), channel_id=1, source_target_pairs={{0,8},{8,0},{16,24},{24,16},{1,9},{9,1},{17,25},{25,17},{2,10},{10... | collective-permute-start | bytes 3244040 | tf_op jit(solution)/shard_map/ppermute | solution.py:33
  79.8 35.6 %all-to-all-start.2 = ((bf16[8,24,2048]{2,1,0:T(8,128)(2,1)}), bf16[8,24,2048]{2,1,0:T(8,128)(2,1)}, u32[]{:S(2)}, u32[]{:S(2)}) async-start(bf16[8,24,2048]{2,1,0:T(8,128)(2,1)} %bitcast.4), calls=%async_computation.2 | async-start | bytes 1572864 | tf_op jit(solution)/shard_map/all_to_all | solution.py:531
  92.6 22.7 %collective-permute-start.23 = (bf16[96,2304]{1,0:T(8,128)(2,1)}, bf16[96,2304]{1,0:T(8,128)(2,1)S(1)}, u32[]{:S(2)}, u32[]{:S(2)}) collective-permute-start(bf16[96,2304]{1,0:T(8,128)(2,1)} %pass_on.2), channel_id=1, source_target_pairs={{0,8},{8,0},{16,24},{24,16},{1,9},{9,1},{17,25},{25,17},{2,10},{10... | collective-permute-start | bytes 1327112 | tf_op jit(solution)/shard_map/ppermute | solution.py:33
  95.1 20.3 %collective-permute-start.24 = (bf16[96,2304]{1,0:T(8,128)(2,1)}, bf16[96,2304]{1,0:T(8,128)(2,1)}, u32[]{:S(2)}, u32[]{:S(2)}) collective-permute-start(bf16[96,2304]{1,0:T(8,128)(2,1)} %pass_on.3), channel_id=1, source_target_pairs={{0,16},{8,24},{16,0},{24,8},{1,17},{9,25},{17,1},{25,9},{2,18},{10... | collective-permute-start | bytes 1327112 | tf_op jit(solution)/shard_map/ppermute | solution.py:33
  96.5 1.4 %collective-permute-start.16 = (bf16[48,2048]{1,0:T(8,128)(2,1)S(1)}, bf16[48,2048]{1,0:T(8,128)(2,1)S(1)}, u32[]{:S(2)}, u32[]{:S(2)}) collective-permute-start(bf16[48,2048]{1,0:T(8,128)(2,1)S(1)} %copy-done.4), channel_id=1, source_target_pairs={{0,1},{1,0},{2,3},{3,2},{4,5},{5,4},{6,7},{7,6},{8,9},{9,8},{10,11... | collective-permute-start | bytes 589832 | tf_op jit(solution)/shard_map/ppermute | solution.py:33
  96.6 1.7 %collective-permute-start.17 = (bf16[48,2048]{1,0:T(8,128)(2,1)S(1)}, bf16[48,2048]{1,0:T(8,128)(2,1)S(1)}, u32[]{:S(2)}, u32[]{:S(2)}) collective-permute-start(bf16[48,2048]{1,0:T(8,128)(2,1)S(1)} %copy-done.6), channel_id=1, source_target_pairs={{0,1},{1,0},{2,3},{3,2},{4,5},{5,4},{6,7},{7,6},{8,9},{9,8},{10,11... | collective-permute-start | bytes 589832 | tf_op jit(solution)/shard_map/ppermute | solution.py:33
  97.1 1.6 %collective-permute-start.18 = (bf16[48,2048]{1,0:T(8,128)(2,1)S(1)}, bf16[48,2048]{1,0:T(8,128)(2,1)S(1)}, u32[]{:S(2)}, u32[]{:S(2)}) collective-permute-start(bf16[48,2048]{1,0:T(8,128)(2,1)S(1)} %copy-done.8), channel_id=1, source_target_pairs={{0,1},{1,0},{2,3},{3,2},{4,5},{5,4},{6,7},{7,6},{8,9},{9,8},{10,11... | collective-permute-start | bytes 589832 | tf_op jit(solution)/shard_map/ppermute | solution.py:33
  98.0 1.7 %collective-permute-start.19 = (bf16[48,2048]{1,0:T(8,128)(2,1)}, bf16[48,2048]{1,0:T(8,128)(2,1)S(1)}, u32[]{:S(2)}, u32[]{:S(2)}) collective-permute-start(bf16[48,2048]{1,0:T(8,128)(2,1)} %collective-permute-done.15.refs_6_), channel_id=1, source_target_pairs={{0,1},{1,0},{2,3},{3,2},{4,5},{5,4},{6,7},{7,6},{8,9},{9,8},{10,11... | collective-permute-start | bytes 589832 | tf_op jit(solution)/shard_map/ppermute | solution.py:33
  98.3 17.1 %collective-permute-start.22 = (bf16[192,512]{1,0:T(8,128)(2,1)}, bf16[192,512]{1,0:T(8,128)(2,1)}, u32[]{:S(2)}, u32[]{:S(2)}) collective-permute-start(bf16[192,512]{1,0:T(8,128)(2,1)} %get-tuple-element.72), channel_id=1, source_target_pairs={{0,24},{8,16},{16,8},{24,0},{1,25},{9,17},{17,9},{25,1},{2,26},{10... | collective-permute-start | bytes 589832 | tf_op jit(solution)/shard_map/ppermute | solution.py:33
  101.6 13.7 %collective-permute-start.4 = (bf16[64,2048]{1,0:T(8,128)(2,1)S(1)}, bf16[64,2048]{1,0:T(8,128)(2,1)}, u32[]{:S(2)}, u32[]{:S(2)}) collective-permute-start(bf16[64,2048]{1,0:T(8,128)(2,1)S(1)} %param.4), channel_id=1, source_target_pairs={{0,16},{8,24},{16,0},{24,8},{1,17},{9,25},{17,1},{25,9},{2,18},{10... | collective-permute-start | bytes 786440 | tf_op jit(solution)/shard_map/cond/branch_1_fun/ppermute | solution.py:33
  (10 other events, 56.3 us)
